TPU v7x, 32 devices: a whole 2x2x4 slice. The times are simulated.
32 devices in a mesh: dp: 8 (over z, y), tensor: 4 (over x, core).
Axes of the slice: x: 2, y: 2, z: 4, core: 2. Of those that a mesh axis runs over, the one named last changes fastest.
Arguments:
- tokens: bfloat16 [32, 256, 768], P(('dp', 'tensor')), may hold values from -6 to 6
- memory: bfloat16 [32, 1024, 768], P(('dp', 'tensor')), may hold values from -6 to 6
- cotangent: bfloat16 [32, 256, 768], P(('dp', 'tensor')), may hold values from -6 to 6
- lengths: int32 [32], P('dp'), may hold values from 64 to 256, as said below
- memory_mask: int32 [32, 1024], P('dp'), may hold values from 0 to 1, as said below
- token_tags: int32 [32, 256], P(('dp', 'tensor')), may hold values 0 or 1
- embedding: bfloat16 [2, 768], replicated, may hold values from -3 to 3
- gain_self: bfloat16 [768], replicated, may hold values from 0.25 to 1.75
- gain_cross: bfloat16 [768], replicated, may hold values from 0.25 to 1.75
- gain_hidden: bfloat16 [768], replicated, may hold values from 0.25 to 1.75
- self_query: bfloat16 [768, 768], P(None, 'tensor'), may hold values from -0.21875 to 0.21875
- self_key: bfloat16 [768, 768], P(None, 'tensor'), may hold values from -0.21875 to 0.21875
- self_value: bfloat16 [768, 768], P(None, 'tensor'), may hold values from -0.21875 to 0.21875
- self_output: bfloat16 [768, 768], P('tensor'), may hold values from -0.875 to 0.875
- position_bias: bfloat16 [32, 12], P(None, 'tensor'), may hold values from -4 to 4
- cross_query: bfloat16 [768, 768], P(None, 'tensor'), may hold values from -0.21875 to 0.21875
- cross_key: bfloat16 [768, 768], P(None, 'tensor'), may hold values from -0.21875 to 0.21875
- cross_value: bfloat16 [768, 768], P(None, 'tensor'), may hold values from -0.21875 to 0.21875
- cross_output: bfloat16 [768, 768], P('tensor'), may hold values from -1.25 to 1.25
- hidden_in: bfloat16 [768, 3072], P(None, 'tensor'), may hold values from -0.21875 to 0.21875
- hidden_out: bfloat16 [3072, 768], P('tensor'), may hold values from -0.15625 to 0.15625
Outputs:
- layer_out: bfloat16 [32, 256, 768], P(('dp', 'tensor'))
- grad_tokens: bfloat16 [32, 256, 768], P(('dp', 'tensor'))
- grad_memory: bfloat16 [32, 1024, 768], P(('dp', 'tensor'))
- grad_embedding: float32 [2, 768], replicated
- grad_gain_self: float32 [768], replicated
- grad_gain_cross: float32 [768], replicated
- grad_gain_hidden: float32 [768], replicated
- grad_self_query: float32 [768, 768], P(None, 'tensor')
- grad_self_key: float32 [768, 768], P(None, 'tensor')
- grad_self_value: float32 [768, 768], P(None, 'tensor')
- grad_self_output: float32 [768, 768], P('tensor')
- grad_position_bias: float32 [32, 12], P(None, 'tensor')
- grad_cross_query: float32 [768, 768], P(None, 'tensor')
- grad_cross_key: float32 [768, 768], P(None, 'tensor')
- grad_cross_value: float32 [768, 768], P(None, 'tensor')
- grad_cross_output: float32 [768, 768], P('tensor')
- grad_hidden_in: float32 [768, 3072], P(None, 'tensor')
- grad_hidden_out: float32 [3072, 768], P('tensor')
Inputs may be any that keep to these rules, and one draw needn't show every extreme that they name: `lengths`: in each aligned block of 4 items one item has length 256; the others are at least 64. `memory_mask`: each row is 1 on a leading run of 256 to 1024 positions and 0 after it; in each aligned block of 4 items one row is all ones.
All inputs are finite; a program needn't handle non-finite values. No bound on the sum of `token_tags` on one device may be relied on, other than what follows from the above.
Results may differ from a plain program's by a relative error of at most 0.03.
Values may be sent and summed in bfloat16 or wider, within the bound.
A program may use at most 128 MiB of HBM per device.

v0:
```python
import math

import jax
import jax.numpy as jnp
import numpy as np
from jax import lax
from jax.sharding import PartitionSpec as P

HEAD_DIM = 64
BUCKETS = 32
MAX_DISTANCE = 128
DEC_LEN = 256


EPSILON = 1e-06
MASKED = -1000000000.0


def pair_buckets(length, buckets, distance):
    exact_span = buckets // 2
    distances = np.arange(length)
    far_bucket = exact_span + np.floor(
        np.log(np.maximum(distances, 1) / exact_span)
        / math.log(distance / exact_span)
        * (buckets - exact_span)
    ).astype(np.int32)
    chosen = np.where(distances < exact_span, distances, np.minimum(far_bucket, buckets - 1))
    offset = np.clip(distances[:, None] - distances[None, :], 0, length - 1)
    return chosen[offset].astype(np.int32)


def gelu(value):
    return jax.nn.gelu(value, approximate=False)


def normalize(stream, gain):
    inverse = lax.rsqrt(jnp.mean(stream * stream, axis=-1, keepdims=True) + EPSILON)
    return (stream * inverse * gain, inverse)


def normalize_back(stream, inverse, gain, gradient):
    scaled = gradient * gain
    grad_gain = jnp.sum(gradient * stream * inverse, axis=(0, 1))
    grad_stream = inverse * scaled - stream * inverse**3 * jnp.mean(
        scaled * stream, axis=-1, keepdims=True
    )
    return (grad_stream, grad_gain)


def project(operand, weight):
    flattened = operand.reshape(-1, operand.shape[-1])
    result = jnp.dot(flattened, weight, preferred_element_type=jnp.float32)
    return result.reshape(operand.shape[:-1] + (weight.shape[1],))


def project_back(gradient, weight):
    return lax.dot_general(
        gradient,
        weight,
        (((gradient.ndim - 1,), (1,)), ((), ())),
        preferred_element_type=jnp.float32,
    )


def outer_sum(operand, gradient):
    left_side = operand.reshape(-1, operand.shape[-1])
    right_side = gradient.reshape(-1, gradient.shape[-1])
    return lax.dot_general(
        left_side, right_side, (((0,), (0,)), ((), ())), preferred_element_type=jnp.float32
    )


def split_heads(matrix):
    return matrix.reshape(matrix.shape[:-1] + (-1, HEAD_DIM))


def merge_heads(matrix):
    return matrix.reshape(matrix.shape[:-2] + (-1,))


def paired(array):
    return array.reshape((array.shape[0] // 2, 2) + array.shape[1:])


def unpaired(array):
    return array.reshape((-1,) + array.shape[2:])


def block_scores(query_block, key_block, score_bias, allowed):
    scores = (
        jnp.einsum("bqhd,bkhd->bhqk", query_block, key_block, preferred_element_type=jnp.float32)
        * 0.125
        + score_bias
    )
    return jnp.where(allowed[:, None], scores, MASKED)


def attend_forward(query_block, key_block, value_block, score_bias, allowed):
    scores = block_scores(query_block, key_block, score_bias, allowed)
    largest = jnp.max(scores, axis=-1, keepdims=True)
    shifted = jnp.exp(scores - largest)
    totals = jnp.sum(shifted, axis=-1, keepdims=True)
    weights = (shifted / totals).astype(jnp.bfloat16)
    mixed = jnp.einsum("bhqk,bkhd->bqhd", weights, value_block, preferred_element_type=jnp.float32)
    return (mixed.astype(jnp.bfloat16), (largest + jnp.log(totals))[..., 0])


def attend_backward(
    query_block, key_block, value_block, score_bias, allowed, log_total, grad_mixed, with_bias
):
    scores = block_scores(query_block, key_block, score_bias, allowed)
    probs = jnp.exp(scores - log_total[..., None])
    grad_probs = jnp.einsum(
        "bqhd,bkhd->bhqk", grad_mixed, value_block, preferred_element_type=jnp.float32
    )
    grad_values = jnp.einsum(
        "bhqk,bqhd->bkhd",
        probs.astype(jnp.bfloat16),
        grad_mixed,
        preferred_element_type=jnp.float32,
    )
    grad_scores = (
        probs * (grad_probs - jnp.sum(probs * grad_probs, axis=-1, keepdims=True))
    ).astype(jnp.bfloat16)
    grad_query = (
        jnp.einsum("bhqk,bkhd->bqhd", grad_scores, key_block, preferred_element_type=jnp.float32)
        * 0.125
    )
    grad_keys = (
        jnp.einsum("bhqk,bqhd->bkhd", grad_scores, query_block, preferred_element_type=jnp.float32)
        * 0.125
    )
    bias_term = (
        jnp.sum(grad_scores.astype(jnp.float32), axis=0)
        if with_bias
        else jnp.zeros((), jnp.float32)
    )
    return (
        grad_query.astype(jnp.bfloat16),
        grad_keys.astype(jnp.bfloat16),
        grad_values.astype(jnp.bfloat16),
        bias_term,
    )


def attend_all(query_rows, key_rows, value_rows, score_bias, allowed):

    def block(packed):
        return attend_forward(packed[0], packed[1], packed[2], score_bias, packed[3])

    mixed, log_total = lax.map(
        block, (paired(query_rows), paired(key_rows), paired(value_rows), paired(allowed))
    )
    return (unpaired(mixed), unpaired(log_total))


def attend_grads(
    query_rows, key_rows, value_rows, score_bias, allowed, log_total, grad_mixed, with_bias
):

    def block(packed):
        return attend_backward(
            packed[0], packed[1], packed[2], score_bias, packed[3], packed[4], packed[5], with_bias
        )

    grad_query, grad_keys, grad_values, bias_terms = lax.map(
        block,
        (
            paired(query_rows),
            paired(key_rows),
            paired(value_rows),
            paired(allowed),
            paired(log_total),
            paired(grad_mixed),
        ),
    )
    return (
        unpaired(grad_query),
        unpaired(grad_keys),
        unpaired(grad_values),
        jnp.sum(bias_terms, axis=0),
    )


def spread(normed):
    return lax.all_gather(normed.astype(jnp.bfloat16), "tensor", axis=0, tiled=True)


def collect(partial_sum):
    return lax.psum_scatter(
        partial_sum.astype(jnp.bfloat16), "tensor", scatter_dimension=0, tiled=True
    ).astype(jnp.float32)


def gather_grad(stream_grad):
    return lax.all_gather(stream_grad.astype(jnp.bfloat16), "tensor", axis=0, tiled=True)


def scatter_grad(partial_grad):
    return lax.psum_scatter(
        partial_grad.astype(jnp.bfloat16), "tensor", scatter_dimension=0, tiled=True
    ).astype(jnp.float32)


def per_device(
    tokens,
    memory,
    cotangent,
    lengths,
    memory_mask,
    token_tags,
    embedding,
    gain_self,
    gain_cross,
    gain_hidden,
    self_query,
    self_key,
    self_value,
    self_output,
    position_bias,
    cross_query,
    cross_key,
    cross_value,
    cross_output,
    hidden_in,
    hidden_out,
):
    bucket_table = jnp.asarray(pair_buckets(DEC_LEN, BUCKETS, MAX_DISTANCE))
    bucket_ids = lax.broadcasted_iota(jnp.int32, (1, 1, BUCKETS), 2)
    pair_onehot = bucket_table[:, :, None] == bucket_ids
    positions = jnp.arange(DEC_LEN)
    self_bias = jnp.einsum(
        "ijb,bh->hij",
        pair_onehot.astype(jnp.bfloat16),
        position_bias,
        preferred_element_type=jnp.float32,
    )
    allowed_self = (positions[None, None, :] <= positions[None, :, None]) & (
        positions[None, None, :] < lengths[:, None, None]
    )
    allowed_cross = (memory_mask == 1)[:, None, :]
    gain_first = gain_self.astype(jnp.float32)
    gain_second = gain_cross.astype(jnp.float32)
    gain_third = gain_hidden.astype(jnp.float32)
    tagged = (token_tags == 1)[..., None]
    table_rows = embedding.astype(jnp.float32)
    stream_zero = tokens.astype(jnp.float32) + jnp.where(tagged, table_rows[1], table_rows[0])
    normed_first, inverse_first = normalize(stream_zero, gain_first)
    rows_first = spread(normed_first)
    query_first = split_heads(project(rows_first, self_query).astype(jnp.bfloat16))
    keys_first = split_heads(project(rows_first, self_key).astype(jnp.bfloat16))
    values_first = split_heads(project(rows_first, self_value).astype(jnp.bfloat16))
    mixed_first, total_first = attend_all(
        query_first, keys_first, values_first, self_bias, allowed_self
    )
    flat_first = merge_heads(mixed_first)
    stream_one = stream_zero + collect(project(flat_first, self_output))
    normed_second, inverse_second = normalize(stream_one, gain_second)
    rows_second, whole_memory = (
        lax.all_gather(normed_second.astype(jnp.bfloat16), "tensor", axis=0, tiled=True),
        lax.all_gather(memory, "tensor", axis=0, tiled=True),
    )
    keys_second = split_heads(project(whole_memory, cross_key).astype(jnp.bfloat16))
    values_second = split_heads(project(whole_memory, cross_value).astype(jnp.bfloat16))
    query_second = split_heads(project(rows_second, cross_query).astype(jnp.bfloat16))
    mixed_second, total_second = attend_all(
        query_second, keys_second, values_second, 0.0, allowed_cross
    )
    flat_second = merge_heads(mixed_second)
    stream_two = stream_one + collect(project(flat_second, cross_output))
    normed_third, inverse_third = normalize(stream_two, gain_third)
    rows_third = spread(normed_third)
    before = project(rows_third, hidden_in)
    active = gelu(before).astype(jnp.bfloat16)
    stream_three = stream_two + collect(project(active, hidden_out))
    layer_out = stream_three.astype(jnp.bfloat16)
    grad_stream = cotangent.astype(jnp.float32)
    grad_rows = gather_grad(grad_stream)
    grad_active = project_back(grad_rows, hidden_out)
    grad_hidden_out = outer_sum(active, grad_rows)
    unused_value, gelu_back = jax.vjp(gelu, before)
    grad_before = gelu_back(grad_active)[0].astype(jnp.bfloat16)
    grad_hidden_in = outer_sum(rows_third, grad_before)
    grad_normed = scatter_grad(project_back(grad_before, hidden_in))
    grad_delta, grad_gain_hidden = normalize_back(
        stream_two, inverse_third, gain_third, grad_normed
    )
    grad_stream = grad_stream + grad_delta
    grad_rows = gather_grad(grad_stream)
    grad_cross_output = outer_sum(flat_second, grad_rows)
    grad_flat = project_back(grad_rows, cross_output).astype(jnp.bfloat16)
    grad_query, grad_keys, grad_values, unused_bias = attend_grads(
        query_second,
        keys_second,
        values_second,
        0.0,
        allowed_cross,
        total_second,
        split_heads(grad_flat),
        False,
    )
    grad_query = merge_heads(grad_query)
    grad_keys = merge_heads(grad_keys)
    grad_values = merge_heads(grad_values)
    grad_cross_query = outer_sum(rows_second, grad_query)
    partial_normed = project_back(grad_query, cross_query)
    grad_cross_key = outer_sum(whole_memory, grad_keys)
    grad_cross_value = outer_sum(whole_memory, grad_values)
    partial_memory = project_back(grad_keys, cross_key) + project_back(grad_values, cross_value)
    grad_normed, memory_sum = (
        lax.psum_scatter(
            partial_normed.astype(jnp.bfloat16), "tensor", scatter_dimension=0, tiled=True
        ).astype(jnp.float32),
        lax.psum_scatter(
            partial_memory.astype(jnp.bfloat16), "tensor", scatter_dimension=0, tiled=True
        ).astype(jnp.float32),
    )
    grad_memory = memory_sum.astype(jnp.bfloat16)
    grad_delta, grad_gain_cross = normalize_back(
        stream_one, inverse_second, gain_second, grad_normed
    )
    grad_stream = grad_stream + grad_delta
    grad_rows = gather_grad(grad_stream)
    grad_self_output = outer_sum(flat_first, grad_rows)
    grad_flat = project_back(grad_rows, self_output).astype(jnp.bfloat16)
    grad_query, grad_keys, grad_values, bias_grad = attend_grads(
        query_first,
        keys_first,
        values_first,
        self_bias,
        allowed_self,
        total_first,
        split_heads(grad_flat),
        True,
    )
    grad_query = merge_heads(grad_query)
    grad_keys = merge_heads(grad_keys)
    grad_values = merge_heads(grad_values)
    grad_self_query = outer_sum(rows_first, grad_query)
    grad_self_key = outer_sum(rows_first, grad_keys)
    grad_self_value = outer_sum(rows_first, grad_values)
    partial_normed = (
        project_back(grad_query, self_query)
        + project_back(grad_keys, self_key)
        + project_back(grad_values, self_value)
    )
    grad_normed = scatter_grad(partial_normed)
    grad_delta, grad_gain_self = normalize_back(stream_zero, inverse_first, gain_first, grad_normed)
    grad_stream = grad_stream + grad_delta
    grad_tokens = grad_stream.astype(jnp.bfloat16)
    grad_position_bias = jnp.einsum(
        "hij,ijb->bh", bias_grad, pair_onehot.astype(jnp.float32), precision=lax.Precision.HIGHEST
    )
    untagged_sum = jnp.sum(jnp.where(tagged, 0.0, grad_stream), axis=(0, 1))
    tagged_sum = jnp.sum(jnp.where(tagged, grad_stream, 0.0), axis=(0, 1))
    grad_embedding = jnp.stack([untagged_sum, tagged_sum])
    small_totals = lax.psum(
        (grad_embedding, grad_gain_self, grad_gain_cross, grad_gain_hidden), ("dp", "tensor")
    )
    weight_totals = lax.psum(
        (
            grad_cross_query,
            grad_cross_key,
            grad_cross_value,
            grad_cross_output,
            grad_hidden_in,
            grad_hidden_out,
            grad_self_query,
            grad_self_key,
            grad_self_value,
            grad_self_output,
            grad_position_bias,
        ),
        "dp",
    )
    return (
        layer_out,
        grad_tokens,
        grad_memory,
        small_totals[0],
        small_totals[1],
        small_totals[2],
        small_totals[3],
        weight_totals[6],
        weight_totals[7],
        weight_totals[8],
        weight_totals[9],
        weight_totals[10],
        weight_totals[0],
        weight_totals[1],
        weight_totals[2],
        weight_totals[3],
        weight_totals[4],
        weight_totals[5],
    )


def solution(mesh):
    in_specs = (
        P(("dp", "tensor"), None, None),
        P(("dp", "tensor"), None, None),
        P(("dp", "tensor"), None, None),
        P("dp"),
        P("dp", None),
        P(("dp", "tensor"), None),
        P(),
        P(),
        P(),
        P(),
        P(None, "tensor"),
        P(None, "tensor"),
        P(None, "tensor"),
        P("tensor", None),
        P(None, "tensor"),
        P(None, "tensor"),
        P(None, "tensor"),
        P(None, "tensor"),
        P("tensor", None),
        P(None, "tensor"),
        P("tensor", None),
    )
    out_specs = (
        P(("dp", "tensor"), None, None),
        P(("dp", "tensor"), None, None),
        P(("dp", "tensor"), None, None),
        P(),
        P(),
        P(),
        P(),
        P(None, "tensor"),
        P(None, "tensor"),
        P(None, "tensor"),
        P("tensor", None),
        P(None, "tensor"),
        P(None, "tensor"),
        P(None, "tensor"),
        P(None, "tensor"),
        P("tensor", None),
        P(None, "tensor"),
        P("tensor", None),
    )
    return jax.shard_map(
        per_device, mesh=mesh, in_specs=in_specs, out_specs=out_specs, check_vma=False
    )
```

profile of v0, /device:TPU:0, one launch (start us, length us, event | category | flops | bytes accessed | tf_op | source)
XLA Modules:
  0.0 893.5 jit_solution(3631603535494176916)
XLA Ops:
  17.3 18.7 %all-gather.8.cloned.1.call-done = bf16[4,256,768]{2,1,0:T(8,128)(2,1)} async-done(((bf16[1,256,768]{2,1,0:T(8,128)(2,1)}), bf16[4,256,768]{2,1,0:T(8,128)(2,1)}) %all-gather.8.cloned.1.call-update) | async-done | bytes 1572880 | tf_op jit(solution)/shard_map/all_gather | solution.py:186
  43.8 9.3 %while.54 = (s32[]{:T(128)}, bf16[2,2,256,3,64]{2,4,3,1,0:T(8,128)(2,1)S(1)}, f32[2,2,3,256]{3,2,1,0:T(4,128)}, bf16[2,2,256,3,64]{2,4,3,1,0:T(8,128)(2,1)}, pre...) while((s32[]{:T(128)}, ...), condition=%wide.region_4.5_spmd, body=%wide.region_1.4_spmd.sunk | while | flops 104299008 | bytes 6742625 | solution.py:151
  55.1 28.2 %reduce-scatter.8.cloned.1.call-done = bf16[1,256,768]{2,1,0:T(8,128)(2,1)} async-done(((bf16[4,256,768]{2,1,0:T(8,128)(2,1)}), bf16[1,256,768]{2,1,0:T(8,128)(2,1)}) %reduce-scatter.8.cloned.1.call-update) | async-done | bytes 393232 | tf_op jit(solution)/shard_map/reduce_scatter | solution.py:190
  88.3 18.9 %all-gather.12.cloned.1.call-done = bf16[4,256,768]{2,1,0:T(8,128)(2,1)} async-done(((bf16[1,256,768]{2,1,0:T(8,128)(2,1)}), bf16[4,256,768]{2,1,0:T(8,128)(2,1)}) %all-gather.12.cloned.1.call-update) | async-done | bytes 1572880 | tf_op jit(solution)/shard_map/all_gather | solution.py:260
  110.1 45.1 %all-gather.10.cloned.1.call-done = bf16[4,1024,768]{2,1,0:T(8,128)(2,1)} async-done(((bf16[1,1024,768]{2,1,0:T(8,128)(2,1)}), bf16[4,1024,768]{2,1,0:T(8,128)(2,1)}) %all-gather.10.cloned.1.call-update) | async-done | bytes 6291472 | tf_op jit(solution)/shard_map/all_gather | solution.py:261
  155.2 6.3 convolution_convert_fusion.7
  165.0 13.4 %while.55 = (s32[]{:T(128)}, bf16[2,2,256,3,64]{2,4,3,1,0:T(8,128)(2,1)}, f32[2,2,3,256]{3,2,1,0:T(4,128)}, bf16[2,2,1024,3,64]{2,4,3,1,0:T(8,128)(2,1)}, pred[2...) while((s32[]{:T(128)}, ...), condition=%wide.region_10.11_spmd, body=%wide.region_7.10_spmd.sunk | while | flops 421624320 | bytes 27204212 | solution.py:151
  182.7 27.0 %reduce-scatter.10.cloned.1.call-done = bf16[1,256,768]{2,1,0:T(8,128)(2,1)} async-done(((bf16[4,256,768]{2,1,0:T(8,128)(2,1)}), bf16[1,256,768]{2,1,0:T(8,128)(2,1)}) %reduce-scatter.10.cloned.1.call-update) | async-done | bytes 393232 | tf_op jit(solution)/shard_map/reduce_scatter | solution.py:190
  215.5 18.8 %all-gather.14.cloned.1.call-done = bf16[4,256,768]{2,1,0:T(8,128)(2,1)} async-done(((bf16[1,256,768]{2,1,0:T(8,128)(2,1)}), bf16[4,256,768]{2,1,0:T(8,128)(2,1)}) %all-gather.14.cloned.1.call-update) | async-done | bytes 1572880 | tf_op jit(solution)/shard_map/all_gather | solution.py:186
  239.5 8.0 multiply_convert_fusion.3
  247.5 8.0 all-gather.16.cloned.1.call-done
  255.5 5.6 add_convert_fusion.2
  265.0 28.3 %reduce-scatter.14.cloned.1.call-done = bf16[1,256,768]{2,1,0:T(8,128)(2,1)} async-done(((bf16[4,256,768]{2,1,0:T(8,128)(2,1)}), bf16[1,256,768]{2,1,0:T(8,128)(2,1)}) %reduce-scatter.14.cloned.1.call-update) | async-done | bytes 393232 | tf_op jit(solution)/shard_map/reduce_scatter | solution.py:200
  298.4 19.3 %all-gather.18.cloned.1.call-done = bf16[4,256,768]{2,1,0:T(8,128)(2,1)} async-done(((bf16[1,256,768]{2,1,0:T(8,128)(2,1)}), bf16[4,256,768]{2,1,0:T(8,128)(2,1)}) %all-gather.18.cloned.1.call-update) | async-done | bytes 1572880 | tf_op jit(solution)/shard_map/all_gather | solution.py:196
  319.8 23.8 %while.56 = (s32[]{:T(128)}, bf16[2,2,256,3,64]{2,4,3,1,0:T(8,128)(2,1)S(1)}, bf16[2,2,1024,3,64]{2,4,3,1,0:T(8,128)(2,1)}, bf16[2,2,1024,3,64]{2,4,3,1,0:T(8,12...) while((s32[]{:T(128)}, ...), condition=%wide.region_18.19_spmd, body=%wide.region_16.18_spmd.sunk | while | flops 1031600640 | bytes 71042248 | solution.py:166
  351.1 23.7 %reduce-scatter.16.cloned.1.call-done = bf16[1,256,768]{2,1,0:T(8,128)(2,1)} async-done(((bf16[4,256,768]{2,1,0:T(8,128)(2,1)}), bf16[1,256,768]{2,1,0:T(8,128)(2,1)}) %reduce-scatter.16.cloned.1.call-update) | async-done | bytes 393232 | tf_op jit(solution)/shard_map/reduce_scatter | solution.py:311
  377.0 28.6 %reduce-scatter.12.cloned.1.call-done = bf16[1,256,768]{2,1,0:T(8,128)(2,1)} async-done(((bf16[4,256,768]{2,1,0:T(8,128)(2,1)}), bf16[1,256,768]{2,1,0:T(8,128)(2,1)}) %reduce-scatter.12.cloned.1.call-update) | async-done | bytes 393232 | tf_op jit(solution)/shard_map/reduce_scatter | solution.py:190
  409.0 19.6 %all-gather.20.cloned.1.call-done = bf16[4,256,768]{2,1,0:T(8,128)(2,1)} async-done(((bf16[1,256,768]{2,1,0:T(8,128)(2,1)}), bf16[4,256,768]{2,1,0:T(8,128)(2,1)}) %all-gather.20.cloned.1.call-update) | async-done | bytes 1572880 | tf_op jit(solution)/shard_map/all_gather | solution.py:196
  433.0 30.9 %while.57 = (s32[]{:T(128)}, bf16[2,2,256,3,64]{2,4,3,1,0:T(8,128)(2,1)}, bf16[2,2,256,3,64]{2,4,3,1,0:T(8,128)(2,1)}, bf16[2,2,256,3,64]{2,4,3,1,0:T(8,128)(2,1...) while((s32[]{:T(128)}, ...), condition=%wide.region_24.25_spmd, body=%wide.region_21.24_spmd.sunk | while | flops 256670208 | bytes 22056636 | solution.py:166
  471.3 6.1 add_convert_fusion
  508.7 6.4 convolution_bitcast_fusion.2
  535.2 22.0 %psum.113 = f32[32,3]{0,1:T(4,128)} all-reduce(f32[32,3]{0,1:T(4,128)S(1)} %fusion.114), channel_id=1, replica_groups=mesh['dp'=8,'tensor'=4] {'dp'}, use_global_device_ids=true, to_apply=%region_42.43 | all-reduce | flops 96 | bytes 768 | tf_op jit(solution)/shard_map/psum | solution.py:360
  561.0 41.6 %all-reduce = (f32[2,768]{1,0:T(2,128)}, f32[768]{0:T(1024)}, f32[768]{0:T(1024)}, f32[768]{0:T(1024)}) all-reduce(f32[2,768]{1,0:T(2,128)S(1)} %pad_maximum_fusion, f32[768]{0:T(1024)S(1)} %get-tuple-element.295, f32[768]{0:T(1024)S(1)} %copy-done.66, f32[768]{0:T(1024)S(1)} %copy-done.65), channel_id=1, replica_groups=mesh['dp'=8,'tensor'=4] {'dp','tensor'}, use_global_device_ids=true, to_apply=%region_30.31 | all-reduce | flops 3840 | bytes 30720 | tf_op jit(solution)/shard_map/psum | solution.py:357
  602.6 271.0 %all-reduce.4.cloned.1.call-done = (f32[768,192]{0,1:T(8,128)}, f32[768,192]{0,1:T(8,128)}, f32[768,192]{0,1:T(8,128)}, f32[192,768]{1,0:T(8,128)}, f32[768,192]...) async-done(((f32[768,192]{0,1:T(8,128)}, f32[768,192]{0,1:T(8,128)}, ...) | async-done | bytes 9437200 | tf_op jit(solution)/shard_map/psum | solution.py:360
  (360 shorter events, 227.0 us)
Async XLA Ops:
  7.2 227.1 %copy-start = (bf16[768,768]{1,0:T(8,128)(2,1)S(1)}, bf16[768,768]{1,0:T(8,128)(2,1)}, u32[]{:S(2)}) copy-start(bf16[768,768]{1,0:T(8,128)(2,1)} %param.49) | copy-start | bytes 3538948
  7.2 28.8 %all-gather.8.cloned.1.call-start = ((), (), s32[]{:S(2)}) async-start(), calls=%async_computation.7 | async-start | bytes 1966080 | tf_op jit(solution)/shard_map/all_gather | solution.py:186
  8.8 76.5 %copy-start.54 = (pred[256]{0:T(512)(128)(4,1)}, pred[256]{0:T(512)(128)(4,1)S(1)}, u32[]{:S(2)}) copy-start(pred[256]{0:T(512)(128)(4,1)S(1)} %compare_reduce_fusion) | copy-start | bytes 772
  13.5 69.9 %reduce-scatter.8.cloned.1.call-start = ((), (), s32[]{:S(2)}) async-start(), calls=%async_computation.8 | async-start | bytes 1966080 | tf_op jit(solution)/shard_map/reduce_scatter | solution.py:190
  55.0 100.1 %copy-start.48 = (bf16[768,192]{0,1:T(8,128)(2,1)S(1)}, bf16[768,192]{0,1:T(8,128)(2,1)}, u32[]{:S(2)}) copy-start(bf16[768,192]{0,1:T(8,128)(2,1)} %param.47) | copy-start | bytes 884740
  55.0 52.2 %all-gather.12.cloned.1.call-start = ((), (), s32[]{:S(2)}) async-start(), calls=%async_computation.10 | async-start | bytes 1966080 | tf_op jit(solution)/shard_map/all_gather | solution.py:260
  55.1 100.0 %copy-start.59 = (f32[768]{0:T(1024)}, f32[768]{0:T(1024)S(1)}, u32[]{:S(2)}) copy-start(f32[768]{0:T(1024)S(1)} %convert_element_type.192) | copy-start | bytes 9220
  87.4 67.7 %all-gather.10.cloned.1.call-start = ((), (), s32[]{:S(2)}) async-start(), calls=%async_computation.9 | async-start | bytes 7864320 | tf_op jit(solution)/shard_map/all_gather | solution.py:261
  88.0 121.7 %reduce-scatter.10.cloned.1.call-start = ((), (), s32[]{:S(2)}) async-start(), calls=%async_computation.11 | async-start | bytes 1966080 | tf_op jit(solution)/shard_map/reduce_scatter | solution.py:190
  181.4 52.9 %all-gather.14.cloned.1.call-start = ((), (), s32[]{:S(2)}) async-start(), calls=%async_computation.12 | async-start | bytes 1966080 | tf_op jit(solution)/shard_map/all_gather | solution.py:186
  214.4 41.1 %all-gather.16.cloned.1.call-start = ((), (), s32[]{:S(2)}) async-start(), calls=%async_computation.14 | async-start | bytes 1966080 | tf_op jit(solution)/shard_map/all_gather | solution.py:196
  215.2 78.1 %reduce-scatter.14.cloned.1.call-start = ((), (), s32[]{:S(2)}) async-start(), calls=%async_computation.15 | async-start | bytes 1966080 | tf_op jit(solution)/shard_map/reduce_scatter | solution.py:200
  265.0 52.7 %all-gather.18.cloned.1.call-start = ((), (), s32[]{:S(2)}) async-start(), calls=%async_computation.16 | async-start | bytes 1966080 | tf_op jit(solution)/shard_map/all_gather | solution.py:196
  297.9 77.0 %reduce-scatter.16.cloned.1.call-start = ((), (), s32[]{:S(2)}) async-start(), calls=%async_computation.17 | async-start | bytes 1966080 | tf_op jit(solution)/shard_map/reduce_scatter | solution.py:311
  346.5 59.1 %reduce-scatter.12.cloned.1.call-start = ((), (), s32[]{:S(2)}) async-start(), calls=%async_computation.13 | async-start | bytes 1966080 | tf_op jit(solution)/shard_map/reduce_scatter | solution.py:190
  346.6 59.0 %copy-start.21 = (bf16[1,256,768]{2,1,0:T(8,128)(2,1)S(1)}, bf16[1,256,768]{2,1,0:T(8,128)(2,1)}, u32[]{:S(2)}) copy-start(bf16[1,256,768]{2,1,0:T(8,128)(2,1)} %param.32) | copy-start | bytes 1179652
  346.6 59.0 %copy-start.22 = (bf16[1,256,768]{2,1,0:T(8,128)(2,1)S(1)}, bf16[1,256,768]{2,1,0:T(8,128)(2,1)}, u32[]{:S(2)}) copy-start(bf16[1,256,768]{2,1,0:T(8,128)(2,1)} %reduce-scatter.14.cloned.1.call-done) | copy-start | bytes 1179652
  346.6 59.0 %copy-start.53 = (f32[768]{0:T(1024)S(1)}, f32[768]{0:T(1024)}, u32[]{:S(2)}) copy-start(f32[768]{0:T(1024)} %convert_element_type.198) | copy-start | bytes 9220
  346.6 59.0 %copy-start.63 = (f32[256]{0:T(256)S(1)}, f32[256]{0:T(256)}, u32[]{:S(2)}) copy-start(f32[256]{0:T(256)} %copy-done.61) | copy-start | bytes 3076
  351.0 77.5 %copy-start.43 = (bf16[192,768]{1,0:T(8,128)(2,1)S(1)}, bf16[192,768]{1,0:T(8,128)(2,1)}, u32[]{:S(2)}) copy-start(bf16[192,768]{1,0:T(8,128)(2,1)} %param.43) | copy-start | bytes 884740
  351.1 77.5 %all-gather.20.cloned.1.call-start = ((), (), s32[]{:S(2)}) async-start(), calls=%async_computation.18 | async-start | bytes 1966080 | tf_op jit(solution)/shard_map/all_gather | solution.py:196
  408.7 148.5 %reduce-scatter.18.cloned.1.call-start = ((), (), s32[]{:S(2)}) async-start(), calls=%async_computation.19 | async-start | bytes 1966080 | tf_op jit(solution)/shard_map/reduce_scatter | solution.py:200
  469.4 133.2 %reduce-scatter.20.cloned.1.call-start = ((), (), s32[]{:S(2)}) async-start(), calls=%async_computation.20 | async-start | bytes 7864320 | tf_op jit(solution)/shard_map/reduce_scatter | solution.py:314
  477.4 396.2 %all-reduce.4.cloned.1.call-start = ((), (), s32[]{:S(2)}) async-start(), calls=%async_computation.21 | async-start | bytes 18874368 | tf_op jit(solution)/shard_map/psum | solution.py:360
  (77 other events, 1183.4 us)
Sparse Core Ops, SparseCore 0:
  13.6 22.3 all-gather.7
  55.2 28.1 reduce-scatter.7
  87.6 19.6 all-gather.11
  108.7 46.3 all-gather.9
  181.5 28.1 reduce-scatter.9
  214.6 19.6 all-gather.13
  235.8 19.6 all-gather.15
  265.1 28.1 reduce-scatter.13
  298.0 19.6 all-gather.17
  346.6 28.1 reduce-scatter.15
  377.4 28.1 reduce-scatter.11
  408.8 19.6 all-gather.19
  469.5 28.1 reduce-scatter.17
  500.7 58.3 reduce-scatter.19
  568.0 305.5 all-reduce.3
where the time goes:
time: 900 us; the launch traced here: 894 us
  waiting for transfers between devices  557 us (62%)
  matrix products  147 us (16%)
  blocking collectives  63.5 us (7%)
  local copies, waits for them, and re-layouts  58.8 us (7%)
  other arithmetic  50.3 us (6%)
  between operations  15.2 us (2%)
    psum x1, waiting for transfers between devices, per_device(): lax.psum((grad_cross_query, grad_cross_key, grad_cross_value, grad_cross_...  271 us
    reduce_scatter x3, waiting for transfers between devices, collect(): lax.psum_scatter(partial_sum.astype(jnp.bfloat16), 'tensor', scatter_dime...  83.8 us
    all_gather x3, waiting for transfers between devices, gather_grad(): lax.all_gather(stream_grad.astype(jnp.bfloat16), 'tensor', axis=0, tiled=...  46.8 us
    all_gather x1, waiting for transfers between devices, per_device(): lax.all_gather(memory, 'tensor', axis=0, tiled=True)  45.1 us
    psum x1, blocking collectives, per_device(): lax.psum((grad_embedding, grad_gain_self, grad_gain_cross, grad_gain_hidd...  41.6 us
    all_gather x2, waiting for transfers between devices, spread(): lax.all_gather(normed.astype(jnp.bfloat16), 'tensor', axis=0, tiled=True)  37.5 us
    dot_general x10, matrix products, project(): result = jnp.dot(flattened, weight, preferred_element_type=jnp.float32)  31 us
    dot_general x10, matrix products, outer_sum(): lax.dot_general(left_side, right_side, (((0,), (0,)), ((), ())), preferre...  30.4 us
  transfers between devices with their start and end apart: 15, of which 13 were waited for; matrix products, arithmetic and copies ran while one was open for 10% of the time, Pallas kernels for 0%

commit v1 on v0

v1 whole, which is shorter than its diff:
```python
import math

import jax, jax.numpy as jnp, numpy as np
from jax import lax
from jax.experimental import pallas as pl
from jax.experimental.pallas import tpu as pltpu
from jax.sharding import PartitionSpec as P

EPSILON=1e-6
MASKED=-1e9
F32=jnp.float32; BF=jnp.bfloat16
NN=(((1,),(0,)),((),())); NT=(((1,),(1,)),((),()))
def mm(a,b,d=NN): return lax.dot_general(a,b,d,preferred_element_type=F32)
def inv_of(h): return lax.rsqrt(jnp.mean(h*h,axis=-1,keepdims=True)+EPSILON)
def norm_back(h,inv,g,r):
    s=r*g
    gg=jnp.sum(r*h*inv,axis=0,keepdims=True)
    return inv*s-h*(inv*inv*inv)*jnp.mean(s*h,axis=-1,keepdims=True),gg

def kernel(tok,mem,cot,tagc,emb,gains,mask1,mask2,btab,
           wqk,wvq,wckv,wso,wco,whin,whout,
           lo,gtok,gmem,small,diag,gqk,gvq,gckv,gso,gco,ghin,ghout,
           vqk,vvq,vckv,vso,vco,vhin,vhout,
           s0,s1,s2,gst,acc,gma,n1,n2,n1T,n2T,n3T,memT,
           qk1,vx1,q2r,kv2,kvT,mixT1,mixT2,lse,gkv,gvq2,rows,st384,st768,stout,sem,osem):
    ws=[(wqk,vqk),(wso,vso),(wvq,vvq),(wckv,vckv),(wco,vco),(whin,vhin),(whout,vhout)]
    cps=[pltpu.make_async_copy(a,b,sem.at[i]) for i,(a,b) in enumerate(ws)]
    for c in cps: c.start()
    g_self=gains[0:1,:]; g_cross=gains[1:2,:]; g_hid=gains[2:3,:]
    lane384=lax.broadcasted_iota(jnp.int32,(1,384),1)
    e0=emb[0:1,:].astype(F32); e1=emb[1:2,:].astype(F32)
    x0=tok[...].astype(F32)+jnp.where(tagc[...]>0.5,e1,e0)
    s0[...]=x0
    nn=(x0*inv_of(x0)*g_self).astype(BF)
    n1[...]=nn; n1T[...]=nn.T
    ji=lax.broadcasted_iota(jnp.int32,(256,256),0); ii=lax.broadcasted_iota(jnp.int32,(256,256),1)
    memT[...]=mem[...].T
    cps[0].wait(); cps[2].wait()
    def self_fwd(t,_):
        x=mm(n1[...],vqk[t])
        qk1[t]=jnp.where(lane384<192,x*0.125,x).astype(BF)
        v=mm(n1[...],vvq[t]).astype(BF)
        vx1[t]=v
        vT=v.T
        allowed=(ji<=ii)&(mask1[...]>0.5)
        for i in range(3):
            q=qk1[t,:,64*i:64*i+64]; k=qk1[t,:,192+64*i:256+64*i]
            b=pltpu.roll(jnp.broadcast_to(btab[t,i:i+1,:],(256,256)),0,1,stride=1,stride_axis=0)
            s=jnp.where(allowed,mm(k,q,NT)+b,MASKED)
            m=jnp.max(s,axis=0,keepdims=True)
            p=jnp.exp(s-m); l=jnp.sum(p,axis=0,keepdims=True)
            o=mm(vT[64*i:64*i+64,:],p.astype(BF))
            mixT1[t,64*i:64*i+64,:]=(o/l).astype(BF)
            lse[t,i:i+1,:]=m+jnp.log(l)
        return 0
    lax.fori_loop(0,4,self_fwd,0)
    cps[1].wait()
    s1[...]=s0[...]
    def so_fwd(t,_):
        s1[...]+=mm(mixT1[t].T,vso[t]); return 0
    lax.fori_loop(0,4,so_fwd,0)
    x1=s1[...]
    nn=(x1*inv_of(x1)*g_cross).astype(BF)
    n2[...]=nn; n2T[...]=nn.T
    cps[3].wait()
    def cross_fwd(t,_):
        q2r[t]=(mm(n2[...],vvq[t])*0.125).astype(BF)
        def proj(r,_):
            rs=pl.ds(pl.multiple_of(r*256,256),256)
            x=mm(mem[rs,:],vckv[t]).astype(BF)
            kv2[t,rs,:]=x
            return 0
        lax.fori_loop(0,4,proj,0)
        kvT[t]=kv2[t].T
        for i in range(3):
            q=q2r[t,:,192+64*i:256+64*i]
            ss=[]
            m=None
            for c in range(4):
                k=kv2[t,256*c:256*c+256,64*i:64*i+64]
                s=mm(k,q,NT)+jnp.concatenate([mask2[256*c:256*c+256,:]]*2,axis=1)
                ss.append(s)
                mc=jnp.max(s,axis=0,keepdims=True)
                m=mc if m is None else jnp.maximum(m,mc)
            l=0.;o=0.
            for c in range(4):
                p=jnp.exp(ss[c]-m)
                l=l+jnp.sum(p,axis=0,keepdims=True)
                o=o+mm(kvT[t,192+64*i:256+64*i,256*c:256*c+256],p.astype(BF))
            mixT2[t,64*i:64*i+64,:]=(o/l).astype(BF)
            lse[4+t,i:i+1,:]=m+jnp.log(l)
        return 0
    lax.fori_loop(0,4,cross_fwd,0)
    cps[4].wait()
    s2[...]=s1[...]
    def co_fwd(t,_):
        s2[...]+=mm(mixT2[t].T,vco[t]); return 0
    lax.fori_loop(0,4,co_fwd,0)
    x2=s2[...]
    nn=(x2*inv_of(x2)*g_hid).astype(BF)
    n3T[...]=nn.T
    rows[...]=nn
    acc[...]=x2
    gst[...]=jnp.zeros_like(x2)
    cps[5].wait(); cps[6].wait()
    def out_copy(t,src,dst,i): return pltpu.make_async_copy(src,dst.at[t],osem.at[i])
    def ffn(t,_):
        def part(c,_):
            cs=pl.ds(pl.multiple_of(c*256,256),256)
            v=mm(rows[...],vhin[t,:,cs])
            phi=0.5*(1.0+lax.erf(v*np.float32(1/math.sqrt(2))))
            act=(v*phi).astype(BF)
            gd=phi+v*(jnp.exp(-0.5*v*v)*np.float32(1/math.sqrt(2*math.pi)))
            acc[...]+=mm(act,vhout[t,cs,:])
            ga=mm(cot[...],vhout[t,cs,:],NT)
            gb=(gd*ga).astype(BF)
            gst[...]+=mm(gb,vhin[t,:,cs],NT)
            st768[0,:,cs]=mm(n3T[...],gb).astype(BF)
            st768[1,cs,:]=mm(act.T,cot[...]).astype(BF)
            return 0
        lax.fori_loop(0,3,part,0)
        c0=out_copy(t,st768.at[0],ghin,0); c1=out_copy(t,st768.at[1],ghout,1)
        c0.start(); c1.start(); c0.wait(); c1.wait()
        return 0
    lax.fori_loop(0,4,ffn,0)
    lo[...]=acc[...].astype(BF)
    d,gg=norm_back(x2,inv_of(x2),g_hid,gst[...])
    small[...]=jnp.zeros_like(small)
    small[4:5,:]=gg
    gst[...]=cot[...].astype(F32)+d
    rows[...]=gst[...].astype(BF)
    gma[...]=jnp.zeros_like(gma)
    acc[...]=jnp.zeros_like(x2)
    def cross_bwd(t,_):
        rw=rows[...]
        w=vco[t]
        G=mm(rw,w,NT).astype(BF)
        GT=mm(w,rw,NT).astype(BF)
        stout[...]=mm(mixT2[t],rw).astype(BF)
        c0=out_copy(t,stout,gco,0); c0.start()
        dqs=[]; dks=[];dvs=[]
        for i in range(3):
            q=q2r[t,:,192+64*i:256+64*i]
            g=G[:,64*i:64*i+64]
            r=jnp.sum(mixT2[t,64*i:64*i+64,:].astype(F32)*GT[64*i:64*i+64,:].astype(F32),axis=0,keepdims=True)
            ls=lse[4+t,i:i+1,:]
            dq=0.; dk=[];dv=[]
            for c in range(4):
                rs=slice(256*c,256*c+256)
                s=mm(kv2[t,rs,64*i:64*i+64],q,NT)+jnp.concatenate([mask2[rs,:]]*2,axis=1)
                p=jnp.exp(s-ls)
                dp=mm(kv2[t,rs,192+64*i:256+64*i],g,NT)
                gs=(p*(dp-r)).astype(BF)
                dv.append(mm(p.astype(BF),g).astype(BF))
                dk.append(mm(gs,q).astype(BF))
                dq=dq+mm(kvT[t,64*i:64*i+64,rs],gs)
            dqs.append(dq*0.125); dks.append(dk); dvs.append(dv)
        for c in range(4):
            gkv[256*c:256*c+256,:]=jnp.concatenate([x[c] for x in dks+dvs],axis=1)
        dqT=jnp.concatenate(dqs,axis=0).astype(BF)
        gvq2[t,:,192:384]=dqT.T
        def rl(r,_):
            rs=pl.ds(pl.multiple_of(r*256,256),256)
            gma[rs,:]+=mm(gkv[rs,:],vckv[t],NT)
            return 0
        lax.fori_loop(0,4,rl,0)
        def rd(r,_):
            rs=pl.ds(pl.multiple_of(r*256,256),256)
            st384[rs,:]=mm(memT[rs,:],gkv[...]).astype(BF)
            return 0
        lax.fori_loop(0,3,rd,0)
        c1=out_copy(t,st384,gckv,1); c1.start()
        acc[...]+=mm(jnp.where(lane384>=192,gvq2[t],0).astype(BF),vvq[t],NT)
        c0.wait(); c1.wait()
        return 0
    lax.fori_loop(0,4,cross_bwd,0)
    gmem[...]=gma[...].astype(BF)
    x1=s1[...]
    d,gg=norm_back(x1,inv_of(x1),g_cross,acc[...])
    small[3:4,:]=gg
    gst[...]+=d
    rows[...]=gst[...].astype(BF)
    acc[...]=jnp.zeros_like(x1)
    J=(ji+ii==255).astype(BF)
    def self_bwd(t,_):
        rw=rows[...]
        w=vso[t]
        G=mm(rw,w,NT).astype(BF)
        GT=mm(w,rw,NT).astype(BF)
        stout[...]=mm(mixT1[t],rw).astype(BF)
        c0=out_copy(t,stout,gso,0); c0.start()
        allowed=(ji<=ii)&(mask1[...]>0.5)
        kT=qk1[t].T
        dqs=[];dks=[];dvs=[]
        for i in range(3):
            q=qk1[t,:,64*i:64*i+64]; k=qk1[t,:,192+64*i:256+64*i]
            b=pltpu.roll(jnp.broadcast_to(btab[t,i:i+1,:],(256,256)),0,1,stride=1,stride_axis=0)
            g=G[:,64*i:64*i+64]
            r=jnp.sum(mixT1[t,64*i:64*i+64,:].astype(F32)*GT[64*i:64*i+64,:].astype(F32),axis=0,keepdims=True)
            s=jnp.where(allowed,mm(k,q,NT)+b,MASKED)
            p=jnp.exp(s-lse[t,i:i+1,:])
            dp=mm(vx1[t,:,64*i:64*i+64],g,NT)
            gs=(p*(dp-r)).astype(BF)
            dvs.append(mm(p.astype(BF),g).astype(BF))
            dks.append(mm(gs,q).astype(BF))
            dqs.append(mm(kT[192+64*i:256+64*i,:],gs)*0.125)
            dd=pltpu.roll(mm(J,gs),1,1,stride=1,stride_axis=0)
            diag[t,i:i+1,:]=jnp.sum(dd,axis=0,keepdims=True)
        dq=jnp.concatenate(dqs,axis=0).astype(BF).T
        gqk_t=jnp.concatenate([dq]+dks,axis=1)
        gvq_t=jnp.concatenate(dvs+[gvq2[t,:,192:384]],axis=1)
        st384[...]=mm(n1T[...],gqk_t).astype(BF)
        c1=out_copy(t,st384,gqk,1); c1.start()
        acc[...]+=mm(gqk_t,vqk[t],NT)+mm(jnp.where(lane384<192,gvq_t,0).astype(BF),vvq[t],NT)
        gkv[0:768,:]=jnp.where(lane384<192,mm(n1T[...],gvq_t),mm(n2T[...],gvq_t)).astype(BF)
        c2=out_copy(t,gkv.at[pl.ds(0,768),:],gvq,2); c2.start()
        c0.wait(); c1.wait(); c2.wait()
        return 0
    lax.fori_loop(0,4,self_bwd,0)
    x0=s0[...]
    d,gg=norm_back(x0,inv_of(x0),g_self,acc[...])
    small[2:3,:]=gg
    g0=gst[...]+d
    gtok[...]=g0.astype(BF)
    tg=tagc[...]>0.5
    small[0:1,:]=jnp.sum(jnp.where(tg,0.0,g0),axis=0,keepdims=True)
    small[1:2,:]=jnp.sum(jnp.where(tg,g0,0.0),axis=0,keepdims=True)

def compute(tok,mem,cot,tagc,emb,gains,mask1,mask2,btab,wqk,wvq,wckv,wso,wco,whin,whout):
    V=pl.BlockSpec(memory_space=pltpu.VMEM); A=pl.BlockSpec(memory_space=pl.ANY)
    S=jax.ShapeDtypeStruct
    outs=[S((256,768),BF),S((256,768),BF),S((1024,768),BF),S((8,768),F32),S((4,8,256),F32),
          S((4,768,384),BF),S((4,768,384),BF),S((4,768,384),BF),S((4,192,768),BF),S((4,192,768),BF),S((4,768,768),BF),S((4,768,768),BF)]
    vm=pltpu.VMEM
    scr=[vm((4,768,384),BF)]*3+[vm((4,192,768),BF)]*2+[vm((4,768,768),BF)]*2+\
        [vm((256,768),F32)]*5+[vm((1024,768),F32)]+[vm((256,768),BF)]*2+[vm((768,256),BF)]*3+[vm((768,1024),BF)]+\
        [vm((4,256,384),BF)]*3+[vm((4,1024,384),BF),vm((4,384,1024),BF),vm((4,192,256),BF),vm((4,192,256),BF),vm((8,8,256),F32),
         vm((1024,384),BF),vm((4,256,384),BF),vm((256,768),BF),vm((768,384),BF),vm((2,768,768),BF),vm((192,768),BF),
         pltpu.SemaphoreType.DMA((7,)),pltpu.SemaphoreType.DMA((3,))]
    return pl.pallas_call(kernel,out_shape=outs,in_specs=[V]*9+[A]*7,out_specs=[V]*5+[A]*7,scratch_shapes=scr,
        compiler_params=pltpu.CompilerParams(vmem_limit_bytes=63<<20))(tok,mem,cot,tagc,emb,gains,mask1,mask2,btab,wqk,wvq,wckv,wso,wco,whin,whout)

BUCKETS=32; MAX_DISTANCE=128
def bucket_of(length=256):
    e=BUCKETS//2
    d=np.arange(length)
    far=e+np.floor(np.log(np.maximum(d,1)/e)/math.log(MAX_DISTANCE/e)*(BUCKETS-e)).astype(np.int32)
    return np.where(d<e,d,np.minimum(far,BUCKETS-1)).astype(np.int32)

def prepare(tokens, memory, cotangent, lengths, memory_mask, token_tags, gain_self, gain_cross, gain_hidden):
    t = lax.axis_index("tensor")
    length = lax.dynamic_index_in_dim(lengths, t, 0, keepdims=False)
    mask = lax.dynamic_index_in_dim(memory_mask, t, 0, keepdims=False)
    mask1 = jnp.broadcast_to((jnp.arange(256)[:, None] < length).astype(F32), (256, 256))
    mask2 = jnp.broadcast_to(jnp.where(mask == 1, 0.0, MASKED).astype(F32)[:, None], (1024, 128))
    tagc = (token_tags == 1).astype(F32).reshape(256, 1)
    gains = jnp.pad(jnp.stack([gain_self, gain_cross, gain_hidden]).astype(F32), ((0, 5), (0, 0)))
    return tokens[0], memory[0], cotangent[0], tagc, gains, mask1, mask2


def per_device(tokens, memory, cotangent, lengths, memory_mask, token_tags, embedding, gain_self, gain_cross, gain_hidden,
               self_query, self_key, self_value, self_output, position_bias, cross_query, cross_key, cross_value,
               cross_output, hidden_in, hidden_out):
    tok, mem, cot, tagc, gains, mask1, mask2 = prepare(
        tokens, memory, cotangent, lengths, memory_mask, token_tags, gain_self, gain_cross, gain_hidden)
    chosen = bucket_of()
    onehot = (chosen[:, None] == np.arange(BUCKETS)[None, :]).astype(np.float32)
    table = jnp.dot(position_bias.T, jnp.asarray(onehot.T, BF), preferred_element_type=F32)
    table = jnp.pad(table, ((0, 5), (0, 0)))
    gather = lambda w: lax.all_gather(w, "tensor", axis=0)
    btab = gather(table)
    wqk = gather(jnp.concatenate([self_query, self_key], 1))
    wvq = gather(jnp.concatenate([self_value, cross_query], 1))
    wckv = gather(jnp.concatenate([cross_key, cross_value], 1))
    lo, gtok, gmem, small, diag, gqk, gvq, gckv, gso, gco, ghin, ghout = compute(
        tok, mem, cot, tagc, embedding, gains, mask1, mask2, btab, wqk, wvq, wckv,
        gather(self_output), gather(cross_output), gather(hidden_in), gather(hidden_out))
    small = lax.psum(small, ("dp", "tensor"))
    def total(g):
        g = lax.psum_scatter(g, "tensor", scatter_dimension=0, tiled=False)
        return lax.psum(g, "dp")
    diag = total(diag)
    pb = jnp.dot(jnp.asarray(onehot.T), diag[:3].T, precision=lax.Precision.HIGHEST)
    a, b, c, so, co, hi, ho = lax.psum(tuple(lax.psum_scatter(g, "tensor", scatter_dimension=0, tiled=False) for g in (gqk, gvq, gckv, gso, gco, ghin, ghout)), "dp")
    f = lambda x: x.astype(F32)
    return (lo[None], gtok[None], gmem[None], small[:2], small[2], small[3], small[4],
            f(a[:, :192]), f(a[:, 192:]), f(b[:, :192]), f(so), pb, f(b[:, 192:]), f(c[:, :192]), f(c[:, 192:]), f(co), f(hi), f(ho))


def solution(mesh):
    item = P(("dp", "tensor"), None, None)
    col, row, rep = P(None, "tensor"), P("tensor", None), P()
    in_specs = (item, item, item, P("dp"), P("dp", None), P(("dp", "tensor"), None), rep, rep, rep, rep,
                col, col, col, row, col, col, col, col, row, col, row)
    out_specs = (item, item, item, rep, rep, rep, rep, col, col, col, row, col, col, col, col, row, col, row)
    return jax.shard_map(per_device, mesh=mesh, in_specs=in_specs, out_specs=out_specs, check_vma=False)
```

time: 900 us -> 782 us (0.87)
  matrix products: 147 us -> 0.84 us
  Pallas kernels: 0 us -> 92.2 us
  other arithmetic: 50.3 us -> 13.1 us
  local copies, waits for them, and re-layouts: 58.8 us -> 24.6 us
  waiting for transfers between devices: 557 us -> 567 us
    dot_general x60 -> x2, matrix products: 147 us -> 0.84 us  [the longest x1 0.72 us: per_device(): jnp.dot(jnp.asarray(onehot.T), diag[:3].T, precision=lax.Precision.HIGHEST)]
    psum x1, waiting for transfers between devices: 271 us -> 134 us  [per_device(): lax.psum(tuple((lax.psum_scatter(g, 'tensor', scatter_dimension=0, tiled=...]
    reduce_scatter x7 -> x8, waiting for transfers between devices: 136 us -> 257 us  [the longest x7 257 us: per_device(): lax.psum_scatter(g, 'tensor', scatter_dimension=0, tiled=False)]
    pallas_call x0 -> x1, Pallas kernels: none -> 92.2 us  [compute(): pl.pallas_call(kernel, out_shape=outs, in_specs=[V] * 9 + [A] * 7, out_sp...]
    all_gather x7, waiting for transfers between devices: 148 us -> 168 us  [per_device(): gather = lambda w: lax.all_gather(w, 'tensor', axis=0)]
    reduce_sum x14 -> x0, other arithmetic: 18.5 us -> none  [the longest x3 5.93 us: normalize_back(): grad_gain = jnp.sum(gradient * stream * inverse, axis=(0, 1))]
    convert_element_type x12 -> x7, other arithmetic: 25.8 us -> 8.06 us  [the longest x6 7.42 us: per_device(): f = lambda x: x.astype(F32)]
    all_gather x0 -> x3, local copies, waits for them, and re-layouts: none -> 12.8 us  [per_device(): gather = lambda w: lax.all_gather(w, 'tensor', axis=0)]
  transfers between devices with their start and end apart: 15 -> 16, of which waited for: 13 -> 15; matrix products, arithmetic and copies ran while one was open for 10% -> 3% of each run, Pallas kernels for 0% -> 0%
where the time goes in v1:
time: 782 us; the launch traced here: 781 us
  waiting for transfers between devices  567 us (73%)
  Pallas kernels  92.2 us (12%)
  blocking collectives  69.2 us (9%)
  local copies, waits for them, and re-layouts  24.6 us (3%)
  between operations  14.2 us (2%)
  other arithmetic  13.1 us (2%)
    reduce_scatter x7, waiting for transfers between devices, per_device(): lax.psum_scatter(g, 'tensor', scatter_dimension=0, tiled=False)  257 us
    all_gather x7, waiting for transfers between devices, per_device(): gather = lambda w: lax.all_gather(w, 'tensor', axis=0)  168 us
    psum x1, waiting for transfers between devices, per_device(): lax.psum(tuple((lax.psum_scatter(g, 'tensor', scatter_dimension=0, tiled=...  134 us
    pallas_call x1, Pallas kernels, compute(): pl.pallas_call(kernel, out_shape=outs, in_specs=[V] * 9 + [A] * 7, out_sp...  92.2 us
    psum x1, blocking collectives, per_device(): small = lax.psum(small, ('dp', 'tensor'))  39.6 us
    psum x1, blocking collectives, total(): return lax.psum(g, 'dp')  23 us
  transfers between devices with their start and end apart: 16, of which 15 were waited for; matrix products, arithmetic and copies ran while one was open for 3% of the time, Pallas kernels for 0%

profile of v1, /device:TPU:0, one launch (start us, length us, event | category | flops | bytes accessed | tf_op | source)
XLA Modules:
  0.0 781.3 jit_solution(9595901591835282632)
XLA Ops:
  7.3 2.0 pad_maximum_fusion
  15.4 6.6 all-gather
  24.1 12.9 %all-gather.16.cloned.1.call-done = bf16[3072,384]{0,1:T(8,128)(2,1)} async-done(((bf16[768,384]{0,1:T(8,128)(2,1)}), bf16[3072,384]{0,1:T(8,128)(2,1)}) %all-gather.16.cloned.1.call-update) | async-done | bytes 2359312 | tf_op jit(solution)/shard_map/all_gather | solution.py:270
  37.0 4.3 copy.50
  41.3 22.0 %all-gather.18.cloned.1.call-done = bf16[3072,384]{0,1:T(8,128)(2,1)} async-done(((bf16[768,384]{0,1:T(8,128)(2,1)}), bf16[3072,384]{0,1:T(8,128)(2,1)}) %all-gather.18.cloned.1.call-update) | async-done | bytes 2359312 | tf_op jit(solution)/shard_map/all_gather | solution.py:270
  63.2 4.3 copy.51
  67.5 22.0 %all-gather.20.cloned.1.call-done = bf16[3072,384]{0,1:T(8,128)(2,1)} async-done(((bf16[768,384]{0,1:T(8,128)(2,1)}), bf16[3072,384]{0,1:T(8,128)(2,1)}) %all-gather.20.cloned.1.call-update) | async-done | bytes 2359312 | tf_op jit(solution)/shard_map/all_gather | solution.py:270
  89.5 4.3 copy.52
  93.8 14.6 %all-gather.22.cloned.1.call-done = bf16[768,768]{1,0:T(8,128)(2,1)} async-done(((bf16[192,768]{1,0:T(8,128)(2,1)}), bf16[768,768]{1,0:T(8,128)(2,1)}) %all-gather.22.cloned.1.call-update) | async-done | bytes 1179664 | tf_op jit(solution)/shard_map/all_gather | solution.py:270
  108.4 18.9 %all-gather.24.cloned.1.call-done = bf16[768,768]{1,0:T(8,128)(2,1)} async-done(((bf16[192,768]{1,0:T(8,128)(2,1)}), bf16[768,768]{1,0:T(8,128)(2,1)}) %all-gather.24.cloned.1.call-update) | async-done | bytes 1179664 | tf_op jit(solution)/shard_map/all_gather | solution.py:270
  127.3 38.9 %all-gather.26.cloned.1.call-done = bf16[3072,768]{1,0:T(8,128)(2,1)} async-done(((bf16[768,768]{1,0:T(8,128)(2,1)}), bf16[3072,768]{1,0:T(8,128)(2,1)}) %all-gather.26.cloned.1.call-update) | async-done | bytes 4718608 | tf_op jit(solution)/shard_map/all_gather | solution.py:270
  166.2 39.1 %all-gather.28.cloned.1.call-done = bf16[3072,768]{1,0:T(8,128)(2,1)} async-done(((bf16[768,768]{1,0:T(8,128)(2,1)}), bf16[3072,768]{1,0:T(8,128)(2,1)}) %all-gather.28.cloned.1.call-update) | async-done | bytes 4718608 | tf_op jit(solution)/shard_map/all_gather | solution.py:270
  207.1 92.2 %shard_map.358 = (bf16[256,768]{1,0:T(8,128)(2,1)}, bf16[256,768]{1,0:T(8,128)(2,1)}, bf16[1024,768]{1,0:T(8,128)(2,1)}, f32[8,768]{1,0:T(8,128)}, f32[4,8,256]{...) custom-call(bf16[256,768]{1,0:T(8,128)(2,1)} %bitcast.44, ...), custom_call_target="tpu_custom_call" | custom-call | tf_op jit(solution)/shard_map/pallas_call | solution.py:240
  303.9 21.3 %reduce-scatter.13.cloned.1.call-done = bf16[1,192,768]{2,1,0:T(8,128)(2,1)} async-done(((bf16[4,192,768]{2,1,0:T(8,128)(2,1)}), bf16[1,192,768]{2,1,0:T(8,128)(2,1)}) %reduce-scatter.13.cloned.1.call-update) | async-done | bytes 294928 | tf_op jit(solution)/shard_map/reduce_scatter | solution.py:284
  325.2 28.5 %reduce-scatter.19.cloned.1.call-done = bf16[1,192,768]{2,1,0:T(8,128)(2,1)} async-done(((bf16[4,192,768]{2,1,0:T(8,128)(2,1)}), bf16[1,192,768]{2,1,0:T(8,128)(2,1)}) %reduce-scatter.19.cloned.1.call-update) | async-done | bytes 294928 | tf_op jit(solution)/shard_map/reduce_scatter | solution.py:284
  353.7 35.5 %reduce-scatter.9.cloned.1.call-done = bf16[1,768,384]{2,1,0:T(8,128)(2,1)} async-done(((bf16[4,768,384]{2,1,0:T(8,128)(2,1)}), bf16[1,768,384]{2,1,0:T(8,128)(2,1)}) %reduce-scatter.9.cloned.1.call-update) | async-done | bytes 589840 | tf_op jit(solution)/shard_map/reduce_scatter | solution.py:284
  389.2 35.8 %reduce-scatter.11.cloned.1.call-done = bf16[1,768,384]{2,1,0:T(8,128)(2,1)} async-done(((bf16[4,768,384]{2,1,0:T(8,128)(2,1)}), bf16[1,768,384]{2,1,0:T(8,128)(2,1)}) %reduce-scatter.11.cloned.1.call-update) | async-done | bytes 589840 | tf_op jit(solution)/shard_map/reduce_scatter | solution.py:284
  424.9 35.5 %reduce-scatter.17.cloned.1.call-done = bf16[1,768,384]{2,1,0:T(8,128)(2,1)} async-done(((bf16[4,768,384]{2,1,0:T(8,128)(2,1)}), bf16[1,768,384]{2,1,0:T(8,128)(2,1)}) %reduce-scatter.17.cloned.1.call-update) | async-done | bytes 589840 | tf_op jit(solution)/shard_map/reduce_scatter | solution.py:284
  460.4 50.6 %reduce-scatter.21.cloned.1.call-done = bf16[1,768,768]{2,1,0:T(8,128)(2,1)} async-done(((bf16[4,768,768]{2,1,0:T(8,128)(2,1)}), bf16[1,768,768]{2,1,0:T(8,128)(2,1)}) %reduce-scatter.21.cloned.1.call-update) | async-done | bytes 1179664 | tf_op jit(solution)/shard_map/reduce_scatter | solution.py:284
  511.0 50.3 %reduce-scatter.23.cloned.1.call-done = bf16[1,768,768]{2,1,0:T(8,128)(2,1)} async-done(((bf16[4,768,768]{2,1,0:T(8,128)(2,1)}), bf16[1,768,768]{2,1,0:T(8,128)(2,1)}) %reduce-scatter.23.cloned.1.call-update) | async-done | bytes 1179664 | tf_op jit(solution)/shard_map/reduce_scatter | solution.py:284
  562.0 39.6 %psum.63 = f32[8,768]{1,0:T(8,128)S(1)} all-reduce(f32[8,768]{1,0:T(8,128)S(1)} %copy-done.12), channel_id=1, replica_groups=mesh['dp'=8,'tensor'=4] {'dp','tensor'}, use_global_device_ids=true, to_apply=%region_0.1 | all-reduce | flops 6144 | bytes 49152 | tf_op jit(solution)/shard_map/psum | solution.py:278
  602.8 23.0 %psum.67 = f32[8,256]{1,0:T(8,128)S(1)} all-reduce(f32[8,256]{1,0:T(8,128)} %bitcast.50), channel_id=1, replica_groups=mesh['dp'=8,'tensor'=4] {'dp'}, use_global_device_ids=true, to_apply=%region_8.9 | all-reduce | flops 2048 | bytes 16384 | tf_op jit(solution)/shard_map/psum | solution.py:281
  626.6 134.2 %all-reduce.5.cloned.1.call-done = (bf16[768,384]{1,0:T(8,128)(2,1)}, bf16[768,384]{1,0:T(8,128)(2,1)}, bf16[192,768]{1,0:T(8,128)(2,1)}, bf16[768,384]{1,0:T(8,...) async-done(((bf16[768,384]{1,0:T(8,128)(2,1)}, bf16[768,384]{1,0:T(8,128)(2,1)}, bf16[192,768]{1,0:T(8,128)(2,1)}, ...) | async-done | bytes 4718608 | tf_op jit(solution)/shard_map/psum | solution.py:284
  760.8 1.9 convert_element_type.48
  (100 shorter events, 29.1 us)
Async XLA Ops:
  7.2 8.1 %copy-start = (bf16[32,3]{0,1:T(4,128)(2,1)S(1)}, bf16[32,3]{0,1:T(4,128)(2,1)}, u32[]{:S(2)}) copy-start(bf16[32,3]{0,1:T(4,128)(2,1)} %param.37) | copy-start | bytes 580
  7.2 2.1 copy-start.7
  7.2 29.8 %all-gather.16.cloned.1.call-start = ((), (), s32[]{:S(2)}) async-start(), calls=%async_computation.16 | async-start | bytes 2949120 | tf_op jit(solution)/shard_map/all_gather | solution.py:270
  9.3 54.0 %all-gather.18.cloned.1.call-start = ((), (), s32[]{:S(2)}) async-start(), calls=%async_computation.17 | async-start | bytes 2949120 | tf_op jit(solution)/shard_map/all_gather | solution.py:270
  10.2 79.3 %all-gather.20.cloned.1.call-start = ((), (), s32[]{:S(2)}) async-start(), calls=%async_computation.18 | async-start | bytes 2949120 | tf_op jit(solution)/shard_map/all_gather | solution.py:270
  11.2 97.2 %all-gather.22.cloned.1.call-start = ((), (), s32[]{:S(2)}) async-start(), calls=%async_computation.19 | async-start | bytes 1474560 | tf_op jit(solution)/shard_map/all_gather | solution.py:270
  11.8 115.5 %all-gather.24.cloned.1.call-start = ((), (), s32[]{:S(2)}) async-start(), calls=%async_computation.20 | async-start | bytes 1474560 | tf_op jit(solution)/shard_map/all_gather | solution.py:270
  12.4 2.3 copy-start.18
  12.4 2.9 copy-start.13
  12.4 153.8 %all-gather.26.cloned.1.call-start = ((), (), s32[]{:S(2)}) async-start(), calls=%async_computation.21 | async-start | bytes 5898240 | tf_op jit(solution)/shard_map/all_gather | solution.py:270
  13.0 192.2 %all-gather.28.cloned.1.call-start = ((), (), s32[]{:S(2)}) async-start(), calls=%async_computation.22 | async-start | bytes 5898240 | tf_op jit(solution)/shard_map/all_gather | solution.py:270
  13.8 311.4 %reduce-scatter.13.cloned.1.call-start = ((), (), s32[]{:S(2)}) async-start(), calls=%async_computation.10 | async-start | bytes 1474560 | tf_op jit(solution)/shard_map/reduce_scatter | solution.py:284
  299.3 54.4 %reduce-scatter.19.cloned.1.call-start = ((), (), s32[]{:S(2)}) async-start(), calls=%async_computation.13 | async-start | bytes 1474560 | tf_op jit(solution)/shard_map/reduce_scatter | solution.py:284
  300.0 89.1 %reduce-scatter.9.cloned.1.call-start = ((), (), s32[]{:S(2)}) async-start(), calls=%async_computation.8 | async-start | bytes 2949120 | tf_op jit(solution)/shard_map/reduce_scatter | solution.py:284
  300.6 124.3 %reduce-scatter.11.cloned.1.call-start = ((), (), s32[]{:S(2)}) async-start(), calls=%async_computation.9 | async-start | bytes 2949120 | tf_op jit(solution)/shard_map/reduce_scatter | solution.py:284
  301.3 159.1 %reduce-scatter.17.cloned.1.call-start = ((), (), s32[]{:S(2)}) async-start(), calls=%async_computation.12 | async-start | bytes 2949120 | tf_op jit(solution)/shard_map/reduce_scatter | solution.py:284
  301.9 209.1 %reduce-scatter.21.cloned.1.call-start = ((), (), s32[]{:S(2)}) async-start(), calls=%async_computation.14 | async-start | bytes 5898240 | tf_op jit(solution)/shard_map/reduce_scatter | solution.py:284
  302.7 258.6 %reduce-scatter.23.cloned.1.call-start = ((), (), s32[]{:S(2)}) async-start(), calls=%async_computation.15 | async-start | bytes 5898240 | tf_op jit(solution)/shard_map/reduce_scatter | solution.py:284
  303.3 299.6 %reduce-scatter.15.cloned.1.call-start = ((), (), s32[]{:S(2)}) async-start(), calls=%async_computation.11 | async-start | bytes 40960 | tf_op jit(solution)/shard_map/reduce_scatter | solution.py:280
  303.8 456.9 %all-reduce.5.cloned.1.call-start = ((), (), s32[]{:S(2)}) async-start(), calls=%async_computation.23 | async-start | bytes 9437184 | tf_op jit(solution)/shard_map/psum | solution.py:284
  561.3 64.6 %copy-start.11 = (f32[32,256]{1,0:T(8,128)S(1)}, f32[32,256]{1,0:T(8,128)}, u32[]{:S(2)}) copy-start(f32[32,256]{1,0:T(8,128)} %constant.30.clone) | copy-start | bytes 98308
  760.8 3.7 copy-start.6
  764.6 2.1 copy-start.3
  772.6 2.1 copy-start.1
  (11 other events, 15.7 us)
Sparse Core Ops, SparseCore 0:
  10.2 26.7 all-gather.15
  39.1 24.0 all-gather.17
  65.4 24.0 all-gather.19
  90.9 17.4 all-gather.21
  109.8 17.4 all-gather.23
  128.7 37.4 all-gather.25
  167.8 37.4 all-gather.27
  299.4 25.7 reduce-scatter.12
  327.9 25.7 reduce-scatter.18
  356.0 33.0 reduce-scatter.8
  391.9 33.0 reduce-scatter.10
  427.3 33.0 reduce-scatter.16
  463.1 47.8 reduce-scatter.20
  513.4 47.8 reduce-scatter.22
  564.2 19.3 reduce-scatter.14
  588.0 172.7 all-reduce.4

commit v2 on v1

v2 whole, which is shorter than its diff:
```python
import math

import jax
import jax.numpy as jnp
import numpy as np
from jax import lax
from jax.experimental import pallas as pl
from jax.experimental.pallas import tpu as pltpu
from jax.sharding import PartitionSpec as P

EPSILON = 1e-6
MASKED = -1e9
BUCKETS = 32
MAX_DISTANCE = 128
F32 = jnp.float32
BF = jnp.bfloat16
NN = (((1,), (0,)), ((), ()))
NT = (((1,), (1,)), ((), ()))
MESH = pl.DeviceIdType.MESH
GATHERED = ("qk", "vq", "so", "ckv", "co", "hin", "hout")
LAST_OF_FEED = ("hout2", 2)
FIRST_REUSE = ("ckv", 0)
CHUNKS = ("hin0", "hout0", "hin1", "hout1", "hin2", "hout2", "co", "ckv", "so", "qk", "vq")


class Remote:
    def __init__(self, *args):
        self.args = args

    def made(self):
        src, dst, send, recv, to = self.args
        return pltpu.make_async_remote_copy(
            src_ref=src, dst_ref=dst, send_sem=send, recv_sem=recv, device_id=to, device_id_type=MESH)

    def start(self):
        self.made().start()

    def wait(self):
        self.made().wait()

    def wait_send(self):
        self.made().wait_send()

    def wait_recv(self):
        self.made().wait_recv()


def mm(a, b, d=NN):
    return lax.dot_general(a, b, d, preferred_element_type=F32)


def inverse_of(h):
    return lax.rsqrt(jnp.mean(h * h, axis=-1, keepdims=True) + EPSILON)


def norm_back(h, inv, g, r):
    s = r * g
    gain = jnp.sum(r * h * inv, axis=0, keepdims=True)
    return inv * s - h * (inv * inv * inv) * jnp.mean(s * h, axis=-1, keepdims=True), gain


def rows_of(start, size):
    return pl.ds(pl.multiple_of(start, 16), size)


def add_into(dst, parts, into=None):
    rows, width = dst.shape
    into = dst if into is None else into
    step = next(n for n in (96, 64, 48, 32, 16) if rows % n == 0 and n * width <= 96 * 768)

    def block(i, _):
        at = rows_of(i * step, step)
        total = dst[at, :].astype(F32)
        for p in parts:
            total = total + p[at, :].astype(F32)
        into[at, :] = total.astype(BF)
        return 0

    lax.fori_loop(0, rows // step, block, 0)


class Chunk:
    def __init__(self, base, row0, rows, col0, width, first, second):
        self.base, self.row0, self.rows, self.col0, self.width = base, row0, rows, col0, width
        self.first, self.second = first, second
        self.by_columns = rows == 192
        self.half = (rows, width // 2) if self.by_columns else (rows // 2, width)
        self.quarter = (self.half[0] // 2, self.half[1])
        self.eighth = (self.half[0] // 4, self.half[1])

    def part(self, shard, row, rows, col, width):
        return self.base.at[shard, rows_of(self.row0 + row, rows), pl.ds(pl.multiple_of(self.col0 + col, 128), width)]

    def whole(self, shard):
        return self.part(shard, 0, self.rows, 0, self.width)

    def place(self, y, z=None, w=None):
        if self.by_columns:
            row, rows, col, width = 0, self.rows, y * (self.width // 2), self.width // 2
        else:
            row, rows, col, width = y * (self.rows // 2), self.rows // 2, 0, self.width
        if z is not None:
            rows = rows // 2
            row = row + z * rows
        if w is not None:
            rows = rows // 2
            row = row + w * rows
        return row, rows, col, width

    def piece(self, shard, *at):
        return self.part(shard, *self.place(*at))

    def result(self, *at):
        row, rows, col, width = self.place(*at)
        return self.second.at[rows_of(row, rows), pl.ds(pl.multiple_of(col, 128), width)]


def bucket_onehot():
    bucket = bucket_of()
    n = lax.broadcasted_iota(jnp.int32, (BUCKETS, 256), 1)
    chosen = jnp.zeros((BUCKETS, 256), jnp.int32)
    for b in range(1, BUCKETS):
        chosen = chosen + jnp.where(n >= int(np.argmax(bucket >= b)), 1, 0)
    return (chosen == lax.broadcasted_iota(jnp.int32, (BUCKETS, 256), 0)).astype(BF)


def layer_kernel(bits, names, *refs):
    R = dict(zip(names, refs, strict=True))
    g = lambda *ns: [R[n] for n in ns]
    tok, mem, cot, lengths, mmask, tags, emb, tab = g("tok", "mem", "cot", "lengths", "mmask", "tags", "emb", "tab")
    vqk, vvq, vso, vckv, vco, vhin, vhout = g("vqk", "vvq", "vso", "vckv", "vco", "vhin", "vhout")
    s0, s1, s2, gst, acc = g("s0", "s1", "s2", "gst", "acc")
    n1, n2, n1T, n2T, n3T, memT = g("n1", "n2", "n1T", "n2T", "n3T", "memT")
    qk1, vx1, q2r, kv2, kvT, mix1, mix2, lse = g("qk1", "vx1", "q2r", "kv2", "kvT", "mix1", "mix2", "lse")
    gvq2, rows, mask2, tagv, btab, sm, smb, gmv = g("gvq2", "rows", "mask2", "tagv", "btab", "sm", "smb", "gmv")
    gsend, grecv, rsend, rrecv, lsem, osem, ssend, srecv, tsend, trecv, credit = g(
        "gsend", "grecv", "rsend", "rrecv", "lsem", "osem", "ssend", "srecv", "tsend", "trecv", "credit")

    dp = lax.axis_index("dp")
    t = lax.axis_index("tensor")
    c = lax.rem(t, 2)
    x = t // 2
    tc = t + 1 - 2 * c
    tx = t + 2 - 4 * x
    td = tc + 2 - 4 * x
    bit = [lax.rem(dp // (1 << b), 2) for b in range(bits)]
    pb = [dp + (1 << b) - (2 << b) * bit[b] for b in range(bits)]
    y, z1, z2 = bit[0], bit[1], bit[2]
    quad, quad_y, quad_z = y + 2 * z1, (1 - y) + 2 * z1, y + 2 * (1 - z1)
    quad_d = 3 - quad

    remote = Remote

    def fwd_shard(s):
        a, b = lax.rem(s, 2), s // 2
        return 2 * (x + b * (1 - 2 * x)) + c + a * (1 - 2 * c)

    def bwd_shard(s):
        a, b = 1 - s // 2, 1 - lax.rem(s, 2)
        return 2 * (x + b * (1 - 2 * x)) + c + a * (1 - 2 * c)

    barrier = pltpu.get_barrier_semaphore()
    partners = [(dp, tc), (dp, tx), (dp, td)] + [(p, t) for p in pb]
    for p in partners:
        pl.semaphore_signal(barrier, inc=1, device_id=p, device_id_type=MESH)
    pl.semaphore_wait(barrier, len(partners))

    weight = {"qk": vqk, "vq": vvq, "so": vso, "ckv": vckv, "co": vco, "hin": vhin, "hout": vhout}
    source = {"so": R["so_in"], "co": R["co_in"], "hin": R["hin_in"], "hout": R["hout_in"]}

    def gather_copies(name):
        i, v = GATHERED.index(name), weight[name]
        height = v.shape[1]
        q = height // 4
        own = source.get(name, v.at[t])

        def copy(j, rws, to, src=None):
            return remote(v.at[tx, rws] if src is None else src, v.at[tx if src is None else t, rws],
                          gsend.at[i, j], grecv.at[i, j], to)

        core = (dp, tc)
        d = {
            "core": remote(own, v.at[t], gsend.at[i, 0], grecv.at[i, 0], core),
            "x": copy(1, rows_of(quad * q, q), (dp, tx), own.at[rows_of(quad * q, q)]),
            "y": copy(2, rows_of(quad * q, q), (pb[0], t)),
            "z": copy(3, rows_of(quad * q, q), (pb[1], t)),
            "cx": copy(4, rows_of(quad * q, q), core),
            "cy": copy(5, rows_of(quad_y * q, q), core),
            "cz": copy(6, rows_of(quad_z * q, q), core),
        }
        if height == 768:
            h = q // 2
            d["yd"] = copy(7, rows_of(quad_z * q, h), (pb[0], t))
            d["zd"] = copy(8, rows_of(quad_y * q + h, h), (pb[1], t))
            d["cyd"] = copy(9, rows_of(quad_d * q, h), core)
            d["czd"] = copy(10, rows_of(quad_d * q + h, h), core)
        elif name == "so":
            d["yd"] = copy(7, rows_of(quad_z * q, q), (pb[0], t))
            d["cyd"] = copy(9, rows_of(quad_d * q, q), core)
        else:
            d["zd"] = copy(8, rows_of(quad_y * q, q), (pb[1], t))
            d["czd"] = copy(10, rows_of(quad_d * q, q), core)
        return d

    def local_copies(name):
        return pltpu.make_async_copy(source[name], weight[name].at[t], lsem.at[GATHERED.index(name)])

    def gather_1(*ns):
        for n in ns:
            d = gather_copies(n)
            d["x"].wait_recv()
            for k in ("y", "z", "cx"):
                d[k].start()

    def gather_2(*ns):
        for n in ns:
            d = gather_copies(n)
            d["y"].wait_recv()
            if "zd" in d:
                d["zd"].start()
            d["cy"].start()
            d["z"].wait_recv()
            if "yd" in d:
                d["yd"].start()
            d["cz"].start()

    def gather_3(*ns):
        for n in ns:
            d = gather_copies(n)
            for a, b in (("yd", "cyd"), ("zd", "czd")):
                if a in d:
                    d[a].wait_recv()
                    d[b].start()

    def gather_4(*ns):
        for n in ns:
            d = gather_copies(n)
            for k in ("cx", "cy", "cz", "cyd", "czd"):
                if k in d:
                    d[k].wait_recv()

    def gather_core(*ns):
        for n in ns:
            gather_copies(n)["core"].wait_recv()
            if n in source:
                local_copies(n).wait()

    def gather_sent(*ns):
        for n in ns:
            for d in gather_copies(n).values():
                d.wait_send()

    for n in source:
        local_copies(n).start()
    for n, a, b in (("qk", "sq", "sk"), ("vq", "sv", "cq")):
        weight[n][t] = jnp.concatenate([R[a][...], R[b][...]], axis=0).T
    for n in ("qk", "vq", "so"):
        d = gather_copies(n)
        d["x"].start()
        d["core"].start()
    btab[t, 0:3, :] = mm(tab[...], bucket_onehot())
    table_copies = [remote(btab.at[t], btab.at[t], tsend.at[j], trecv.at[j], (dp, to)) for j, to in enumerate((tc, tx, td))]
    for d in table_copies:
        d.start()
    vckv[t] = jnp.concatenate([R["ck"][...], R["cv"][...]], axis=0).T
    for n in ("ckv", "co", "hin", "hout"):
        d = gather_copies(n)
        d["x"].start()
        d["core"].start()

    f = CHUNKS.index
    table = {}
    for n in CHUNKS:
        if n.startswith("hin"):
            k = int(n[3:]) * 256
            table[n] = Chunk(vhin, 0, 768, k, 256, R["rb1a"].at[:, :, pl.ds(k, 256)], R["rb2hin"].at[:, pl.ds(k, 256)])
        elif n.startswith("hout"):
            k = int(n[4:]) * 256
            table[n] = Chunk(vhout, k, 256, 0, 768, R["rb1b"].at[:, pl.ds(k, 256), :], R["rb2hout"].at[pl.ds(k, 256), :])
        else:
            rb1 = {"ckv": lambda: R["rb1a"].at[:, :, pl.ds(0, 384)], "qk": lambda: R["rb1a"].at[:, :, pl.ds(384, 384)],
                   "vq": lambda: R["rb1b"].at[:, :, pl.ds(0, 384)], "so": lambda: R["rb1so"], "co": lambda: R["rb1co"]}[n]()
            v = weight[n]
            table[n] = Chunk(v, 0, v.shape[1], 0, v.shape[2], rb1, R["rb2" + n])
    outs = {"hin": R["ohin"], "hout": R["ohout"], "co": R["oco"], "ckv": R["ockv"], "so": R["oso"], "qk": R["oqk"], "vq": R["ovq"]}

    def r_copy(n, j):
        k, i = table[n], f(n)
        sems = (rsend.at[i, j], rrecv.at[i, j])
        if j == 0:
            return remote(k.whole(td), k.first.at[0], *sems, (dp, tc))
        if j == 1:
            return remote(k.whole(tc), k.first.at[1], *sems, (dp, tc))
        if j == 2:
            return remote(k.whole(tx), k.second, *sems, (dp, tx))
        if j == 3:
            return remote(k.piece(t, 1 - y), R["yb_" + n], *sems, (pb[0], t))
        if j == 4:
            return remote(k.piece(t, y, 1 - z1), R["zb_" + n], *sems, (pb[1], t))
        if j == 5:
            return remote(k.piece(t, y, z1, 1 - z2), R["wb_" + n], *sems, (pb[2], t))
        if j == 6:
            e = k.result(y, z1, z2)
            return remote(e, e, *sems, (pb[2], t))
        if j == 7:
            e = k.result(y, z1)
            return remote(e, e, *sems, (pb[1], t))
        if j == 8:
            e = k.result(y)
            return remote(e, e, *sems, (pb[0], t))
        e = k.piece(t, y, z1, z2)
        return remote(e, R["eb_" + n].at[j - 9], *sems, (pb[j - 6], t))

    def out_copy(n):
        k = table[n]
        if n.startswith("hin"):
            dst = outs["hin"].at[:, pl.ds(k.col0, 256)]
        elif n.startswith("hout"):
            dst = outs["hout"].at[pl.ds(k.row0, 256), :]
        else:
            dst = outs[n]
        return pltpu.make_async_copy(k.second, dst, osem.at[f(n)])

    def step(n, j):
        k = table[n]
        if j == 0:
            r_copy(n, 0).start()
            r_copy(n, 1).start()
        elif j == 1:
            r_copy(n, 0).wait_recv()
            add_into(k.whole(tx), [k.first.at[0]])
            r_copy(n, 2).start()
        elif j == 2:
            r_copy(n, 1).wait_recv()
            add_into(k.whole(t), [k.first.at[1]])
        elif j == 3:
            r_copy(n, 2).wait_recv()
            add_into(k.whole(t), [k.second])
            r_copy(n, 3).start()
        elif j == 4:
            r_copy(n, 3).wait_recv()
            add_into(k.piece(t, y), [R["yb_" + n]])
            r_copy(n, 4).start()
        elif j == 5:
            r_copy(n, 4).wait_recv()
            add_into(k.piece(t, y, z1), [R["zb_" + n]])
            r_copy(n, 5).start()
        elif j == 6:
            r_copy(n, 5).wait_recv()
            own = k.piece(t, y, z1, z2)
            add_into(own, [R["wb_" + n]], k.result(y, z1, z2) if bits == 3 else None)
            for b in range(3, bits):
                r_copy(n, 6 + b).start()
                r_copy(n, 6 + b).wait()
                add_into(own, [R["eb_" + n].at[b - 3]], k.result(y, z1, z2) if b == bits - 1 else None)
            r_copy(n, 6).start()
        elif j == 7:
            r_copy(n, 6).wait_recv()
            r_copy(n, 7).start()
        elif j == 8:
            r_copy(n, 7).wait_recv()
            r_copy(n, 8).start()
        elif j == 9:
            r_copy(n, 8).wait_recv()
            out_copy(n).start()

    to = [(dp, tc), (dp, tx)] + [(p, t) for p in pb]

    def small_step(j):
        if j:
            copy = remote(sm, smb.at[j - 1], ssend.at[j - 1], srecv.at[j - 1], to[j - 1])
            copy.wait()
            sm[...] = sm[...] + smb[j - 1]
        if j < len(to):
            remote(sm, smb.at[j], ssend.at[j], srecv.at[j], to[j]).start()

    def run(place):
        for n, j in SCHEDULE[place]:
            if n == "small":
                small_step(j)
                continue
            if (n, j) == FIRST_REUSE:
                pl.semaphore_wait(credit, 1)
            step(n, j)
            if (n, j) == LAST_OF_FEED:
                pl.semaphore_signal(credit, inc=1, device_id=(dp, tc), device_id_type=MESH)

    g_self, g_cross, g_hid = (R[n][...].astype(F32).reshape(1, 768) for n in ("gain1", "gain2", "gain3"))
    lane384 = lax.broadcasted_iota(jnp.int32, (1, 384), 1)
    ji = lax.broadcasted_iota(jnp.int32, (256, 256), 0)
    ii = lax.broadcasted_iota(jnp.int32, (256, 256), 1)
    length = lengths[t]
    allowed = lambda: (ji <= ii) & (ji < length)
    tagv[...] = jnp.broadcast_to((tags[...] == 1).astype(F32), (128, 256)).T
    tagged = lambda: jnp.concatenate([tagv[...]] * 6, axis=1) > 0.5
    x0 = tok[...].astype(F32) + jnp.where(tagged(), emb[1:2, :].astype(F32), emb[0:1, :].astype(F32))
    s0[...] = x0
    nn = (x0 * inverse_of(x0) * g_self).astype(BF)
    n1[...] = nn
    n1T[...] = nn.T
    gather_core("qk", "vq")
    for d in table_copies:
        d.wait_recv()

    def bias_of(shard, i):
        return pltpu.roll(jnp.broadcast_to(btab[shard, i:i + 1, :], (256, 256)), 0, 1, stride=1, stride_axis=0)

    def project_memory(shard):
        def block(r, _):
            at = rows_of(r * 256, 256)
            kv2[shard, at, :] = mm(mem[at, :], vckv[shard]).astype(BF)
            return 0
        lax.fori_loop(0, 4, block, 0)

    def transpose_memory():
        valid = mmask[pl.ds(t, 1), :]
        mask2[...] = jnp.broadcast_to(jnp.where(valid == 1, 0.0, MASKED).astype(F32), (128, 1024)).T
        memT[...] = mem[...].T

    def hooks(s, table_of):
        for k, todo in table_of.items():
            @pl.when(s == k)
            def _():
                todo()

    def before_far_shards():
        gather_1("qk")
        transpose_memory()
        gather_1("vq")
        gather_core("ckv")
        project_memory(t)
        gather_1("so")
        gather_2("qk")
        project_memory(tc)
        gather_2("vq", "so")
        gather_1("ckv", "co")
        gather_3("qk", "vq", "so")
        gather_4("qk", "vq")

    def self_forward(s, _):
        hooks(s, {2: before_far_shards, 3: lambda: (gather_2("ckv", "co"), gather_1("hin"))})
        k = fwd_shard(s)
        a = mm(n1[...], vqk[k])
        qk1[k] = jnp.where(lane384 < 192, a * 0.125, a).astype(BF)
        v = mm(n1[...], vvq[k]).astype(BF)
        vx1[k] = v
        vT = v.T
        for i in range(3):
            q, kk = qk1[k, :, 64 * i:64 * i + 64], qk1[k, :, 192 + 64 * i:256 + 64 * i]
            scores = jnp.where(allowed(), mm(kk, q, NT) + bias_of(k, i), MASKED)
            most = jnp.max(scores, axis=0, keepdims=True)
            p = jnp.exp(scores - most)
            total = jnp.sum(p, axis=0, keepdims=True)
            o = mm(vT[64 * i:64 * i + 64, :], p.astype(BF))
            mix1[k, 64 * i:64 * i + 64, :] = (o / total).astype(BF)
            lse[k, i:i + 1, :] = most + jnp.log(total)
        return 0

    lax.fori_loop(0, 4, self_forward, 0)
    gather_3("ckv", "co")
    gather_core("so")
    gather_4("so")

    def project_out(target, mix, w):
        def block(k, _):
            target[...] += mm(mix[k].T, w[k])
            return 0
        lax.fori_loop(0, 4, block, 0)

    s1[...] = s0[...]
    project_out(s1, mix1, vso)
    x1 = s1[...]
    nn = (x1 * inverse_of(x1) * g_cross).astype(BF)
    n2[...] = nn
    n2T[...] = nn.T

    def cross_scores(shard, i, r, q):
        at = slice(256 * r, 256 * r + 256)
        return mm(kv2[shard, at, 64 * i:64 * i + 64], q, NT) + jnp.concatenate([mask2[at, :]] * 2, axis=1)

    def cross_forward(s, _):
        def far():
            gather_4("ckv")
            gather_2("hin")
            project_memory(tx)

        hooks(s, {1: lambda: gather_1("hout"), 2: far, 3: lambda: (project_memory(td), gather_3("hin"), gather_2("hout"))})
        k = fwd_shard(s)
        q2r[k] = (mm(n2[...], vvq[k]) * 0.125).astype(BF)
        kvT[...] = kv2[k, :, 128:384].T
        for i in range(3):
            q = q2r[k, :, 192 + 64 * i:256 + 64 * i]
            ss = [cross_scores(k, i, r, q) for r in range(4)]
            most = jnp.max(jnp.maximum(jnp.maximum(ss[0], ss[1]), jnp.maximum(ss[2], ss[3])), axis=0, keepdims=True)
            total, o = 0.0, 0.0
            for r in range(4):
                p = jnp.exp(ss[r] - most)
                total = total + jnp.sum(p, axis=0, keepdims=True)
                o = o + mm(kvT[64 + 64 * i:128 + 64 * i, 256 * r:256 * r + 256], p.astype(BF))
            mix2[k, 64 * i:64 * i + 64, :] = (o / total).astype(BF)
            lse[4 + k, i:i + 1, :] = most + jnp.log(total)
        return 0

    lax.fori_loop(0, 4, cross_forward, 0)
    gather_core("co")
    gather_4("co")
    s2[...] = s1[...]
    project_out(s2, mix2, vco)
    x2 = s2[...]
    nn = (x2 * inverse_of(x2) * g_hid).astype(BF)
    n3T[...] = nn.T
    rows[...] = nn
    acc[...] = x2
    gst[...] = jnp.zeros_like(x2)
    gather_core("hin", "hout")

    def feed(j, _):
        def far():
            gather_3("hout")
            gather_4("hin", "hout")
            gather_sent("hin", "hout")

        hooks(j, {6: far, 8: lambda: run("feed8"), 10: lambda: run("feed10")})
        k = fwd_shard(lax.rem(j, 2) + 2 * (j // 6))
        cs = pl.ds(pl.multiple_of((lax.rem(j, 6) // 2) * 256, 256), 256)
        v = mm(rows[...], vhin[k, :, cs])
        phi = 0.5 * (1.0 + lax.erf(v * np.float32(1 / math.sqrt(2))))
        act = (v * phi).astype(BF)
        slope = phi + v * (jnp.exp(-0.5 * v * v) * np.float32(1 / math.sqrt(2 * math.pi)))
        acc[...] += mm(act, vhout[k, cs, :])
        gb = (slope * mm(cot[...], vhout[k, cs, :], NT)).astype(BF)
        gst[...] += mm(gb, vhin[k, :, cs], NT)
        vhin[k, :, cs] = mm(n3T[...], gb).astype(BF)
        vhout[k, cs, :] = mm(act.T, cot[...]).astype(BF)
        return 0

    lax.fori_loop(0, 12, feed, 0)
    run("feed_end")
    gather_sent("qk", "vq", "so", "ckv", "co")
    for d in table_copies:
        d.wait_send()
    lo_v, gt_v = R["lov"], R["gtv"]
    lo_v[...] = acc[...].astype(BF)
    lo_copy = pltpu.make_async_copy(lo_v, R["lo"], lsem.at[7])
    lo_copy.start()
    d, gain = norm_back(x2, inverse_of(x2), g_hid, gst[...])

    def put_small(row, value):
        for i in range(3):
            at = 3 * row + i
            sm[at // 8, at % 8:at % 8 + 1, :] = value[:, 256 * i:256 * i + 256]

    sm[...] = jnp.zeros_like(sm)
    put_small(4, gain)
    gst[...] = cot[...].astype(F32) + d
    run("norm3")
    rows[...] = gst[...].astype(BF)
    acc[...] = jnp.zeros_like(x2)

    def cross_backward(s, _):
        hooks(s, {i: (lambda i=i: run("cross%d" % i)) for i in range(4)})
        k = bwd_shard(s)
        rw = rows[...]
        w = vco[k]
        G = mm(rw, w, NT).astype(BF)
        GT = mm(w, rw, NT).astype(BF)
        vco[k] = mm(mix2[k], rw).astype(BF)
        kvT[...] = kv2[k, :, 0:256].T
        dqs, dks, dvs = [], [], []
        for i in range(3):
            q = q2r[k, :, 192 + 64 * i:256 + 64 * i]
            gi = G[:, 64 * i:64 * i + 64]
            r = jnp.sum(mix2[k, 64 * i:64 * i + 64, :].astype(F32) * GT[64 * i:64 * i + 64, :].astype(F32), axis=0, keepdims=True)
            ls = lse[4 + k, i:i + 1, :]
            dq, dk, dv = 0.0, [], []
            for b in range(4):
                at = slice(256 * b, 256 * b + 256)
                p = jnp.exp(cross_scores(k, i, b, q) - ls)
                dp_ = mm(kv2[k, at, 192 + 64 * i:256 + 64 * i], gi, NT)
                gs = (p * (dp_ - r)).astype(BF)
                dv.append(mm(p.astype(BF), gi).astype(BF))
                dk.append(mm(gs, q).astype(BF))
                dq = dq + mm(kvT[64 * i:64 * i + 64, at], gs)
            dqs.append(dq * 0.125)
            dks.append(dk)
            dvs.append(dv)
        for b in range(4):
            kv2[k, 256 * b:256 * b + 256, :] = jnp.concatenate([v[b] for v in dks + dvs], axis=1)
        gvq2[k, :, 192:384] = jnp.concatenate(dqs, axis=0).astype(BF).T
        acc[...] += mm(jnp.where(lane384 >= 192, gvq2[k], 0).astype(BF), vvq[k], NT)
        return 0

    lax.fori_loop(0, 4, cross_backward, 0)
    run("cross_end")

    def memory_grad(r, _):
        at = rows_of(r * 256, 256)
        total = mm(kv2[0, at, :], vckv[0], NT)
        for k in range(1, 4):
            total = total + mm(kv2[k, at, :], vckv[k], NT)
        gmv[at, :] = total.astype(BF)
        return 0

    lax.fori_loop(0, 4, memory_grad, 0)
    gm_copy = pltpu.make_async_copy(gmv, R["gmem"], lsem.at[8])
    gm_copy.start()
    run("mem_half")

    def memory_weights(s, _):
        k = bwd_shard(s)

        def block(r, _):
            at = rows_of(r * 256, 256)
            vckv[k, at, :] = mm(memT[at, :], kv2[k]).astype(BF)
            return 0
        lax.fori_loop(0, 3, block, 0)
        return 0

    lax.fori_loop(0, 4, memory_weights, 0)
    run("mem_end")
    d, gain = norm_back(s1[...], inverse_of(s1[...]), g_cross, acc[...])
    put_small(3, gain)
    gst[...] += d
    rows[...] = gst[...].astype(BF)
    acc[...] = jnp.zeros_like(x2)

    def self_backward(s, _):
        hooks(s, {i: (lambda i=i: run("self%d" % i)) for i in range(4)})
        k = bwd_shard(s)
        rw = rows[...]
        w = vso[k]
        G = mm(rw, w, NT).astype(BF)
        GT = mm(w, rw, NT).astype(BF)
        vso[k] = mm(mix1[k], rw).astype(BF)
        kT = qk1[k, :, 128:384].T
        flip = (ji + ii == 255).astype(BF)
        dqs, dks, dvs = [], [], []
        for i in range(3):
            q, kk = qk1[k, :, 64 * i:64 * i + 64], qk1[k, :, 192 + 64 * i:256 + 64 * i]
            gi = G[:, 64 * i:64 * i + 64]
            r = jnp.sum(mix1[k, 64 * i:64 * i + 64, :].astype(F32) * GT[64 * i:64 * i + 64, :].astype(F32), axis=0, keepdims=True)
            scores = jnp.where(allowed(), mm(kk, q, NT) + bias_of(k, i), MASKED)
            p = jnp.exp(scores - lse[k, i:i + 1, :])
            dp_ = mm(vx1[k, :, 64 * i:64 * i + 64], gi, NT)
            gs = (p * (dp_ - r)).astype(BF)
            dvs.append(mm(p.astype(BF), gi).astype(BF))
            dks.append(mm(gs, q).astype(BF))
            dqs.append(mm(kT[64 + 64 * i:128 + 64 * i, :], gs) * 0.125)
            shifted = pltpu.roll(mm(flip, gs), 1, 1, stride=1, stride_axis=0)
            sm[2 + k, i:i + 1, :] = jnp.sum(shifted, axis=0, keepdims=True)
        g_qk = jnp.concatenate([jnp.concatenate(dqs, axis=0).astype(BF).T] + dks, axis=1)
        g_vq = jnp.concatenate(dvs + [gvq2[k, :, 192:384]], axis=1)
        acc[...] += mm(g_qk, vqk[k], NT) + mm(jnp.where(lane384 < 192, g_vq, 0).astype(BF), vvq[k], NT)
        vqk[k] = mm(n1T[...], g_qk).astype(BF)
        vvq[k] = jnp.where(lane384 < 192, mm(n1T[...], g_vq), mm(n2T[...], g_vq)).astype(BF)
        return 0

    lax.fori_loop(0, 4, self_backward, 0)
    run("self_end")
    d, gain = norm_back(s0[...], inverse_of(s0[...]), g_self, acc[...])
    put_small(2, gain)
    g0 = gst[...] + d
    gt_v[...] = g0.astype(BF)
    gt_copy = pltpu.make_async_copy(gt_v, R["gtok"], lsem.at[9])
    gt_copy.start()
    put_small(0, jnp.sum(jnp.where(tagged(), 0.0, g0), axis=0, keepdims=True))
    put_small(1, jnp.sum(jnp.where(tagged(), g0, 0.0), axis=0, keepdims=True))

    run("fin")
    run("end")
    for j in range(6, len(to) + 1):
        small_step(j)
    R["smo"][...] = sm[0:2]
    R["dgo"][...] = sm[2 + t]
    for n in CHUNKS:
        for j in range(9 + bits - 3):
            if j < 9:
                r_copy(n, j).wait_send()
        out_copy(n).wait()
    lo_copy.wait()
    gm_copy.wait()
    gt_copy.wait()


SCHEDULE = {
    'feed8': (('hin0', 0), ('hout0', 0),),
    'feed10': (('hin1', 0), ('hout1', 0), ('hin0', 1), ('hin0', 2),),
    'feed_end': (('hout0', 1), ('hin1', 1), ('hout1', 1), ('hin2', 0), ('hout2', 0), ('hout0', 2), ('hin1', 2), ('hout1', 2),),
    'norm3': (('hin2', 1),),
    'cross0': (('hin2', 2), ('hout2', 1),),
    'cross1': (('hin0', 3), ('hout2', 2),),
    'cross2': (('co', 0),),
    'cross3': (('co', 1), ('hin0', 4), ('hout0', 3),),
    'cross_end': (('hin1', 3), ('hin0', 5), ('co', 2),),
    'mem_half': (('hin0', 6), ('hout0', 4),),
    'mem_end': (('ckv', 0), ('hin0', 7), ('hin1', 4), ('hout1', 3), ('hout0', 5),),
    'self0': (),
    'self1': (('ckv', 1), ('hin0', 8), ('hin2', 3), ('ckv', 2), ('hin1', 5),),
    'self2': (('so', 0), ('hout0', 6), ('hout1', 4),),
    'self3': (('so', 1), ('hin0', 9), ('hin1', 6), ('hout2', 3),),
    'self_end': (('qk', 0), ('vq', 0), ('hout0', 7), ('hout1', 5), ('hin2', 4), ('so', 2), ('hin1', 7), ('co', 3),),
    'fin': (('small', 0), ('qk', 1), ('hout0', 8), ('vq', 1), ('hout2', 4), ('qk', 2), ('small', 1), ('hout1', 6), ('co', 4), ('vq', 2),),
    'end': (('hin2', 5), ('hin1', 8), ('hout0', 9), ('hout2', 5), ('ckv', 3), ('hout1', 7), ('co', 5), ('hin1', 9), ('hin2', 6), ('so', 3), ('hout2', 6), ('hout1', 8), ('ckv', 4), ('co', 6), ('so', 4), ('hin2', 7), ('hout2', 7), ('hout1', 9), ('qk', 3), ('ckv', 5), ('co', 7), ('so', 5), ('hin2', 8), ('hout2', 8), ('qk', 4), ('ckv', 6), ('vq', 3), ('hin2', 9), ('co', 8), ('small', 2), ('so', 6), ('hout2', 9), ('qk', 5), ('ckv', 7), ('so', 7), ('vq', 4), ('qk', 6), ('co', 9), ('small', 3), ('ckv', 8), ('so', 8), ('vq', 5), ('qk', 7), ('ckv', 9), ('small', 4), ('so', 9), ('vq', 6), ('qk', 8), ('small', 5), ('vq', 7), ('qk', 9), ('vq', 8), ('vq', 9),),
}


def layer(bits, ins):
    S = jax.ShapeDtypeStruct
    V, A, M = (pl.BlockSpec(memory_space=s) for s in (pltpu.VMEM, pl.ANY, pltpu.SMEM))
    vm = pltpu.VMEM
    in_names = ("tok", "mem", "cot", "lengths", "mmask", "tags", "emb", "gain1", "gain2", "gain3", "tab", "sq", "sk", "sv", "cq", "ck", "cv",
                "so_in", "co_in", "hin_in", "hout_in")
    in_specs = [V, V, V, M] + [V] * 13 + [A] * 4
    out = {
        "lo": S((256, 768), BF), "gtok": S((256, 768), BF), "gmem": S((1024, 768), BF), "smo": S((2, 8, 256), F32), "dgo": S((8, 256), F32),
        "oqk": S((768, 384), BF), "ovq": S((768, 384), BF), "ockv": S((768, 384), BF), "oso": S((192, 768), BF), "oco": S((192, 768), BF),
        "ohin": S((768, 768), BF), "ohout": S((768, 768), BF),
    }
    out_specs = [V if n in ("smo", "dgo") else A for n in out]
    wide, tall = (256, 768), (768, 256)
    scratch = {
        "vqk": vm((4, 768, 384), BF), "vvq": vm((4, 768, 384), BF), "vckv": vm((4, 768, 384), BF),
        "vso": vm((4, 192, 768), BF), "vco": vm((4, 192, 768), BF), "vhin": vm((4, 768, 768), BF), "vhout": vm((4, 768, 768), BF),
        "s0": vm(wide, F32), "s1": vm(wide, F32), "s2": vm(wide, F32), "gst": vm(wide, F32), "acc": vm(wide, F32),
        "n1": vm(wide, BF), "n2": vm(wide, BF), "n1T": vm(tall, BF), "n2T": vm(tall, BF), "n3T": vm(tall, BF), "memT": vm((768, 1024), BF),
        "qk1": vm((4, 256, 384), BF), "vx1": vm((4, 256, 384), BF), "q2r": vm((4, 256, 384), BF), "kv2": vm((4, 1024, 384), BF),
        "kvT": vm((256, 1024), BF), "mix1": vm((4, 192, 256), BF), "mix2": vm((4, 192, 256), BF), "lse": vm((8, 8, 256), F32),
        "gvq2": vm((4, 256, 384), BF), "rows": vm(wide, BF), "mask2": vm((1024, 128), F32), "tagv": vm((256, 128), F32),
        "btab": vm((4, 8, 256), F32), "sm": vm((6, 8, 256), F32), "smb": vm((2 + bits, 6, 8, 256), F32), "gmv": vm((1024, 768), BF),
        "lov": vm(wide, BF), "gtv": vm(wide, BF),
        "rb1a": vm((2, 768, 768), BF), "rb1b": vm((2, 768, 768), BF), "rb1so": vm((2, 192, 768), BF), "rb1co": vm((2, 192, 768), BF),
        "rb2hin": vm((768, 768), BF), "rb2hout": vm((768, 768), BF),
        "rb2co": vm((192, 768), BF), "rb2so": vm((192, 768), BF), "rb2ckv": vm((768, 384), BF), "rb2qk": vm((768, 384), BF), "rb2vq": vm((768, 384), BF),
    }
    shape_of = {"hin": (768, 256), "hou": (256, 768), "co": (192, 768), "so": (192, 768), "ckv": (768, 384), "qk": (768, 384), "vq": (768, 384)}
    for n in CHUNKS:
        r, w = shape_of[n[:3]]
        k = Chunk(None, 0, r, 0, w, None, None)
        scratch["yb_" + n], scratch["zb_" + n], scratch["wb_" + n] = vm(k.half, BF), vm(k.quarter, BF), vm(k.eighth, BF)
        if bits > 3:
            scratch["eb_" + n] = vm((bits - 3,) + k.eighth, BF)
    dma = pltpu.SemaphoreType.DMA
    sems = {
        "gsend": dma((7, 11)), "grecv": dma((7, 11)), "rsend": dma((11, 6 + bits)), "rrecv": dma((11, 6 + bits)), "lsem": dma((10,)),
        "osem": dma((11,)), "ssend": dma((2 + bits,)), "srecv": dma((2 + bits,)), "tsend": dma((3,)), "trecv": dma((3,)),
        "credit": pltpu.SemaphoreType.REGULAR,
    }
    names = in_names + tuple(out) + tuple(scratch) + tuple(sems)

    def kernel(*refs):
        layer_kernel(bits, names, *refs)

    return pl.pallas_call(
        kernel, out_shape=list(out.values()), in_specs=in_specs, out_specs=out_specs,
        scratch_shapes=list(scratch.values()) + list(sems.values()),
        compiler_params=pltpu.CompilerParams(collective_id=0, has_side_effects=True, vmem_limit_bytes=VMEM_LIMIT),
    )(*ins)


VMEM_LIMIT = 64 * 1024 * 1024 - 64 * 1024


def bucket_of(length=256):
    exact = BUCKETS // 2
    n = np.arange(length)
    far = exact + np.floor(np.log(np.maximum(n, 1) / exact) / math.log(MAX_DISTANCE / exact) * (BUCKETS - exact)).astype(np.int32)
    return np.where(n < exact, n, np.minimum(far, BUCKETS - 1)).astype(np.int32)


def finish_kernel(lo, gtok, gmem, smo, dgo, qk, vq, ckv, so, co, hin, hout,
                  o_lo, o_gtok, o_gmem, o_emb, o_g1, o_g2, o_g3, o_sq, o_sk, o_sv, o_so, o_pb, o_cq, o_ck, o_cv, o_co, o_hin, o_hout):
    o_lo[...] = lo[...]
    o_gtok[...] = gtok[...]
    o_gmem[...] = gmem[...]
    for source, first, second in ((qk, o_sq, o_sk), (vq, o_sv, o_cq), (ckv, o_ck, o_cv)):
        turned = source[...].T.astype(F32)
        first[...] = turned[0:192, :]
        second[...] = turned[192:384, :]
    o_so[...] = so[...].astype(F32)
    o_co[...] = co[...].astype(F32)
    o_hin[...] = hin[...].astype(F32)
    o_hout[...] = hout[...].astype(F32)

    @pl.when(pl.program_id(0) == 0)
    def _():
        def small(row):
            return jnp.concatenate([smo[(3 * row + i) // 8, (3 * row + i) % 8:(3 * row + i) % 8 + 1, :] for i in range(3)], axis=1)
        o_emb[0:1, :] = small(0)
        o_emb[1:2, :] = small(1)
        o_g1[...] = small(2).reshape(768)
        o_g2[...] = small(3).reshape(768)
        o_g3[...] = small(4).reshape(768)
        total = lax.dot_general(dgo[...], bucket_onehot().astype(F32), NT, precision=lax.Precision.HIGHEST, preferred_element_type=F32)
        o_pb[...] = total[0:3, :]


def finish(args):
    S = jax.ShapeDtypeStruct
    n = 2
    cut = lambda r, w: pl.BlockSpec((r // n, w), lambda i: (i, 0))
    turned = pl.BlockSpec((192, 768 // n), lambda i: (0, i))
    full = lambda *s: pl.BlockSpec(s, lambda i: (0,) * len(s))
    flat, square = (192, 768), (768, 768)
    ends = [cut(256, 768), cut(256, 768), cut(1024, 768)]
    in_specs = ends + [full(2, 8, 256), full(8, 256)] + [cut(768, 384)] * 3 + [cut(*flat)] * 2 + [cut(*square)] * 2
    shapes = [S((256, 768), BF), S((256, 768), BF), S((1024, 768), BF), S((2, 768), F32)] + [S((768,), F32)] * 3
    shapes += [S(flat, F32)] * 3 + [S(flat, F32), S((3, 32), F32)] + [S(flat, F32)] * 3 + [S(flat, F32), S(square, F32), S(square, F32)]
    out_specs = ends + [full(2, 768)] + [full(768)] * 3
    out_specs += [turned] * 3 + [cut(*flat), full(3, 32)] + [turned] * 3 + [cut(*flat), cut(*square), cut(*square)]
    return pl.pallas_call(finish_kernel, grid=(n,), out_shape=shapes, in_specs=in_specs, out_specs=out_specs,
                          compiler_params=pltpu.CompilerParams(vmem_limit_bytes=VMEM_LIMIT))(*args)


def per_device(bits, tokens, memory, cotangent, lengths, memory_mask, token_tags, embedding, gain_self, gain_cross, gain_hidden,
               self_query, self_key, self_value, self_output, position_bias, cross_query, cross_key, cross_value,
               cross_output, hidden_in, hidden_out):
    lo, gtok, gmem, smo, dgo, qk, vq, ckv, so, co, hin, hout = layer(bits, (
        tokens[0], memory[0], cotangent[0], lengths, memory_mask, token_tags, embedding, gain_self, gain_cross, gain_hidden, position_bias.T,
        self_query.T, self_key.T, self_value.T, cross_query.T, cross_key.T, cross_value.T, self_output, cross_output, hidden_in, hidden_out))
    (lo, gtok, gmem, g_emb, g1, g2, g3, sq, sk, sv, g_so, pb, cq, ck, cv, g_co, hi, ho) = finish(
        (lo, gtok, gmem, smo, dgo, qk, vq, ckv, so, co, hin, hout))
    return (lo[None], gtok[None], gmem[None], g_emb, g1, g2, g3, sq.T, sk.T, sv.T, g_so, pb.T, cq.T, ck.T, cv.T, g_co, hi, ho)


def solution(mesh):
    bits = int(math.log2(mesh.shape["dp"]))
    item = P(("dp", "tensor"), None, None)
    col, row, rep = P(None, "tensor"), P("tensor", None), P()
    in_specs = (item, item, item, P("dp"), P("dp", None), P(("dp", "tensor"), None), rep, rep, rep, rep,
                col, col, col, row, col, col, col, col, row, col, row)
    out_specs = (item, item, item, rep, rep, rep, rep, col, col, col, row, col, col, col, col, row, col, row)
    return jax.shard_map(lambda *a: per_device(bits, *a), mesh=mesh, in_specs=in_specs, out_specs=out_specs, check_vma=False)
```

time: 782 us -> 232 us (0.30)
  waiting for transfers between devices: 567 us -> 0 us
  Pallas kernels: 92.2 us -> 231 us
  blocking collectives: 69.2 us -> 0 us
  local copies, waits for them, and re-layouts: 24.6 us -> 0 us
  between operations: 14.2 us -> 0.83 us
  other arithmetic: 13.1 us -> 0 us
    reduce_scatter x8 -> x0, waiting for transfers between devices: 257 us -> none  [the longest x7 257 us: per_device(): lax.psum_scatter(g, 'tensor', scatter_dimension=0, tiled=False)]
    all_gather x7 -> x0, waiting for transfers between devices: 168 us -> none  [per_device(): gather = lambda w: lax.all_gather(w, 'tensor', axis=0)]
    pallas_call x1 -> x2, Pallas kernels: 92.2 us -> 231 us  [the longest x1 223 us: layer(): pl.pallas_call(kernel, out_shape=list(out.values()), in_specs=in_specs, o...]
    psum x1 -> x0, waiting for transfers between devices: 134 us -> none  [per_device(): lax.psum(tuple((lax.psum_scatter(g, 'tensor', scatter_dimension=0, tiled=...]
    psum x2 -> x0, blocking collectives: 62.6 us -> none  [the longest x1 39.6 us: per_device(): small = lax.psum(small, ('dp', 'tensor'))]
    all_gather x3 -> x0, local copies, waits for them, and re-layouts: 12.8 us -> none  [per_device(): gather = lambda w: lax.all_gather(w, 'tensor', axis=0)]
    convert_element_type x7 -> x0, other arithmetic: 8.06 us -> none  [the longest x6 7.42 us: per_device(): f = lambda x: x.astype(F32)]
  transfers between devices with their start and end apart: 16 -> 0, of which waited for: 15 -> 0; matrix products, arithmetic and copies ran while one was open for 3% -> 0% of each run, Pallas kernels for 0% -> 0%
where the time goes in v2:
time: 232 us; the launch traced here: 231 us
  Pallas kernels  231 us (100%)
    pallas_call x1, Pallas kernels, layer(): pl.pallas_call(kernel, out_shape=list(out.values()), in_specs=in_specs, o...  223 us
    pallas_call x1, Pallas kernels, finish(): pl.pallas_call(finish_kernel, grid=(n,), out_shape=shapes, in_specs=in_sp...  7.22 us

profile of v2, /device:TPU:0, one launch (start us, length us, event | category | flops | bytes accessed | tf_op | source)
XLA Modules:
  0.0 231.3 jit_solution(1752478804468198937)
XLA Ops:
  0.7 223.3 %shard_map.340 = (bf16[256,768]{1,0:T(8,128)(2,1)}, bf16[256,768]{1,0:T(8,128)(2,1)}, bf16[1024,768]{1,0:T(8,128)(2,1)}, f32[2,8,256]{2,1,0:T(8,128)}, f32[8,256...) custom-call(bf16[256,768]{1,0:T(8,128)(2,1)} %bitcast.21, ...), custom_call_target="tpu_custom_call" | custom-call | tf_op jit(solution)/shard_map/pallas_call | solution.py:753
  224.0 7.2 %shard_map.341 = (bf16[256,768]{1,0:T(8,128)(2,1)}, bf16[256,768]{1,0:T(8,128)(2,1)}, bf16[1024,768]{1,0:T(8,128)(2,1)}, f32[2,768]{1,0:T(2,128)}, f32[768]{0:T(...) custom-call(bf16[256,768]{1,0:T(8,128)(2,1)} %get-tuple-element.48.l, ...), custom_call_target="tpu_custom_call" | custom-call | tf_op jit(solution)/shard_map/pallas_call | solution.py:810

commit v3 on v1

v3 whole, which is shorter than its diff:
```python
import math
from types import SimpleNamespace

import jax
import jax.numpy as jnp
import numpy as np
from jax import lax
from jax.experimental import pallas as pl
from jax.experimental.pallas import tpu as pltpu
from jax.sharding import PartitionSpec as P

EPSILON = 1e-6
MASKED = -1e9
BUCKETS = 32
MAX_DISTANCE = 128
VMEM_LIMIT = 64 * 1024 * 1024 - 64 * 1024
F32 = jnp.float32
BF = jnp.bfloat16
NN = (((1,), (0,)), ((), ()))
NT = (((1,), (1,)), ((), ()))
MESH = pl.DeviceIdType.MESH

UNITS = ((0, 0, 384), (0, 384, 384), (1, 0, 384), (1, 384, 384), (2, 0, 512), (2, 512, 512), (2, 1024, 512))
CHUNKS = (
    (2, 0, 256, 'xyq'),
    (2, 256, 256, 'yqx'),
    (2, 512, 256, 'xyq'),
    (2, 768, 256, 'yzxw'),
    (2, 1024, 128, 'xyzw'),
    (2, 1152, 384, 'xyzw'),
    (1, 384, 384, 'xyzw'),
    (1, 0, 384, 'xyzw'),
    (0, 0, 256, 'xyq'),
    (0, 256, 256, 'xyzw'),
    (0, 512, 128, 'xyzw'),
    (0, 640, 128, 'xyzw'),
)
SCHEDULE = (
    (), (11, 2, 3, 21, 12, 13, 4, 31, 22, 23, 14), (), (), (1,), (32, 33, 41, 24), (), (34, 51), (), (), (42, 43), (52, 53, 61),
    (44, 54), (), (62, 63), (1000, 1010), (64, 1001), (1002, 1011, 1012, 1020, 1030), (), (1021, 1022, 1031, 1032, 1040, 1050),
    (), (), (1041, 1042, 1051, 1052, 1003, 1013), (1060, 1023), (1061, 1033, 1043), (1062, 1004), (1014, 1024, 1034), (), (),
    (1070, 1044), (), (), (1005, 1053, 1071), (1072, 1045), (1080, 1090, 1100, 1110, 1025), (1081,),
    (1082, 1091, 1092, 1101, 1102, 1111, 1006, 1046, 1112, 1054), (200, 1015, 1063),
    (1026, 1047, 201, 1035, 1055, 1007, 1048, 1016, 1064, 1036, 1056, 1027, 1073, 1065, 1049, 1037, 1017, 1057, 1083, 1038, 1066, 1074, 1058, 1084, 1093, 1067, 1075, 1039, 1103, 1085, 1068, 1113, 202, 1059, 1076, 1094, 1104, 1086, 1095, 1077, 1105, 1069, 1096, 1114, 1078, 203, 1106, 1115, 1097, 204, 1087, 1107, 1116, 1098, 1108, 1079, 205, 1117, 1099, 1118, 1109, 1119),
)


class Remote:
    def __init__(self, *args):
        self.args = args

    def made(self):
        src, dst, send, recv, to = self.args
        return pltpu.make_async_remote_copy(
            src_ref=src, dst_ref=dst, send_sem=send, recv_sem=recv, device_id=to, device_id_type=MESH)

    def start(self):
        self.made().start()

    def wait(self):
        self.made().wait()

    def wait_send(self):
        self.made().wait_send()

    def wait_recv(self):
        self.made().wait_recv()


def mm(a, b, d=NN):
    return lax.dot_general(a, b, d, preferred_element_type=F32)


def inverse_of(h):
    return lax.rsqrt(jnp.mean(h * h, axis=-1, keepdims=True) + EPSILON)


def norm_back(h, inv, g, r):
    s = r * g
    gain = jnp.sum(r * h * inv, axis=0, keepdims=True)
    return inv * s - h * (inv * inv * inv) * jnp.mean(s * h, axis=-1, keepdims=True), gain


def rows_of(start, size):
    return pl.ds(pl.multiple_of(start, 16), size)


def add_into(dst, parts, into=None):
    rows = dst.shape[0]
    into = dst if into is None else into
    step = next(n for n in (64, 48, 32, 16) if rows % n == 0)

    def block(i, _):
        at = rows_of(i * step, step)
        total = dst[at, :].astype(F32)
        for part in parts:
            total = total + part[at, :].astype(F32)
        into[at, :] = total.astype(BF)
        return 0

    lax.fori_loop(0, rows // step, block, 0)


def bucket_of(length=256):
    exact = BUCKETS // 2
    n = np.arange(length)
    far = exact + np.floor(np.log(np.maximum(n, 1) / exact) / math.log(MAX_DISTANCE / exact) * (BUCKETS - exact)).astype(np.int32)
    return np.where(n < exact, n, np.minimum(far, BUCKETS - 1)).astype(np.int32)


def bucket_onehot():
    bucket = bucket_of()
    n = lax.broadcasted_iota(jnp.int32, (BUCKETS, 256), 1)
    chosen = jnp.zeros((BUCKETS, 256), jnp.int32)
    for b in range(1, BUCKETS):
        chosen = chosen + jnp.where(n >= int(np.argmax(bucket >= b)), 1, 0)
    return (chosen == lax.broadcasted_iota(jnp.int32, (BUCKETS, 256), 0)).astype(BF)


def third(size, i):
    cut = {96: (32, 32, 32), 128: (32, 48, 48)}[size]
    return sum(cut[:i]), cut[i]


def layer_kernel(bits, r):
    dp = lax.axis_index("dp")
    t = lax.axis_index("tensor")
    c = lax.rem(t, 2)
    x = t // 2
    tc = t + 1 - 2 * c
    tx = t + 2 - 4 * x
    td = tc + 2 - 4 * x
    bit = [lax.rem(dp // (1 << b), 2) for b in range(bits)]
    pb = [dp + (1 << b) - (2 << b) * bit[b] for b in range(bits)]
    y, z1, z2 = bit[0], bit[1], bit[2]
    quad, quad_y, quad_z = y + 2 * z1, (1 - y) + 2 * z1, y + 2 * (1 - z1)
    quad_d = 3 - quad
    weights = (r.own, r.cross, r.feed)

    def fwd_shard(s):
        a, b = lax.rem(s, 2), s // 2
        return 2 * (x + b * (1 - 2 * x)) + c + a * (1 - 2 * c)

    def bwd_shard(s):
        a, b = 1 - s // 2, 1 - lax.rem(s, 2)
        return 2 * (x + b * (1 - 2 * x)) + c + a * (1 - 2 * c)

    loads = []

    def load(src, dst):
        loads.append(pltpu.make_async_copy(src, dst, r.lsem.at[len(loads)]))
        loads[-1].start()
        return loads[-1]

    slot = lambda v, i: v.at[t, pl.ds(192 * i, 192), :]
    token_load = load(r.tok_in, r.tok)
    self_loads = [load(src, slot(r.own, i)) for i, src in enumerate((r.sq, r.sk, r.sv, r.so))]
    cross_loads = [load(src, slot(r.cross, i)) for i, src in enumerate((r.ck, r.cv, r.cq, r.co))]
    hin_load = load(r.hin, r.raw)
    hout_loads = [load(r.hout.at[pl.ds(256 * i, 256), :], r.feed.at[t, pl.ds(512 * i + 256, 256), :]) for i in range(3)]
    memory_load = load(r.mem_in, r.mem)
    cotangent_load = load(r.cot_in, r.cot)

    barrier = pltpu.get_barrier_semaphore()
    partners = [(dp, tc), (dp, tx), (dp, td)] + [(p, t) for p in pb]
    for p in partners:
        pl.semaphore_signal(barrier, inc=1, device_id=p, device_id_type=MESH)

    g_self, g_cross, g_hid = (g[...].astype(F32).reshape(1, 768) for g in (r.gain1, r.gain2, r.gain3))
    ji = lax.broadcasted_iota(jnp.int32, (256, 256), 0)
    ii = lax.broadcasted_iota(jnp.int32, (256, 256), 1)
    length = r.lengths[t]
    allowed = lambda: (ji <= ii) & (ji < length)
    r.btab[t, 0:3, :] = mm(r.tab[...], bucket_onehot())
    r.tagv[...] = jnp.broadcast_to((r.tags[...] == 1).astype(F32), (128, 256)).T
    tagged = lambda: jnp.concatenate([r.tagv[...]] * 6, axis=1) > 0.5
    token_load.wait()
    x0 = r.tok[...].astype(F32) + jnp.where(tagged(), r.emb[1:2, :].astype(F32), r.emb[0:1, :].astype(F32))
    r.s0[...] = x0
    r.n1[...] = (x0 * inverse_of(x0) * g_self).astype(BF)
    for d in self_loads:
        d.wait()
    pl.semaphore_wait(barrier, len(partners))

    def gather_copy(u, j):
        a, row, size = UNITS[u]
        v, q = weights[a], size // 4
        sems = (r.gsend.at[u, j], r.grecv.at[u, j])
        at = lambda shard, quarter, first=0, n=q: v.at[shard, rows_of(row + quarter * q + first, n), :]
        core, over_x, over_y, over_z = (dp, tc), (dp, tx), (pb[0], t), (pb[1], t)
        if j == 0:
            ref, to = v.at[t, pl.ds(row, size), :], core
        elif j == 1:
            ref, to = at(t, quad), over_x
        elif j == 2:
            ref, to = at(t, quad_d, *third(q, 0)), over_x
        elif j == 3:
            ref, to = at(tx, quad), over_y
        elif j == 4:
            ref, to = at(tx, quad), over_z
        elif j == 5:
            ref, to = at(tx, quad), core
        elif j == 6:
            ref, to = at(tx, quad_y, *third(q, 2)), over_z
        elif j == 7:
            ref, to = at(tx, quad_y), core
        elif j == 8:
            ref, to = at(tx, quad_z, *third(q, 1)), over_y
        elif j == 9:
            ref, to = at(tx, quad_z), core
        else:
            ref, to = at(tx, quad_d), core
        return Remote(ref, ref, *sems, to)

    GATHER = {0: ((), (1, 2, 0)), 1: ((1,), (3, 4, 5)), 2: ((3,), (6, 7)), 3: ((4,), (8, 9)), 4: ((2, 8, 6), (10,)),
              5: ((0,), ()), 6: ((5, 7, 9, 10), ())}

    def gather_step(u, step):
        arrived, onward = GATHER[step]
        for j in arrived:
            gather_copy(u, j).wait_recv()
        for j in onward:
            gather_copy(u, j).start()

    def gather_sent(us, js):
        for u in us:
            for j in js:
                gather_copy(u, j).wait_send()

    last_of_feed = max(n for n, k in enumerate(CHUNKS) if k[0] == 2)

    def view(n, shard, first=0, size=None):
        a, row, rows, _ = CHUNKS[n]
        return weights[a].at[shard, rows_of(row + first, rows if size is None else size), :]

    def place(n, halves):
        first, size = 0, CHUNKS[n][2]
        for b in halves:
            size = size // 2
            first = first + b * size
        return first, size

    def result(n, halves):
        first, size = place(n, halves)
        return r.result[n].at[rows_of(first, size), :]

    flips = ((0, 1), (1, 0), (1, 1))
    turn = lambda b, f: b + f * (1 - 2 * b)
    along_z = [dp + f1 * (2 - 4 * z1) + f2 * (4 - 8 * z2) for f1, f2 in flips]

    def plan_of(n):
        order, buffers = CHUNKS[n][3], iter(r.parts[n])
        halves, shards, stages, gathers, count = [], [tx, t], [], [], iter(range(99))

        def copy(src, dst, to):
            j = next(count)
            return Remote(src, dst, r.rsend.at[n, j], r.rrecv.at[n, j], to)

        def piece(shard, at):
            return view(n, shard, *place(n, at))

        for d in order:
            buf = next(buffers)
            if d == "x":
                stages.append(([copy(piece(tx, halves), buf.at[0], (dp, tx))], [(piece(t, halves), [buf.at[0]])]))
                shards = [t]
                continue
            if d == "q":
                mine, others = [z1, z2], [([turn(z1, f1), turn(z2, f2)], p) for (f1, f2), p in zip(flips, along_z)]
            else:
                b = "yzw".index(d)
                mine, others = [bit[b]], [([1 - bit[b]], pb[b])]
            m = len(others)
            stages.append((
                [copy(piece(k, halves + o), buf.at[m * i + j], (p, t)) for i, k in enumerate(shards) for j, (o, p) in enumerate(others)],
                [(piece(k, halves + mine), [buf.at[m * i + j] for j in range(m)]) for i, k in enumerate(shards)]))
            halves = halves + mine
            gathers.append((list(halves), [p for _, p in others]))
        back = [[copy(result(n, at), result(n, at), (p, t)) for p in ps] for at, ps in reversed(gathers)]
        more = [(copy(piece(t, halves), r.more[n].at[b - 3], (pb[b], t)), r.more[n].at[b - 3]) for b in range(3, bits)]
        core = [copy(view(n, td), r.first[n].at[0], (dp, tc)), copy(view(n, tc), r.first[n].at[1], (dp, tc))]
        return SimpleNamespace(core=core, stages=stages, back=back, more=more, mine=piece(t, halves), result=result(n, halves))

    plans = [plan_of(n) for n in range(len(CHUNKS))]

    def out_copy(n):
        a, row, rows, _ = CHUNKS[n]
        return pltpu.make_async_copy(r.result[n], (r.own_out, r.cross_out, r.feed_out)[a].at[pl.ds(row, rows), :], r.osem.at[n])

    def start(copies):
        for d in copies:
            d.start()

    def reduce_step(n, j):
        p = plans[n]
        x_first = CHUNKS[n][3][0] == "x"
        if j == 0:
            if n == last_of_feed + 1:
                pl.semaphore_wait(r.credit, 1)
            start(p.core)
        elif j == 1:
            p.core[0].wait_recv()
            add_into(view(n, tx), [r.first[n].at[0]])
            if x_first:
                start(p.stages[0][0])
        elif j == 2:
            p.core[1].wait_recv()
            add_into(view(n, t), [r.first[n].at[1]])
            if n == last_of_feed:
                pl.semaphore_signal(r.credit, inc=1, device_id=(dp, tc), device_id_type=MESH)
            if not x_first:
                start(p.stages[0][0])
        elif j - 3 < len(p.stages):
            copies, sums = p.stages[j - 3]
            for d in copies:
                d.wait_recv()
            last = j - 2 == len(p.stages)
            for target, parts in sums:
                add_into(target, parts, p.result if last and not p.more else None)
            if not last:
                start(p.stages[j - 2][0])
                return
            for i, (copy, part) in enumerate(p.more):
                copy.start()
                copy.wait()
                add_into(p.mine, [part], p.result if i + 1 == len(p.more) else None)
            start(p.back[0])
        else:
            i = j - 3 - len(p.stages)
            for d in p.back[i]:
                d.wait_recv()
            if i + 1 < len(p.back):
                start(p.back[i + 1])
            else:
                out_copy(n).start()

    to = [(dp, tc), (dp, tx)] + [(p, t) for p in pb]

    def small_step(j):
        if j:
            Remote(r.sm, r.smb.at[j - 1], r.ssend.at[j - 1], r.srecv.at[j - 1], to[j - 1]).wait()
            r.sm[...] = r.sm[...] + r.smb[j - 1]
        if j < len(to):
            Remote(r.sm, r.smb.at[j], r.ssend.at[j], r.srecv.at[j], to[j]).start()

    places = iter(SCHEDULE)

    def run(todo):
        for e in todo:
            if e >= 1000:
                reduce_step((e - 1000) // 10, e % 10)
            elif e >= 200:
                small_step(e - 200)
            else:
                gather_step(e // 10, e % 10)

    def here():
        run(next(places))

    def take(count):
        return [next(places) for _ in range(count)]

    def hooks(s, todos, extra=None):
        for k, todo in enumerate(todos):
            more = (extra or {}).get(k)
            if todo or more:
                @pl.when(s == k)
                def _():
                    run(todo)
                    if more:
                        more()

    gather_step(0, 0)
    gather_step(1, 0)
    tables = [Remote(r.btab.at[t], r.btab.at[t], r.tsend.at[j], r.trecv.at[j], (dp, k)) for j, k in enumerate((tc, tx, td))]
    for d in tables:
        d.start()
    for d in cross_loads:
        d.wait()
    gather_step(2, 0)
    gather_step(3, 0)
    hin_load.wait()
    for d in hout_loads:
        d.wait()
    for i in range(3):
        r.feed[t, 512 * i:512 * i + 256, :] = r.raw[:, 256 * i:256 * i + 256].T
        gather_step(4 + i, 0)
    def bias_of(shard, i):
        return pltpu.roll(jnp.broadcast_to(r.btab[shard, i:i + 1, :], (256, 256)), 0, 1, stride=1, stride_axis=0)

    lane576 = lax.broadcasted_iota(jnp.int32, (1, 576), 1)

    def project_memory(shard):
        w = r.cross.at[shard, pl.ds(0, 384), :]

        def block(i, _):
            at = rows_of(i * 256, 256)
            r.kv[shard, at, :] = mm(r.mem[at, :], w[...], NT).astype(BF)
            return 0
        lax.fori_loop(0, 4, block, 0)
        for i in range(4):
            r.kvT[shard, :, 256 * i:256 * i + 256] = mm(w[...], r.mem[256 * i:256 * i + 256, :], NT).astype(BF)

    def near_memory():
        memory_load.wait()
        valid = r.mmask[pl.ds(t, 1), :]
        r.mask2[...] = jnp.broadcast_to(jnp.where(valid == 1, 0.0, MASKED).astype(F32), (128, 1024)).T
        project_memory(t)
        run(inside[0])
        gather_step(2, 5)
        project_memory(tc)
        run(inside[1])
        gather_step(0, 6)
        gather_step(1, 6)

    def self_near():
        gather_step(0, 5)
        gather_step(1, 5)
        for d in tables:
            d.wait_recv()

    def self_forward(s, _):
        hooks(s, turns, {1: self_near, 2: near_memory})
        k = fwd_shard(s)
        w = r.own.at[k, pl.ds(0, 576), :]
        a = mm(r.n1[...], w[...], NT)
        r.qkv[k] = jnp.where(lane576 < 192, a * 0.125, a).astype(BF)
        r.kvT1[k] = mm(r.own[k, 192:576, :], r.n1[...], NT).astype(BF)
        for i in range(3):
            q, kk = r.qkv[k, :, 64 * i:64 * i + 64], r.qkv[k, :, 192 + 64 * i:256 + 64 * i]
            scores = jnp.where(allowed(), mm(kk, q, NT) + bias_of(k, i), MASKED)
            most = jnp.max(scores, axis=0, keepdims=True)
            p = jnp.exp(scores - most)
            total = jnp.sum(p, axis=0, keepdims=True)
            o = mm(r.kvT1[k, 192 + 64 * i:256 + 64 * i, :], p.astype(BF))
            r.mix1[k, 64 * i:64 * i + 64, :] = (o / total).astype(BF)
            r.lse[k, i:i + 1, :] = most + jnp.log(total)
        return 0

    def project_out(target, mix, w):
        def block(k, _):
            target[...] += mm(mix[k].T, w[k, 576:768, :])
            return 0
        lax.fori_loop(0, 4, block, 0)

    inside, turns = take(2), take(4)
    lax.fori_loop(0, 4, self_forward, 0)
    here()
    r.s1[...] = r.s0[...]
    project_out(r.s1, r.mix1, r.own)
    x1 = r.s1[...]
    r.n2[...] = (x1 * inverse_of(x1) * g_cross).astype(BF)
    here()
    gather_step(3, 5)

    def cross_scores(shard, i, b, q):
        at = slice(256 * b, 256 * b + 256)
        return mm(r.kv[shard, at, 64 * i:64 * i + 64], q, NT) + jnp.concatenate([r.mask2[at, :]] * 2, axis=1)

    def far_memory_1():
        project_memory(tx)

    def far_memory_2():
        gather_step(2, 6)
        gather_step(3, 6)
        project_memory(td)

    def cross_forward(s, _):
        hooks(s, turns_1, {2: far_memory_1, 3: far_memory_2})
        k = fwd_shard(s)
        w = r.cross.at[k, pl.ds(384, 192), :]
        r.q2[k] = (mm(r.n2[...], w[...], NT) * 0.125).astype(BF)
        for i in range(3):
            q = r.q2[k, :, 64 * i:64 * i + 64]
            ss = [cross_scores(k, i, b, q) for b in range(4)]
            most = jnp.max(jnp.maximum(jnp.maximum(ss[0], ss[1]), jnp.maximum(ss[2], ss[3])), axis=0, keepdims=True)
            total, o = 0.0, 0.0
            for b in range(4):
                p = jnp.exp(ss[b] - most)
                total = total + jnp.sum(p, axis=0, keepdims=True)
                o = o + mm(r.kvT[k, 192 + 64 * i:256 + 64 * i, 256 * b:256 * b + 256], p.astype(BF))
            r.mix2[k, 64 * i:64 * i + 64, :] = (o / total).astype(BF)
            r.lse[4 + k, i:i + 1, :] = most + jnp.log(total)
        return 0

    turns_1 = take(4)
    lax.fori_loop(0, 4, cross_forward, 0)
    here()
    r.s2[...] = r.s1[...]
    project_out(r.s2, r.mix2, r.cross)
    x2 = r.s2[...]
    r.rows[...] = (x2 * inverse_of(x2) * g_hid).astype(BF)
    r.acc[...] = x2
    r.gst[...] = jnp.zeros_like(x2)
    cotangent_load.wait()
    for u in (4, 5, 6):
        gather_step(u, 5)

    def feed_waits(u):
        def far():
            gather_step(u, 6)
            gather_sent((u,), range(3, 11))
        return {0: lambda: gather_sent((u,), (0, 1, 2)), 1: far}

    def feed(j, _):
        hooks(j, turns_2, {2 * i + k: f for i in range(3) for k, f in feed_waits(4 + i).items()})
        pair = lax.rem(j, 2)
        first = (j // 2) * 512
        refs, acts, gbs = [], [], []
        for i in range(2):
            k = fwd_shard(2 * pair + i)
            w_in, w_out = (r.feed.at[k, rows_of(first + 256 * m, 256), :] for m in range(2))
            v = mm(r.rows[...], w_in[...], NT)
            ga = mm(r.cot[...], w_out[...], NT)
            phi = 0.5 * (1.0 + lax.erf(v * np.float32(1 / math.sqrt(2))))
            acts.append((v * phi).astype(BF))
            slope = phi + v * (jnp.exp(-0.5 * v * v) * np.float32(1 / math.sqrt(2 * math.pi)))
            gbs.append((slope * ga).astype(BF))
            refs.append((w_in, w_out))
        r.acc[...] += mm(acts[0], refs[0][1][...]) + mm(acts[1], refs[1][1][...])
        r.gst[...] += mm(gbs[0], refs[0][0][...]) + mm(gbs[1], refs[1][0][...])
        for (w_in, w_out), act, gb in zip(refs, acts, gbs):
            w_in[...] = mm(gb.T, r.rows[...]).astype(BF)
            w_out[...] = mm(act.T, r.cot[...]).astype(BF)
        return 0

    turns_2 = take(6)
    lax.fori_loop(0, 6, feed, 0)
    here()
    gather_sent(range(4), range(11))
    for d in tables:
        d.wait_send()
    r.lov[...] = r.acc[...].astype(BF)
    stores = [pltpu.make_async_copy(a, b, r.esem.at[i]) for i, (a, b) in enumerate(((r.lov, r.lo), (r.gmv, r.gmem), (r.gtv, r.gtok)))]
    stores[0].start()
    d, gain = norm_back(x2, inverse_of(x2), g_hid, r.gst[...])

    def put_small(row, value):
        for i in range(3):
            at = 3 * row + i
            r.sm[at // 8, at % 8:at % 8 + 1, :] = value[:, 256 * i:256 * i + 256]

    r.sm[...] = jnp.zeros_like(r.sm)
    put_small(4, gain)
    r.gst[...] = r.cot[...].astype(F32) + d
    here()
    r.rows[...] = r.gst[...].astype(BF)
    r.acc[...] = jnp.zeros_like(x2)

    def cross_backward(s, _):
        hooks(s, turns_3)
        k = bwd_shard(s)
        rw = r.rows[...]
        w = r.cross[k, 576:768, :]
        G = mm(rw, w, NT).astype(BF)
        GT = mm(w, rw, NT).astype(BF)
        r.cross[k, 576:768, :] = mm(r.mix2[k], rw).astype(BF)
        dqs, dks, dvs = [], [], []
        for i in range(3):
            q = r.q2[k, :, 64 * i:64 * i + 64]
            gi, gT = G[:, 64 * i:64 * i + 64], GT[64 * i:64 * i + 64, :]
            inner = jnp.sum(r.mix2[k, 64 * i:64 * i + 64, :].astype(F32) * gT.astype(F32), axis=0, keepdims=True)
            ls = r.lse[4 + k, i:i + 1, :]
            dq, dk, dv = 0.0, [], []
            for b in range(4):
                at = slice(256 * b, 256 * b + 256)
                p = jnp.exp(cross_scores(k, i, b, q) - ls)
                dp_ = mm(r.kv[k, at, 192 + 64 * i:256 + 64 * i], gi, NT)
                gs = (p * (dp_ - inner)).astype(BF)
                dq = dq + mm(r.kvT[k, 64 * i:64 * i + 64, at], gs)
                dk.append(mm(gs, q).astype(BF))
                dv.append(mm(p.astype(BF), gi).astype(BF))
            dqs.append((dq * 0.125).astype(BF))
            dks.append(dk)
            dvs.append(dv)
        for b in range(4):
            r.kv[k, 256 * b:256 * b + 256, :] = jnp.concatenate([v[b] for v in dks + dvs], axis=1)
        r.kvT[k] = r.kv[k].T
        dqT = jnp.concatenate(dqs, axis=0)
        r.acc[...] += mm(dqT.T, r.cross[k, 384:576, :])
        r.cross[k, 384:576, :] = mm(dqT, r.n2[...]).astype(BF)
        return 0

    turns_3 = take(4)
    lax.fori_loop(0, 4, cross_backward, 0)
    here()

    def memory_grad(i, _):
        at = rows_of(i * 256, 256)
        total = 0.0
        for k in range(4):
            total = total + mm(r.kv[k, at, :], r.cross[k, 0:384, :])
        r.gmv[at, :] = total.astype(BF)
        return 0

    lax.fori_loop(0, 4, memory_grad, 0)
    stores[1].start()
    here()

    def memory_weights(s, _):
        hooks(s, turns_4)
        k = bwd_shard(s)

        def block(i, _):
            at = rows_of(i * 192, 192)
            r.cross[k, at, :] = mm(r.kvT[k, at, :], r.mem[...]).astype(BF)
            return 0
        lax.fori_loop(0, 2, block, 0)
        return 0

    turns_4 = take(4)
    lax.fori_loop(0, 4, memory_weights, 0)
    here()
    d, gain = norm_back(r.s1[...], inverse_of(r.s1[...]), g_cross, r.acc[...])
    put_small(3, gain)
    r.gst[...] += d
    r.rows[...] = r.gst[...].astype(BF)
    r.acc[...] = jnp.zeros_like(x2)

    def self_backward(s, _):
        hooks(s, turns_5)
        k = bwd_shard(s)
        rw = r.rows[...]
        w = r.own[k, 576:768, :]
        G = mm(rw, w, NT).astype(BF)
        GT = mm(w, rw, NT).astype(BF)
        r.own[k, 576:768, :] = mm(r.mix1[k], rw).astype(BF)
        flip = (ji + ii == 255).astype(BF)
        dqs, dks, dvs = [], [], []
        for i in range(3):
            q, kk = r.qkv[k, :, 64 * i:64 * i + 64], r.qkv[k, :, 192 + 64 * i:256 + 64 * i]
            gi, gT = G[:, 64 * i:64 * i + 64], GT[64 * i:64 * i + 64, :]
            inner = jnp.sum(r.mix1[k, 64 * i:64 * i + 64, :].astype(F32) * gT.astype(F32), axis=0, keepdims=True)
            scores = jnp.where(allowed(), mm(kk, q, NT) + bias_of(k, i), MASKED)
            p = jnp.exp(scores - r.lse[k, i:i + 1, :])
            dp_ = mm(r.qkv[k, :, 384 + 64 * i:448 + 64 * i], gi, NT)
            gs = (p * (dp_ - inner)).astype(BF)
            dvs.append(mm(p.astype(BF), gi).astype(BF))
            dks.append(mm(gs, q).astype(BF))
            dqs.append((mm(r.kvT1[k, 64 * i:64 * i + 64, :], gs) * 0.125).astype(BF))
            shifted = pltpu.roll(mm(flip, gs), 1, 1, stride=1, stride_axis=0)
            r.sm[2 + k, i:i + 1, :] = jnp.sum(shifted, axis=0, keepdims=True)
        dqT = jnp.concatenate(dqs, axis=0)
        dkv = jnp.concatenate(dks + dvs, axis=1)
        r.acc[...] += mm(dqT.T, r.own[k, 0:192, :]) + mm(dkv, r.own[k, 192:576, :])
        r.own[k, 0:192, :] = mm(dqT, r.n1[...]).astype(BF)
        r.own[k, 192:576, :] = mm(dkv.T, r.n1[...]).astype(BF)
        return 0

    turns_5 = take(4)
    lax.fori_loop(0, 4, self_backward, 0)
    here()
    d, gain = norm_back(r.s0[...], inverse_of(r.s0[...]), g_self, r.acc[...])
    put_small(2, gain)
    g0 = r.gst[...] + d
    r.gtv[...] = g0.astype(BF)
    stores[2].start()
    put_small(0, jnp.sum(jnp.where(tagged(), 0.0, g0), axis=0, keepdims=True))
    put_small(1, jnp.sum(jnp.where(tagged(), g0, 0.0), axis=0, keepdims=True))
    here()
    here()
    for j in range(6, len(to) + 1):
        small_step(j)
    r.smo[...] = r.sm[0:2]
    r.dgo[...] = r.sm[2 + t]
    for n, p in enumerate(plans):
        for d in p.core + sum([copies for copies, _ in p.stages], []) + sum(p.back, []):
            d.wait_send()
        out_copy(n).wait()
    for d in stores:
        d.wait()


def layer(bits, ins):
    S = jax.ShapeDtypeStruct
    V, A, M = (pl.BlockSpec(memory_space=s) for s in (pltpu.VMEM, pl.ANY, pltpu.SMEM))
    vm = pltpu.VMEM
    inputs = dict(tok_in=A, mem_in=A, cot_in=A, lengths=M, mmask=V, tags=V, emb=V, gain1=V, gain2=V, gain3=V, tab=V,
                  sq=A, sk=A, sv=A, so=A, cq=A, ck=A, cv=A, co=A, hin=A, hout=A)
    wide, square = (256, 768), (768, 768)
    out = dict(lo=S(wide, BF), gtok=S(wide, BF), gmem=S((1024, 768), BF), smo=S((2, 8, 256), F32), dgo=S((8, 256), F32),
               own_out=S(square, BF), cross_out=S(square, BF), feed_out=S((1536, 768), BF))
    out_specs = [A, A, A, V, V, A, A, A]
    sizes = [n for _, _, n, _ in CHUNKS]

    def parts_of(n, order):
        shards, buffers = 2, []
        for d in order:
            if d == "x":
                shards = 1
                buffers.append(vm((1, n, 768), BF))
            else:
                n = n // 4 if d == "q" else n // 2
                buffers.append(vm((shards * (3 if d == "q" else 1), n, 768), BF))
        return buffers

    scratch = dict(
        own=vm((4, 768, 768), BF), cross=vm((4, 768, 768), BF), feed=vm((4, 1536, 768), BF), raw=vm(square, BF),
        tok=vm(wide, BF), cot=vm(wide, BF), mem=vm((1024, 768), BF),
        s0=vm(wide, F32), s1=vm(wide, F32), s2=vm(wide, F32), gst=vm(wide, F32), acc=vm(wide, F32),
        n1=vm(wide, BF), n2=vm(wide, BF), rows=vm(wide, BF),
        qkv=vm((4, 256, 576), BF), kvT1=vm((4, 384, 256), BF), q2=vm((4, 256, 192), BF),
        kv=vm((4, 1024, 384), BF), kvT=vm((4, 384, 1024), BF), mix1=vm((4, 192, 256), BF), mix2=vm((4, 192, 256), BF),
        lse=vm((8, 8, 256), F32), mask2=vm((1024, 128), F32), tagv=vm((256, 128), F32), btab=vm((4, 8, 256), F32),
        sm=vm((6, 8, 256), F32), smb=vm((2 + bits, 6, 8, 256), F32), gmv=vm((1024, 768), BF), lov=vm(wide, BF), gtv=vm(wide, BF),
        receive=vm((2, 1536, 768), BF),
    )
    parts = [parts_of(n, order) for _, _, n, order in CHUNKS]
    results = [vm((n, 768), BF) for n in sizes]
    more = [vm((bits - 3, n // 8, 768), BF) for n in sizes] if bits > 3 else []
    dma = pltpu.SemaphoreType.DMA
    sems = dict(gsend=dma((7, 11)), grecv=dma((7, 11)), rsend=dma((len(CHUNKS), 16 + bits)), rrecv=dma((len(CHUNKS), 16 + bits)), lsem=dma((15,)), osem=dma((len(CHUNKS),)),
                esem=dma((3,)), ssend=dma((2 + bits,)), srecv=dma((2 + bits,)), tsend=dma((3,)), trecv=dma((3,)),
                credit=pltpu.SemaphoreType.REGULAR)
    names = list(inputs) + list(out) + list(scratch) + list(sems)

    def kernel(*refs):
        r = SimpleNamespace(**dict(zip(names, refs)))
        rest = iter(refs[len(names):])
        r.parts = [[next(rest) for _ in p] for p in parts]
        r.result = [next(rest) for _ in results]
        r.more = [next(rest) for _ in more]
        r.first, at = [], [0, 0]
        for a, _, n, _ in CHUNKS:
            shared = int(a != 2)
            r.first.append(r.receive.at[:, pl.ds(at[shared], n), :])
            at[shared] += n
        layer_kernel(bits, r)

    return pl.pallas_call(
        kernel, out_shape=list(out.values()), in_specs=list(inputs.values()), out_specs=out_specs,
        scratch_shapes=list(scratch.values()) + list(sems.values()) + sum(parts, []) + results + more,
        compiler_params=pltpu.CompilerParams(collective_id=0, has_side_effects=True, vmem_limit_bytes=VMEM_LIMIT),
    )(*ins)


def finish_kernel(lo, gtok, gmem, smo, dgo, own, cross, feed,
                  o_lo, o_gtok, o_gmem, o_emb, o_g1, o_g2, o_g3, o_sq, o_sk, o_sv, o_so, o_pb, o_cq, o_ck, o_cv, o_co, o_hin, o_hout):
    o_lo[...] = lo[...]
    o_gtok[...] = gtok[...]
    o_gmem[...] = gmem[...]
    for i, o in enumerate((o_sq, o_sk, o_sv, o_so)):
        o[...] = own[192 * i:192 * i + 192, :].astype(F32)
    for i, o in enumerate((o_ck, o_cv, o_cq, o_co)):
        o[...] = cross[192 * i:192 * i + 192, :].astype(F32)
    for i in range(3):
        o_hin[:, 256 * i:256 * i + 256] = feed[512 * i:512 * i + 256, :].T.astype(F32)
        o_hout[256 * i:256 * i + 256, :] = feed[512 * i + 256:512 * i + 512, :].astype(F32)

    @pl.when(pl.program_id(0) == 0)
    def _():
        def small(row):
            return jnp.concatenate([smo[(3 * row + i) // 8, (3 * row + i) % 8:(3 * row + i) % 8 + 1, :] for i in range(3)], axis=1)
        o_emb[0:1, :] = small(0)
        o_emb[1:2, :] = small(1)
        o_g1[...] = small(2).reshape(768)
        o_g2[...] = small(3).reshape(768)
        o_g3[...] = small(4).reshape(768)
        total = lax.dot_general(dgo[...], bucket_onehot().astype(F32), NT, precision=lax.Precision.HIGHEST, preferred_element_type=F32)
        o_pb[...] = total[0:3, :]


def finish(args):
    S = jax.ShapeDtypeStruct
    n = 3
    cut = lambda rows: pl.BlockSpec((rows, 768 // n), lambda i: (0, i))
    full = lambda *s: pl.BlockSpec(s, lambda i: (0,) * len(s))
    flat, square = S((192, 768), F32), S((768, 768), F32)
    shapes = [S((256, 768), BF), S((256, 768), BF), S((1024, 768), BF), S((2, 768), F32)] + [S((768,), F32)] * 3
    shapes += [flat] * 4 + [S((3, 32), F32)] + [flat] * 4 + [square, square]
    ends = [cut(256), cut(256), cut(1024)]
    in_specs = ends + [full(2, 8, 256), full(8, 256), cut(768), cut(768), cut(1536)]
    out_specs = ends + [full(2, 768)] + [full(768)] * 3 + [cut(192)] * 4 + [full(3, 32)] + [cut(192)] * 4
    out_specs += [pl.BlockSpec((768 // n, 768), lambda i: (i, 0)), cut(768)]
    return pl.pallas_call(finish_kernel, grid=(n,), out_shape=shapes, in_specs=in_specs, out_specs=out_specs,
                          compiler_params=pltpu.CompilerParams(vmem_limit_bytes=VMEM_LIMIT))(*args)


def per_device(bits, tokens, memory, cotangent, lengths, memory_mask, token_tags, embedding, gain_self, gain_cross, gain_hidden,
               self_query, self_key, self_value, self_output, position_bias, cross_query, cross_key, cross_value,
               cross_output, hidden_in, hidden_out):
    parts = layer(bits, (
        tokens[0], memory[0], cotangent[0], lengths, memory_mask, token_tags, embedding, gain_self, gain_cross, gain_hidden, position_bias.T,
        self_query.T, self_key.T, self_value.T, self_output, cross_query.T, cross_key.T, cross_value.T, cross_output, hidden_in, hidden_out))
    lo, gtok, gmem, g_emb, g1, g2, g3, sq, sk, sv, so, pb, cq, ck, cv, co, hin, hout = finish(parts)
    return (lo[None], gtok[None], gmem[None], g_emb, g1, g2, g3, sq.T, sk.T, sv.T, so, pb.T, cq.T, ck.T, cv.T, co, hin, hout)


def solution(mesh):
    bits = int(math.log2(mesh.shape["dp"]))
    item = P(("dp", "tensor"), None, None)
    col, row, rep = P(None, "tensor"), P("tensor", None), P()
    in_specs = (item, item, item, P("dp"), P("dp", None), P(("dp", "tensor"), None), rep, rep, rep, rep,
                col, col, col, row, col, col, col, col, row, col, row)
    out_specs = (item, item, item, rep, rep, rep, rep, col, col, col, row, col, col, col, col, row, col, row)
    return jax.shard_map(lambda *a: per_device(bits, *a), mesh=mesh, in_specs=in_specs, out_specs=out_specs, check_vma=False)
```

time: 782 us -> 203 us (0.26)
  waiting for transfers between devices: 567 us -> 0 us
  Pallas kernels: 92.2 us -> 202 us
  blocking collectives: 69.2 us -> 0 us
  local copies, waits for them, and re-layouts: 24.6 us -> 0 us
  between operations: 14.2 us -> 0.83 us
  other arithmetic: 13.1 us -> 0 us
    reduce_scatter x8 -> x0, waiting for transfers between devices: 257 us -> none  [the longest x7 257 us: per_device(): lax.psum_scatter(g, 'tensor', scatter_dimension=0, tiled=False)]
    all_gather x7 -> x0, waiting for transfers between devices: 168 us -> none  [per_device(): gather = lambda w: lax.all_gather(w, 'tensor', axis=0)]
    psum x1 -> x0, waiting for transfers between devices: 134 us -> none  [per_device(): lax.psum(tuple((lax.psum_scatter(g, 'tensor', scatter_dimension=0, tiled=...]
    pallas_call x1 -> x2, Pallas kernels: 92.2 us -> 202 us  [the longest x1 194 us: layer(): pl.pallas_call(kernel, out_shape=list(out.values()), in_specs=list(inputs...]
    psum x2 -> x0, blocking collectives: 62.6 us -> none  [the longest x1 39.6 us: per_device(): small = lax.psum(small, ('dp', 'tensor'))]
    all_gather x3 -> x0, local copies, waits for them, and re-layouts: 12.8 us -> none  [per_device(): gather = lambda w: lax.all_gather(w, 'tensor', axis=0)]
    convert_element_type x7 -> x0, other arithmetic: 8.06 us -> none  [the longest x6 7.42 us: per_device(): f = lambda x: x.astype(F32)]
  transfers between devices with their start and end apart: 16 -> 0, of which waited for: 15 -> 0; matrix products, arithmetic and copies ran while one was open for 3% -> 0% of each run, Pallas kernels for 0% -> 0%
where the time goes in v3:
time: 203 us
  Pallas kernels  202 us (100%)
    pallas_call x1, Pallas kernels, layer(): pl.pallas_call(kernel, out_shape=list(out.values()), in_specs=list(inputs...  194 us
    pallas_call x1, Pallas kernels, finish(): pl.pallas_call(finish_kernel, grid=(n,), out_shape=shapes, in_specs=in_sp...  8.05 us

profile of v3, /device:TPU:0, one launch (start us, length us, event | category | flops | bytes accessed | tf_op | source)
XLA Modules:
  0.0 202.5 jit_solution(13766387750726671818)
XLA Ops:
  0.7 193.7 %shard_map.340 = (bf16[256,768]{1,0:T(8,128)(2,1)}, bf16[256,768]{1,0:T(8,128)(2,1)}, bf16[1024,768]{1,0:T(8,128)(2,1)}, f32[2,8,256]{2,1,0:T(8,128)}, f32[8,256...) custom-call(bf16[256,768]{1,0:T(8,128)(2,1)} %bitcast.21, ...), custom_call_target="tpu_custom_call" | custom-call | tf_op jit(solution)/shard_map/pallas_call | solution.py:730
  194.3 8.1 %shard_map.341 = (bf16[256,768]{1,0:T(8,128)(2,1)}, bf16[256,768]{1,0:T(8,128)(2,1)}, bf16[1024,768]{1,0:T(8,128)(2,1)}, f32[2,768]{1,0:T(2,128)}, f32[768]{0:T(...) custom-call(bf16[256,768]{1,0:T(8,128)(2,1)} %get-tuple-element.44.l, ...), custom_call_target="tpu_custom_call" | custom-call | tf_op jit(solution)/shard_map/pallas_call | solution.py:775

commit v4 on v3

--- a/solution.py
+++ b/solution.py
@@ -20,28 +20,27 @@
 NT = (((1,), (1,)), ((), ()))
 MESH = pl.DeviceIdType.MESH
 
-UNITS = ((0, 0, 384), (0, 384, 384), (1, 0, 384), (1, 384, 384), (2, 0, 512), (2, 512, 512), (2, 1024, 512))
+UNITS = ((0, 384), (384, 384))
 CHUNKS = (
-    (2, 0, 256, 'xyq'),
-    (2, 256, 256, 'yqx'),
-    (2, 512, 256, 'xyq'),
-    (2, 768, 256, 'yzxw'),
-    (2, 1024, 128, 'xyzw'),
-    (2, 1152, 384, 'xyzw'),
-    (1, 384, 384, 'xyzw'),
-    (1, 0, 384, 'xyzw'),
-    (0, 0, 256, 'xyq'),
-    (0, 256, 256, 'xyzw'),
-    (0, 512, 128, 'xyzw'),
-    (0, 640, 128, 'xyzw'),
+    (2, 0, 256, 'yq'),
+    (2, 256, 256, 'yq'),
+    (2, 512, 256, 'yzw'),
+    (2, 768, 256, 'yzw'),
+    (2, 1024, 512, 'yzw'),
+    (1, 384, 128, 'yxzw'),
+    (1, 512, 256, 'xyzw'),
+    (1, 0, 256, 'xyzw'),
+    (1, 256, 128, 'xzwy'),
+    (0, 0, 384, 'yq'),
+    (0, 384, 384, 'yzw'),
 )
 SCHEDULE = (
-    (), (11, 2, 3, 21, 12, 13, 4, 31, 22, 23, 14), (), (), (1,), (32, 33, 41, 24), (), (34, 51), (), (), (42, 43), (52, 53, 61),
-    (44, 54), (), (62, 63), (1000, 1010), (64, 1001), (1002, 1011, 1012, 1020, 1030), (), (1021, 1022, 1031, 1032, 1040, 1050),
-    (), (), (1041, 1042, 1051, 1052, 1003, 1013), (1060, 1023), (1061, 1033, 1043), (1062, 1004), (1014, 1024, 1034), (), (),
-    (1070, 1044), (), (), (1005, 1053, 1071), (1072, 1045), (1080, 1090, 1100, 1110, 1025), (1081,),
-    (1082, 1091, 1092, 1101, 1102, 1111, 1006, 1046, 1112, 1054), (200, 1015, 1063),
-    (1026, 1047, 201, 1035, 1055, 1007, 1048, 1016, 1064, 1036, 1056, 1027, 1073, 1065, 1049, 1037, 1017, 1057, 1083, 1038, 1066, 1074, 1058, 1084, 1093, 1067, 1075, 1039, 1103, 1085, 1068, 1113, 202, 1059, 1076, 1094, 1104, 1086, 1095, 1077, 1105, 1069, 1096, 1114, 1078, 203, 1106, 1115, 1097, 204, 1087, 1107, 1116, 1098, 1108, 1079, 205, 1117, 1099, 1118, 1109, 1119),
+    (), (), (), (), (), (), (1, 11, 2, 3, 12, 13, 4), (), (14,), (), (), (), (), (), (), (), (), (1000, 1010, 1020),
+    (1030, 1040, 1001, 1011, 1021, 1031, 1041), (1002,), (), (1012,), (1050, 1060, 1022, 1003), (1013, 1032, 1023), (),
+    (1051, 1052, 1061, 1062, 1004), (1042,), (), (), (1070, 1080, 1014), (), (1033,), (), (1024, 1053), (1043,), (1005, 1034),
+    (1071, 1072, 1081, 1082, 1015, 1025), (1090,), (1100, 1063, 1044, 1091, 1054, 1101, 1035, 1026, 1064, 1055, 1045, 1036),
+    (200, 1065),
+    (1092, 1056, 201, 1046, 1102, 1073, 1066, 1027, 1083, 202, 1093, 1037, 1057, 1103, 1067, 1084, 1047, 1058, 1074, 1094, 203, 1068, 1059, 1104, 1085, 1075, 204, 1095, 1105, 1069, 1076, 1086, 205, 1087, 1106, 1077, 1088, 1078, 1107, 1089, 1079),
 )
 
 
@@ -136,6 +135,8 @@
     quad, quad_y, quad_z = y + 2 * z1, (1 - y) + 2 * z1, y + 2 * (1 - z1)
     quad_d = 3 - quad
     weights = (r.own, r.cross, r.feed)
+    slot_of = lambda a, shard: shard if a == 1 else lax.rem(shard, 2)
+    mine, other = rows_of(256 * x, 256), rows_of(256 - 256 * x, 256)
 
     def fwd_shard(s):
         a, b = lax.rem(s, 2), s // 2
@@ -144,6 +145,10 @@
     def bwd_shard(s):
         a, b = 1 - s // 2, 1 - lax.rem(s, 2)
         return 2 * (x + b * (1 - 2 * x)) + c + a * (1 - 2 * c)
+
+    def item_shard(s):
+        a, b = lax.rem(s, 2), s // 2
+        return x + b * (1 - 2 * x), c + a * (1 - 2 * c)
 
     loads = []
 
@@ -152,39 +157,34 @@
         loads[-1].start()
         return loads[-1]
 
-    slot = lambda v, i: v.at[t, pl.ds(192 * i, 192), :]
+    slot = lambda v, k, i: v.at[k, pl.ds(192 * i, 192), :]
     token_load = load(r.tok_in, r.tok)
-    self_loads = [load(src, slot(r.own, i)) for i, src in enumerate((r.sq, r.sk, r.sv, r.so))]
-    cross_loads = [load(src, slot(r.cross, i)) for i, src in enumerate((r.ck, r.cv, r.cq, r.co))]
-    hin_load = load(r.hin, r.raw)
-    hout_loads = [load(r.hout.at[pl.ds(256 * i, 256), :], r.feed.at[t, pl.ds(512 * i + 256, 256), :]) for i in range(3)]
+    self_loads = [load(src, slot(r.own, c, i)) for i, src in enumerate((r.sq, r.sk, r.sv, r.so))]
+    cross_loads = [load(src, slot(r.cross, t, i)) for i, src in enumerate((r.ck, r.cv, r.cq, r.co))]
     memory_load = load(r.mem_in, r.mem)
-    cotangent_load = load(r.cot_in, r.cot)
+    feed_loads = [load(src, r.feed.at[c, pl.ds(768 * i, 768), :]) for i, src in enumerate((r.hin, r.hout))]
+    cotangent_load = load(r.cot_in, r.cot.at[mine, :])
 
     barrier = pltpu.get_barrier_semaphore()
-    partners = [(dp, tc), (dp, tx), (dp, td)] + [(p, t) for p in pb]
+    partners = [(dp, tc), (dp, tx)] + [(p, t) for p in pb]
     for p in partners:
         pl.semaphore_signal(barrier, inc=1, device_id=p, device_id_type=MESH)
 
     g_self, g_cross, g_hid = (g[...].astype(F32).reshape(1, 768) for g in (r.gain1, r.gain2, r.gain3))
     ji = lax.broadcasted_iota(jnp.int32, (256, 256), 0)
     ii = lax.broadcasted_iota(jnp.int32, (256, 256), 1)
-    length = r.lengths[t]
-    allowed = lambda: (ji <= ii) & (ji < length)
-    r.btab[t, 0:3, :] = mm(r.tab[...], bucket_onehot())
+    r.btab[c, 0:3, :] = mm(r.tab[...], bucket_onehot())
     r.tagv[...] = jnp.broadcast_to((r.tags[...] == 1).astype(F32), (128, 256)).T
     tagged = lambda: jnp.concatenate([r.tagv[...]] * 6, axis=1) > 0.5
     token_load.wait()
     x0 = r.tok[...].astype(F32) + jnp.where(tagged(), r.emb[1:2, :].astype(F32), r.emb[0:1, :].astype(F32))
     r.s0[...] = x0
-    r.n1[...] = (x0 * inverse_of(x0) * g_self).astype(BF)
-    for d in self_loads:
-        d.wait()
+    r.n1[mine, :] = (x0 * inverse_of(x0) * g_self).astype(BF)
     pl.semaphore_wait(barrier, len(partners))
 
     def gather_copy(u, j):
-        a, row, size = UNITS[u]
-        v, q = weights[a], size // 4
+        row, size = UNITS[u]
+        v, q = r.cross, size // 4
         sems = (r.gsend.at[u, j], r.grecv.at[u, j])
         at = lambda shard, quarter, first=0, n=q: v.at[shard, rows_of(row + quarter * q + first, n), :]
         core, over_x, over_y, over_z = (dp, tc), (dp, tx), (pb[0], t), (pb[1], t)
@@ -227,11 +227,9 @@
             for j in js:
                 gather_copy(u, j).wait_send()
 
-    last_of_feed = max(n for n, k in enumerate(CHUNKS) if k[0] == 2)
-
     def view(n, shard, first=0, size=None):
         a, row, rows, _ = CHUNKS[n]
-        return weights[a].at[shard, rows_of(row + first, rows if size is None else size), :]
+        return weights[a].at[slot_of(a, shard), rows_of(row + first, rows if size is None else size), :]
 
     def place(n, halves):
         first, size = 0, CHUNKS[n][2]
@@ -250,7 +248,7 @@
 
     def plan_of(n):
         order, buffers = CHUNKS[n][3], iter(r.parts[n])
-        halves, shards, stages, gathers, count = [], [tx, t], [], [], iter(range(99))
+        halves, shards, stages, gathers, count = [], [tx, t] if "x" in order else [t], [], [], iter(range(99))
 
         def copy(src, dst, to):
             j = next(count)
@@ -278,7 +276,8 @@
             gathers.append((list(halves), [p for _, p in others]))
         back = [[copy(result(n, at), result(n, at), (p, t)) for p in ps] for at, ps in reversed(gathers)]
         more = [(copy(piece(t, halves), r.more[n].at[b - 3], (pb[b], t)), r.more[n].at[b - 3]) for b in range(3, bits)]
-        core = [copy(view(n, td), r.first[n].at[0], (dp, tc)), copy(view(n, tc), r.first[n].at[1], (dp, tc))]
+        far = [(td, tx)] if "x" in order else []
+        core = [(copy(view(n, a), r.first[n].at[i], (dp, tc)), view(n, b), r.first[n].at[i]) for i, (a, b) in enumerate(far + [(tc, t)])]
         return SimpleNamespace(core=core, stages=stages, back=back, more=more, mine=piece(t, halves), result=result(n, halves))
 
     plans = [plan_of(n) for n in range(len(CHUNKS))]
@@ -293,32 +292,24 @@
 
     def reduce_step(n, j):
         p = plans[n]
-        x_first = CHUNKS[n][3][0] == "x"
+        m = len(p.core)
         if j == 0:
-            if n == last_of_feed + 1:
-                pl.semaphore_wait(r.credit, 1)
-            start(p.core)
-        elif j == 1:
-            p.core[0].wait_recv()
-            add_into(view(n, tx), [r.first[n].at[0]])
-            if x_first:
+            start([d for d, _, _ in p.core])
+        elif j <= m:
+            copy, target, part = p.core[j - 1]
+            copy.wait_recv()
+            add_into(target, [part])
+            if j == (1 if CHUNKS[n][3][0] == "x" else m):
                 start(p.stages[0][0])
-        elif j == 2:
-            p.core[1].wait_recv()
-            add_into(view(n, t), [r.first[n].at[1]])
-            if n == last_of_feed:
-                pl.semaphore_signal(r.credit, inc=1, device_id=(dp, tc), device_id_type=MESH)
-            if not x_first:
-                start(p.stages[0][0])
-        elif j - 3 < len(p.stages):
-            copies, sums = p.stages[j - 3]
+        elif j - m <= len(p.stages):
+            copies, sums = p.stages[j - m - 1]
             for d in copies:
                 d.wait_recv()
-            last = j - 2 == len(p.stages)
+            last = j - m == len(p.stages)
             for target, parts in sums:
                 add_into(target, parts, p.result if last and not p.more else None)
             if not last:
-                start(p.stages[j - 2][0])
+                start(p.stages[j - m][0])
                 return
             for i, (copy, part) in enumerate(p.more):
                 copy.start()
@@ -326,7 +317,7 @@
                 add_into(p.mine, [part], p.result if i + 1 == len(p.more) else None)
             start(p.back[0])
         else:
-            i = j - 3 - len(p.stages)
+            i = j - m - 1 - len(p.stages)
             for d in p.back[i]:
                 d.wait_recv()
             if i + 1 < len(p.back):
@@ -370,25 +361,40 @@
                     if more:
                         more()
 
+    def over_x(j, src, dst):
+        return Remote(src, dst, r.xsend.at[j], r.xrecv.at[j], (dp, tx))
+
+    def to_core(j, src, dst):
+        return Remote(src, dst, r.csend.at[j], r.crecv.at[j], (dp, tc))
+
+    trade = [over_x(j, v.at[mine, :], v.at[mine, :]) for j, v in enumerate((r.n1, r.cot, r.n3, r.rows1))]
+    trade_n1, trade_cot, trade_n3, trade_rows = trade
+    give = [over_x(4 + j, r.out.at[j], r.arrived.at[j]) for j in range(4)]
+    give_s1, give_lo, give_gn, give_gn1 = give
+    core_own, core_feed, core_tab = (to_core(j, v.at[c], v.at[c]) for j, v in enumerate((r.own, r.feed, r.btab)))
+    trade_n1.start()
+    for d in self_loads:
+        d.wait()
+    core_own.start()
+    core_tab.start()
+    for d in cross_loads:
+        d.wait()
     gather_step(0, 0)
     gather_step(1, 0)
-    tables = [Remote(r.btab.at[t], r.btab.at[t], r.tsend.at[j], r.trecv.at[j], (dp, k)) for j, k in enumerate((tc, tx, td))]
-    for d in tables:
-        d.start()
-    for d in cross_loads:
+    for d in feed_loads:
         d.wait()
-    gather_step(2, 0)
-    gather_step(3, 0)
-    hin_load.wait()
-    for d in hout_loads:
-        d.wait()
-    for i in range(3):
-        r.feed[t, 512 * i:512 * i + 256, :] = r.raw[:, 256 * i:256 * i + 256].T
-        gather_step(4 + i, 0)
-    def bias_of(shard, i):
-        return pltpu.roll(jnp.broadcast_to(r.btab[shard, i:i + 1, :], (256, 256)), 0, 1, stride=1, stride_axis=0)
+    core_feed.start()
 
     lane576 = lax.broadcasted_iota(jnp.int32, (1, 576), 1)
+
+    def bias_of(f, i):
+        return pltpu.roll(jnp.broadcast_to(r.btab[f, i:i + 1, :], (256, 256)), 0, 1, stride=1, stride_axis=0)
+
+    def allowed(e):
+        return (ji <= ii) & (ji < r.lengths[2 * e + c])
+
+    def columns(e):
+        return pl.ds(pl.multiple_of(256 * e, 256), 256)
 
     def project_memory(shard):
         w = r.cross.at[shard, pl.ds(0, 384), :]
@@ -401,75 +407,70 @@
         for i in range(4):
             r.kvT[shard, :, 256 * i:256 * i + 256] = mm(w[...], r.mem[256 * i:256 * i + 256, :], NT).astype(BF)
 
+    def near_self():
+        core_own.wait_recv()
+        core_tab.wait_recv()
+
     def near_memory():
         memory_load.wait()
         valid = r.mmask[pl.ds(t, 1), :]
         r.mask2[...] = jnp.broadcast_to(jnp.where(valid == 1, 0.0, MASKED).astype(F32), (128, 1024)).T
         project_memory(t)
-        run(inside[0])
-        gather_step(2, 5)
+        run(turns[3])
+        gather_step(0, 5)
         project_memory(tc)
-        run(inside[1])
-        gather_step(0, 6)
-        gather_step(1, 6)
-
-    def self_near():
-        gather_step(0, 5)
-        gather_step(1, 5)
-        for d in tables:
-            d.wait_recv()
+        run(turns[4])
+        trade_n1.wait_recv()
 
     def self_forward(s, _):
-        hooks(s, turns, {1: self_near, 2: near_memory})
-        k = fwd_shard(s)
-        w = r.own.at[k, pl.ds(0, 576), :]
-        a = mm(r.n1[...], w[...], NT)
+        hooks(s, [turns[0], turns[1], turns[2], turns[5]], {1: near_self, 2: near_memory})
+        e, f = item_shard(s)
+        k = 2 * e + f
+        rows = r.n1.at[rows_of(256 * e, 256), :]
+        a = mm(rows[...], r.own[f, 0:576, :], NT)
         r.qkv[k] = jnp.where(lane576 < 192, a * 0.125, a).astype(BF)
-        r.kvT1[k] = mm(r.own[k, 192:576, :], r.n1[...], NT).astype(BF)
+        r.kvT1[k] = mm(r.own[f, 192:576, :], rows[...], NT).astype(BF)
         for i in range(3):
             q, kk = r.qkv[k, :, 64 * i:64 * i + 64], r.qkv[k, :, 192 + 64 * i:256 + 64 * i]
-            scores = jnp.where(allowed(), mm(kk, q, NT) + bias_of(k, i), MASKED)
+            scores = jnp.where(allowed(e), mm(kk, q, NT) + bias_of(f, i), MASKED)
             most = jnp.max(scores, axis=0, keepdims=True)
             p = jnp.exp(scores - most)
             total = jnp.sum(p, axis=0, keepdims=True)
             o = mm(r.kvT1[k, 192 + 64 * i:256 + 64 * i, :], p.astype(BF))
-            r.mix1[k, 64 * i:64 * i + 64, :] = (o / total).astype(BF)
+            r.mix1[f, 64 * i:64 * i + 64, columns(e)] = (o / total).astype(BF)
             r.lse[k, i:i + 1, :] = most + jnp.log(total)
         return 0
 
-    def project_out(target, mix, w):
-        def block(k, _):
-            target[...] += mm(mix[k].T, w[k, 576:768, :])
-            return 0
-        lax.fori_loop(0, 4, block, 0)
-
-    inside, turns = take(2), take(4)
+    def self_out(e):
+        return mm(r.mix1[0, :, columns(e)].T, r.own[0, 576:768, :]) + mm(r.mix1[1, :, columns(e)].T, r.own[1, 576:768, :])
+
+    turns = take(6)
     lax.fori_loop(0, 4, self_forward, 0)
-    here()
-    r.s1[...] = r.s0[...]
-    project_out(r.s1, r.mix1, r.own)
-    x1 = r.s1[...]
+    r.out[0] = self_out(1 - x).astype(BF)
+    give_s1.start()
+    cotangent_load.wait()
+    trade_cot.start()
+    r.s1[...] = r.s0[...] + self_out(x)
+    here()
+    project_memory(tx)
+    here()
+    gather_step(0, 6)
+    project_memory(td)
+    here()
+    give_s1.wait_recv()
+    x1 = r.s1[...] + r.arrived[0].astype(F32)
+    r.s1[...] = x1
     r.n2[...] = (x1 * inverse_of(x1) * g_cross).astype(BF)
-    here()
-    gather_step(3, 5)
+    gather_step(1, 5)
 
     def cross_scores(shard, i, b, q):
         at = slice(256 * b, 256 * b + 256)
         return mm(r.kv[shard, at, 64 * i:64 * i + 64], q, NT) + jnp.concatenate([r.mask2[at, :]] * 2, axis=1)
 
-    def far_memory_1():
-        project_memory(tx)
-
-    def far_memory_2():
-        gather_step(2, 6)
-        gather_step(3, 6)
-        project_memory(td)
-
     def cross_forward(s, _):
-        hooks(s, turns_1, {2: far_memory_1, 3: far_memory_2})
+        hooks(s, turns_1, {3: lambda: gather_step(1, 6)})
         k = fwd_shard(s)
-        w = r.cross.at[k, pl.ds(384, 192), :]
-        r.q2[k] = (mm(r.n2[...], w[...], NT) * 0.125).astype(BF)
+        r.q2[k] = (mm(r.n2[...], r.cross[k, 384:576, :], NT) * 0.125).astype(BF)
         for i in range(3):
             q = r.q2[k, :, 64 * i:64 * i + 64]
             ss = [cross_scores(k, i, b, q) for b in range(4)]
@@ -486,54 +487,72 @@
     turns_1 = take(4)
     lax.fori_loop(0, 4, cross_forward, 0)
     here()
-    r.s2[...] = r.s1[...]
-    project_out(r.s2, r.mix2, r.cross)
-    x2 = r.s2[...]
-    r.rows[...] = (x2 * inverse_of(x2) * g_hid).astype(BF)
-    r.acc[...] = x2
-    r.gst[...] = jnp.zeros_like(x2)
-    cotangent_load.wait()
-    for u in (4, 5, 6):
-        gather_step(u, 5)
-
-    def feed_waits(u):
-        def far():
-            gather_step(u, 6)
-            gather_sent((u,), range(3, 11))
-        return {0: lambda: gather_sent((u,), (0, 1, 2)), 1: far}
-
-    def feed(j, _):
-        hooks(j, turns_2, {2 * i + k: f for i in range(3) for k, f in feed_waits(4 + i).items()})
-        pair = lax.rem(j, 2)
-        first = (j // 2) * 512
-        refs, acts, gbs = [], [], []
-        for i in range(2):
-            k = fwd_shard(2 * pair + i)
-            w_in, w_out = (r.feed.at[k, rows_of(first + 256 * m, 256), :] for m in range(2))
-            v = mm(r.rows[...], w_in[...], NT)
-            ga = mm(r.cot[...], w_out[...], NT)
+    x2 = r.s1[...]
+    for k in range(4):
+        x2 = x2 + mm(r.mix2[k].T, r.cross[k, 576:768, :])
+    r.s2[...] = x2
+    r.n3[mine, :] = (x2 * inverse_of(x2) * g_hid).astype(BF)
+    trade_n3.start()
+    r.sums[mine, :] = x2
+    r.sums[other, :] = jnp.zeros_like(x2)
+    r.grads[...] = jnp.zeros_like(r.grads)
+    core_feed.wait_recv()
+
+    def far_rows():
+        trade_cot.wait_recv()
+        trade_n3.wait_recv()
+
+    def feed(s, _):
+        hooks(s, [turns_2[0], (), turns_2[1]], {2: far_rows})
+        e, f = item_shard(s)
+        at = rows_of(256 * e, 256)
+        rows, cot = r.n3.at[at, :], r.cot.at[at, :]
+        for i in range(3):
+            cs = slice(256 * i, 256 * i + 256)
+            v = mm(rows[...], r.feed[f, 0:768, cs])
+            ga = mm(cot[...], r.feed[f, 768 + 256 * i:1024 + 256 * i, :], NT)
             phi = 0.5 * (1.0 + lax.erf(v * np.float32(1 / math.sqrt(2))))
-            acts.append((v * phi).astype(BF))
+            act = (v * phi).astype(BF)
             slope = phi + v * (jnp.exp(-0.5 * v * v) * np.float32(1 / math.sqrt(2 * math.pi)))
-            gbs.append((slope * ga).astype(BF))
-            refs.append((w_in, w_out))
-        r.acc[...] += mm(acts[0], refs[0][1][...]) + mm(acts[1], refs[1][1][...])
-        r.gst[...] += mm(gbs[0], refs[0][0][...]) + mm(gbs[1], refs[1][0][...])
-        for (w_in, w_out), act, gb in zip(refs, acts, gbs):
-            w_in[...] = mm(gb.T, r.rows[...]).astype(BF)
-            w_out[...] = mm(act.T, r.cot[...]).astype(BF)
-        return 0
-
-    turns_2 = take(6)
-    lax.fori_loop(0, 6, feed, 0)
-    here()
-    gather_sent(range(4), range(11))
-    for d in tables:
-        d.wait_send()
-    r.lov[...] = r.acc[...].astype(BF)
-    stores = [pltpu.make_async_copy(a, b, r.esem.at[i]) for i, (a, b) in enumerate(((r.lov, r.lo), (r.gmv, r.gmem), (r.gtv, r.gtok)))]
-    stores[0].start()
-    d, gain = norm_back(x2, inverse_of(x2), g_hid, r.gst[...])
+            r.act[:, cs] = act
+            r.actT[f, cs, columns(e)] = act.T
+            r.gb[f, at, cs] = (slope * ga).astype(BF)
+        r.sums[at, :] += mm(r.act[...], r.feed[f, 768:1536, :])
+        r.grads[at, :] += mm(r.gb[f, at, :], r.feed[f, 0:768, :], NT)
+        return 0
+
+    turns_2 = take(2)
+    lax.fori_loop(0, 4, feed, 0)
+    r.out[2] = r.grads[other, :].astype(BF)
+    give_gn.start()
+    r.out[1] = r.sums[other, :].astype(BF)
+    give_lo.start()
+    here()
+    core_feed.wait_send()
+
+    def feed_weights(f, _):
+        def block(i, _):
+            at = rows_of(256 * i, 256)
+            r.feed[f, at, :] = mm(r.n3[:, pl.ds(pl.multiple_of(256 * i, 256), 256)].T, r.gb[f]).astype(BF)
+            return 0
+        lax.fori_loop(0, 3, block, 0)
+        return 0
+
+    lax.fori_loop(0, 2, feed_weights, 0)
+    here()
+
+    def feed_out_weights(f, _):
+        def block(i, _):
+            at = rows_of(256 * i, 256)
+            r.feed[f, rows_of(768 + 256 * i, 256), :] = mm(r.actT[f, at, :], r.cot[...]).astype(BF)
+            return 0
+        lax.fori_loop(0, 3, block, 0)
+        return 0
+
+    lax.fori_loop(0, 2, feed_out_weights, 0)
+    here()
+    give_gn.wait_recv()
+    d, gain = norm_back(x2, inverse_of(x2), g_hid, r.grads[mine, :] + r.arrived[2].astype(F32))
 
     def put_small(row, value):
         for i in range(3):
@@ -542,15 +561,16 @@
 
     r.sm[...] = jnp.zeros_like(r.sm)
     put_small(4, gain)
-    r.gst[...] = r.cot[...].astype(F32) + d
-    here()
-    r.rows[...] = r.gst[...].astype(BF)
+    r.gst[...] = r.cot[mine, :].astype(F32) + d
+    gather_sent(range(2), range(11))
+    here()
+    r.rows2[...] = r.gst[...].astype(BF)
     r.acc[...] = jnp.zeros_like(x2)
 
     def cross_backward(s, _):
         hooks(s, turns_3)
         k = bwd_shard(s)
-        rw = r.rows[...]
+        rw = r.rows2[...]
         w = r.cross[k, 576:768, :]
         G = mm(rw, w, NT).astype(BF)
         GT = mm(w, rw, NT).astype(BF)
@@ -584,6 +604,18 @@
     turns_3 = take(4)
     lax.fori_loop(0, 4, cross_backward, 0)
     here()
+    x1 = r.s1[...]
+    d, gain = norm_back(x1, inverse_of(x1), g_cross, r.acc[...])
+    put_small(3, gain)
+    x1 = r.gst[...] + d
+    r.gst[...] = x1
+    r.rows1[mine, :] = x1.astype(BF)
+    trade_rows.start()
+    here()
+    give_lo.wait_recv()
+    r.lov[...] = (r.sums[mine, :] + r.arrived[1].astype(F32)).astype(BF)
+    stores = [pltpu.make_async_copy(a, b, r.esem.at[i]) for i, (a, b) in enumerate(((r.lov, r.lo), (r.gmv, r.gmem), (r.gtv, r.gtok)))]
+    stores[0].start()
 
     def memory_grad(i, _):
         at = rows_of(i * 256, 256)
@@ -611,27 +643,24 @@
     turns_4 = take(4)
     lax.fori_loop(0, 4, memory_weights, 0)
     here()
-    d, gain = norm_back(r.s1[...], inverse_of(r.s1[...]), g_cross, r.acc[...])
-    put_small(3, gain)
-    r.gst[...] += d
-    r.rows[...] = r.gst[...].astype(BF)
-    r.acc[...] = jnp.zeros_like(x2)
+    r.grads[...] = jnp.zeros_like(r.grads)
 
     def self_backward(s, _):
-        hooks(s, turns_5)
-        k = bwd_shard(s)
-        rw = r.rows[...]
-        w = r.own[k, 576:768, :]
+        hooks(s, turns_5, {2: trade_rows.wait_recv})
+        e, f = item_shard(s)
+        k = 2 * e + f
+        here_rows = rows_of(256 * e, 256)
+        rw = r.rows1[here_rows, :]
+        w = r.own[f, 576:768, :]
         G = mm(rw, w, NT).astype(BF)
         GT = mm(w, rw, NT).astype(BF)
-        r.own[k, 576:768, :] = mm(r.mix1[k], rw).astype(BF)
         flip = (ji + ii == 255).astype(BF)
         dqs, dks, dvs = [], [], []
         for i in range(3):
             q, kk = r.qkv[k, :, 64 * i:64 * i + 64], r.qkv[k, :, 192 + 64 * i:256 + 64 * i]
             gi, gT = G[:, 64 * i:64 * i + 64], GT[64 * i:64 * i + 64, :]
-            inner = jnp.sum(r.mix1[k, 64 * i:64 * i + 64, :].astype(F32) * gT.astype(F32), axis=0, keepdims=True)
-            scores = jnp.where(allowed(), mm(kk, q, NT) + bias_of(k, i), MASKED)
+            inner = jnp.sum(r.mix1[f, 64 * i:64 * i + 64, columns(e)].astype(F32) * gT.astype(F32), axis=0, keepdims=True)
+            scores = jnp.where(allowed(e), mm(kk, q, NT) + bias_of(f, i), MASKED)
             p = jnp.exp(scores - r.lse[k, i:i + 1, :])
             dp_ = mm(r.qkv[k, :, 384 + 64 * i:448 + 64 * i], gi, NT)
             gs = (p * (dp_ - inner)).astype(BF)
@@ -639,18 +668,30 @@
             dks.append(mm(gs, q).astype(BF))
             dqs.append((mm(r.kvT1[k, 64 * i:64 * i + 64, :], gs) * 0.125).astype(BF))
             shifted = pltpu.roll(mm(flip, gs), 1, 1, stride=1, stride_axis=0)
-            r.sm[2 + k, i:i + 1, :] = jnp.sum(shifted, axis=0, keepdims=True)
+            r.sm[2 + 2 * x + f, i:i + 1, :] += jnp.sum(shifted, axis=0, keepdims=True)
         dqT = jnp.concatenate(dqs, axis=0)
         dkv = jnp.concatenate(dks + dvs, axis=1)
-        r.acc[...] += mm(dqT.T, r.own[k, 0:192, :]) + mm(dkv, r.own[k, 192:576, :])
-        r.own[k, 0:192, :] = mm(dqT, r.n1[...]).astype(BF)
-        r.own[k, 192:576, :] = mm(dkv.T, r.n1[...]).astype(BF)
+        r.gT[f, 0:192, columns(e)] = dqT
+        r.gT[f, 192:576, columns(e)] = dkv.T
+        r.grads[here_rows, :] += mm(dqT.T, r.own[f, 0:192, :]) + mm(dkv, r.own[f, 192:576, :])
         return 0
 
     turns_5 = take(4)
     lax.fori_loop(0, 4, self_backward, 0)
-    here()
-    d, gain = norm_back(r.s0[...], inverse_of(r.s0[...]), g_self, r.acc[...])
+    r.out[3] = r.grads[other, :].astype(BF)
+    give_gn1.start()
+    core_own.wait_send()
+    here()
+    for f in range(2):
+        r.own[f, 0:384, :] = mm(r.gT[f, 0:384, :], r.n1[...]).astype(BF)
+    here()
+    for f in range(2):
+        r.own[f, 384:576, :] = mm(r.gT[f, 384:576, :], r.n1[...]).astype(BF)
+        r.own[f, 576:768, :] = mm(r.mix1[f], r.rows1[...]).astype(BF)
+    here()
+    give_gn1.wait_recv()
+    x0 = r.s0[...]
+    d, gain = norm_back(x0, inverse_of(x0), g_self, r.grads[mine, :] + r.arrived[3].astype(F32))
     put_small(2, gain)
     g0 = r.gst[...] + d
     r.gtv[...] = g0.astype(BF)
@@ -664,11 +705,13 @@
     r.smo[...] = r.sm[0:2]
     r.dgo[...] = r.sm[2 + t]
     for n, p in enumerate(plans):
-        for d in p.core + sum([copies for copies, _ in p.stages], []) + sum(p.back, []):
+        for d in [d for d, _, _ in p.core] + sum([copies for copies, _ in p.stages], []) + sum(p.back, []):
             d.wait_send()
         out_copy(n).wait()
     for d in stores:
         d.wait()
+    for d in trade + give + [core_tab]:
+        d.wait_send()
 
 
 def layer(bits, ins):
@@ -684,7 +727,7 @@
     sizes = [n for _, _, n, _ in CHUNKS]
 
     def parts_of(n, order):
-        shards, buffers = 2, []
+        shards, buffers = 2 if "x" in order else 1, []
         for d in order:
             if d == "x":
                 shards = 1
@@ -694,24 +737,25 @@
                 buffers.append(vm((shards * (3 if d == "q" else 1), n, 768), BF))
         return buffers
 
+    both = (512, 768)
     scratch = dict(
-        own=vm((4, 768, 768), BF), cross=vm((4, 768, 768), BF), feed=vm((4, 1536, 768), BF), raw=vm(square, BF),
-        tok=vm(wide, BF), cot=vm(wide, BF), mem=vm((1024, 768), BF),
-        s0=vm(wide, F32), s1=vm(wide, F32), s2=vm(wide, F32), gst=vm(wide, F32), acc=vm(wide, F32),
-        n1=vm(wide, BF), n2=vm(wide, BF), rows=vm(wide, BF),
-        qkv=vm((4, 256, 576), BF), kvT1=vm((4, 384, 256), BF), q2=vm((4, 256, 192), BF),
-        kv=vm((4, 1024, 384), BF), kvT=vm((4, 384, 1024), BF), mix1=vm((4, 192, 256), BF), mix2=vm((4, 192, 256), BF),
-        lse=vm((8, 8, 256), F32), mask2=vm((1024, 128), F32), tagv=vm((256, 128), F32), btab=vm((4, 8, 256), F32),
+        own=vm((2, 768, 768), BF), cross=vm((4, 768, 768), BF), feed=vm((2, 1536, 768), BF),
+        tok=vm(wide, BF), cot=vm(both, BF), mem=vm((1024, 768), BF), n1=vm(both, BF), n3=vm(both, BF), rows1=vm(both, BF),
+        out=vm((4, 256, 768), BF), arrived=vm((4, 256, 768), BF),
+        s0=vm(wide, F32), s1=vm(wide, F32), s2=vm(wide, F32), gst=vm(wide, F32), acc=vm(wide, F32), sums=vm(both, F32), grads=vm(both, F32),
+        n2=vm(wide, BF), rows2=vm(wide, BF), act=vm(wide, BF), actT=vm((2, 768, 512), BF), gb=vm((2, 512, 768), BF),
+        qkv=vm((4, 256, 576), BF), kvT1=vm((4, 384, 256), BF), q2=vm((4, 256, 192), BF), gT=vm((2, 576, 512), BF),
+        kv=vm((4, 1024, 384), BF), kvT=vm((4, 384, 1024), BF), mix1=vm((2, 192, 512), BF), mix2=vm((4, 192, 256), BF),
+        lse=vm((8, 8, 256), F32), mask2=vm((1024, 128), F32), tagv=vm((256, 128), F32), btab=vm((2, 8, 256), F32),
         sm=vm((6, 8, 256), F32), smb=vm((2 + bits, 6, 8, 256), F32), gmv=vm((1024, 768), BF), lov=vm(wide, BF), gtv=vm(wide, BF),
-        receive=vm((2, 1536, 768), BF),
     )
+    first = [vm((2 if "x" in order else 1, n, 768), BF) for _, _, n, order in CHUNKS]
     parts = [parts_of(n, order) for _, _, n, order in CHUNKS]
     results = [vm((n, 768), BF) for n in sizes]
     more = [vm((bits - 3, n // 8, 768), BF) for n in sizes] if bits > 3 else []
     dma = pltpu.SemaphoreType.DMA
-    sems = dict(gsend=dma((7, 11)), grecv=dma((7, 11)), rsend=dma((len(CHUNKS), 16 + bits)), rrecv=dma((len(CHUNKS), 16 + bits)), lsem=dma((15,)), osem=dma((len(CHUNKS),)),
-                esem=dma((3,)), ssend=dma((2 + bits,)), srecv=dma((2 + bits,)), tsend=dma((3,)), trecv=dma((3,)),
-                credit=pltpu.SemaphoreType.REGULAR)
+    sems = dict(gsend=dma((2, 11)), grecv=dma((2, 11)), xsend=dma((8,)), xrecv=dma((8,)), csend=dma((3,)), crecv=dma((3,)), rsend=dma((len(CHUNKS), 16 + bits)), rrecv=dma((len(CHUNKS), 16 + bits)), lsem=dma((13,)), osem=dma((len(CHUNKS),)),
+                esem=dma((3,)), ssend=dma((2 + bits,)), srecv=dma((2 + bits,)))
     names = list(inputs) + list(out) + list(scratch) + list(sems)
 
     def kernel(*refs):
@@ -720,16 +764,12 @@
         r.parts = [[next(rest) for _ in p] for p in parts]
         r.result = [next(rest) for _ in results]
         r.more = [next(rest) for _ in more]
-        r.first, at = [], [0, 0]
-        for a, _, n, _ in CHUNKS:
-            shared = int(a != 2)
-            r.first.append(r.receive.at[:, pl.ds(at[shared], n), :])
-            at[shared] += n
+        r.first = [next(rest) for _ in first]
         layer_kernel(bits, r)
 
     return pl.pallas_call(
         kernel, out_shape=list(out.values()), in_specs=list(inputs.values()), out_specs=out_specs,
-        scratch_shapes=list(scratch.values()) + list(sems.values()) + sum(parts, []) + results + more,
+        scratch_shapes=list(scratch.values()) + list(sems.values()) + sum(parts, []) + results + more + first,
         compiler_params=pltpu.CompilerParams(collective_id=0, has_side_effects=True, vmem_limit_bytes=VMEM_LIMIT),
     )(*ins)
 
@@ -743,9 +783,8 @@
         o[...] = own[192 * i:192 * i + 192, :].astype(F32)
     for i, o in enumerate((o_ck, o_cv, o_cq, o_co)):
         o[...] = cross[192 * i:192 * i + 192, :].astype(F32)
-    for i in range(3):
-        o_hin[:, 256 * i:256 * i + 256] = feed[512 * i:512 * i + 256, :].T.astype(F32)
-        o_hout[256 * i:256 * i + 256, :] = feed[512 * i + 256:512 * i + 512, :].astype(F32)
+    o_hin[...] = feed[0:768, :].astype(F32)
+    o_hout[...] = feed[768:1536, :].astype(F32)
 
     @pl.when(pl.program_id(0) == 0)
     def _():
@@ -771,7 +810,7 @@
     ends = [cut(256), cut(256), cut(1024)]
     in_specs = ends + [full(2, 8, 256), full(8, 256), cut(768), cut(768), cut(1536)]
     out_specs = ends + [full(2, 768)] + [full(768)] * 3 + [cut(192)] * 4 + [full(3, 32)] + [cut(192)] * 4
-    out_specs += [pl.BlockSpec((768 // n, 768), lambda i: (i, 0)), cut(768)]
+    out_specs += [cut(768), cut(768)]
     return pl.pallas_call(finish_kernel, grid=(n,), out_shape=shapes, in_specs=in_specs, out_specs=out_specs,
                           compiler_params=pltpu.CompilerParams(vmem_limit_bytes=VMEM_LIMIT))(*args)
 

time: 203 us -> 186 us (0.916)
  Pallas kernels: 202 us -> 185 us
    pallas_call x1, Pallas kernels: 194 us -> 177 us  [layer(): pl.pallas_call(kernel, out_shape=list(out.values()), in_specs=list(inputs...]
where the time goes in v4:
time: 186 us
  Pallas kernels  185 us (99%)
    pallas_call x1, Pallas kernels, layer(): pl.pallas_call(kernel, out_shape=list(out.values()), in_specs=list(inputs...  177 us
    pallas_call x1, Pallas kernels, finish(): pl.pallas_call(finish_kernel, grid=(n,), out_shape=shapes, in_specs=in_sp...  7.94 us

profile of v4, /device:TPU:0, one launch (start us, length us, event | category | flops | bytes accessed | tf_op | source)
XLA Modules:
  0.0 186.2 jit_solution(13295492260673826245)
XLA Ops:
  0.7 177.4 %shard_map.340 = (bf16[256,768]{1,0:T(8,128)(2,1)}, bf16[256,768]{1,0:T(8,128)(2,1)}, bf16[1024,768]{1,0:T(8,128)(2,1)}, f32[2,8,256]{2,1,0:T(8,128)}, f32[8,256...) custom-call(bf16[256,768]{1,0:T(8,128)(2,1)} %bitcast.21, ...), custom_call_target="tpu_custom_call" | custom-call | tf_op jit(solution)/shard_map/pallas_call | solution.py:770
  178.1 7.9 %shard_map.341 = (bf16[256,768]{1,0:T(8,128)(2,1)}, bf16[256,768]{1,0:T(8,128)(2,1)}, bf16[1024,768]{1,0:T(8,128)(2,1)}, f32[2,768]{1,0:T(2,128)}, f32[768]{0:T(...) custom-call(bf16[256,768]{1,0:T(8,128)(2,1)} %get-tuple-element.44.l, ...), custom_call_target="tpu_custom_call" | custom-call | tf_op jit(solution)/shard_map/pallas_call | solution.py:814

commit v5 on v4

--- a/solution.py
+++ b/solution.py
@@ -20,27 +20,28 @@
 NT = (((1,), (1,)), ((), ()))
 MESH = pl.DeviceIdType.MESH
 
-UNITS = ((0, 384), (384, 384))
+UNITS = ((0, 384), (384, 192), (576, 192))
 CHUNKS = (
-    (2, 0, 256, 'yq'),
-    (2, 256, 256, 'yq'),
-    (2, 512, 256, 'yzw'),
-    (2, 768, 256, 'yzw'),
+    (2, 0, 256, 'yzw'),
+    (2, 256, 256, 'yzw'),
+    (2, 512, 256, 'yq'),
+    (2, 768, 256, 'zyw'),
     (2, 1024, 512, 'yzw'),
     (1, 384, 128, 'yxzw'),
-    (1, 512, 256, 'xyzw'),
-    (1, 0, 256, 'xyzw'),
-    (1, 256, 128, 'xzwy'),
-    (0, 0, 384, 'yq'),
-    (0, 384, 384, 'yzw'),
+    (1, 512, 256, 'yxzw'),
+    (1, 0, 128, 'yxzw'),
+    (1, 128, 256, 'yxzw'),
+    (0, 0, 384, 'yzw'),
+    (0, 384, 128, 'yq'),
+    (0, 512, 256, 'zwy'),
 )
 SCHEDULE = (
-    (), (), (), (), (), (), (1, 11, 2, 3, 12, 13, 4), (), (14,), (), (), (), (), (), (), (), (), (1000, 1010, 1020),
-    (1030, 1040, 1001, 1011, 1021, 1031, 1041), (1002,), (), (1012,), (1050, 1060, 1022, 1003), (1013, 1032, 1023), (),
-    (1051, 1052, 1061, 1062, 1004), (1042,), (), (), (1070, 1080, 1014), (), (1033,), (), (1024, 1053), (1043,), (1005, 1034),
-    (1071, 1072, 1081, 1082, 1015, 1025), (1090,), (1100, 1063, 1044, 1091, 1054, 1101, 1035, 1026, 1064, 1055, 1045, 1036),
-    (200, 1065),
-    (1092, 1056, 201, 1046, 1102, 1073, 1066, 1027, 1083, 202, 1093, 1037, 1057, 1103, 1067, 1084, 1047, 1058, 1074, 1094, 203, 1068, 1059, 1104, 1085, 1075, 204, 1095, 1105, 1069, 1076, 1086, 205, 1087, 1106, 1077, 1088, 1078, 1107, 1089, 1079),
+    (), (), (), (1,), (), (2, 3), (4, 11), (), (12, 13), (14,), (21,), (), (22, 23), (24,), (), (), (), (), (1000,), (1010,),
+    (1020,), (1030,), (), (1040, 1001, 1011, 1021, 1031), (1041,), (), (), (1050, 1060), (1004,), (1002,), (1012, 1032, 1003),
+    (1022, 1013), (), (), (1051, 1052, 1042, 1061, 1062, 1023), (1033, 1014, 1005), (), (), (1070, 1080, 1053, 1043), (), (), (),
+    (), (1054, 1024), (1063, 1034), (1071, 1072, 1081, 1082, 1015), (1090,),
+    (1100, 1110, 1025, 1055, 1006, 1064, 1044, 1091, 1101, 1111, 1035, 1073, 1016, 1056, 1065), (200,),
+    (1074, 1083, 201, 1112, 1045, 1007, 1075, 1084, 202, 1113, 1066, 1092, 1102, 1085, 1093, 1046, 1017, 203, 1076, 1057, 1086, 1067, 204, 1114, 1058, 1094, 1047, 1068, 1077, 1087, 1059, 205, 1103, 1078, 1115, 1069, 1088, 1095, 1079, 1104, 1036, 1089, 1096, 1105, 1116, 1037, 1097, 1117),
 )
 
 
@@ -114,11 +115,6 @@
     for b in range(1, BUCKETS):
         chosen = chosen + jnp.where(n >= int(np.argmax(bucket >= b)), 1, 0)
     return (chosen == lax.broadcasted_iota(jnp.int32, (BUCKETS, 256), 0)).astype(BF)
-
-
-def third(size, i):
-    cut = {96: (32, 32, 32), 128: (32, 48, 48)}[size]
-    return sum(cut[:i]), cut[i]
 
 
 def layer_kernel(bits, r):
@@ -159,8 +155,11 @@
 
     slot = lambda v, k, i: v.at[k, pl.ds(192 * i, 192), :]
     token_load = load(r.tok_in, r.tok)
+    small_loads = [load(a, b) for a, b in ((r.emb_in, r.emb), (r.tags_in, r.tags), (r.gain1_in, r.gain1), (r.tab_in, r.tab),
+                                           (r.gain2_in, r.gain2), (r.gain3_in, r.gain3), (r.mmask_in, r.mmask))]
+    key_loads = [load(src, slot(r.cross, t, i)) for i, src in enumerate((r.ck, r.cv))]
     self_loads = [load(src, slot(r.own, c, i)) for i, src in enumerate((r.sq, r.sk, r.sv, r.so))]
-    cross_loads = [load(src, slot(r.cross, t, i)) for i, src in enumerate((r.ck, r.cv, r.cq, r.co))]
+    query_loads = [load(src, slot(r.cross, t, 2 + i)) for i, src in enumerate((r.cq, r.co))]
     memory_load = load(r.mem_in, r.mem)
     feed_loads = [load(src, r.feed.at[c, pl.ds(768 * i, 768), :]) for i, src in enumerate((r.hin, r.hout))]
     cotangent_load = load(r.cot_in, r.cot.at[mine, :])
@@ -170,6 +169,8 @@
     for p in partners:
         pl.semaphore_signal(barrier, inc=1, device_id=p, device_id_type=MESH)
 
+    for d in small_loads:
+        d.wait()
     g_self, g_cross, g_hid = (g[...].astype(F32).reshape(1, 768) for g in (r.gain1, r.gain2, r.gain3))
     ji = lax.broadcasted_iota(jnp.int32, (256, 256), 0)
     ii = lax.broadcasted_iota(jnp.int32, (256, 256), 1)
@@ -185,6 +186,7 @@
     def gather_copy(u, j):
         row, size = UNITS[u]
         v, q = r.cross, size // 4
+        part = 32 if q == 48 else q // 2
         sems = (r.gsend.at[u, j], r.grecv.at[u, j])
         at = lambda shard, quarter, first=0, n=q: v.at[shard, rows_of(row + quarter * q + first, n), :]
         core, over_x, over_y, over_z = (dp, tc), (dp, tx), (pb[0], t), (pb[1], t)
@@ -192,8 +194,6 @@
             ref, to = v.at[t, pl.ds(row, size), :], core
         elif j == 1:
             ref, to = at(t, quad), over_x
-        elif j == 2:
-            ref, to = at(t, quad_d, *third(q, 0)), over_x
         elif j == 3:
             ref, to = at(tx, quad), over_y
         elif j == 4:
@@ -201,18 +201,18 @@
         elif j == 5:
             ref, to = at(tx, quad), core
         elif j == 6:
-            ref, to = at(tx, quad_y, *third(q, 2)), over_z
+            ref, to = at(tx, quad_y, part, q - part), over_z
         elif j == 7:
             ref, to = at(tx, quad_y), core
         elif j == 8:
-            ref, to = at(tx, quad_z, *third(q, 1)), over_y
+            ref, to = at(tx, quad_z, 0, part), over_y
         elif j == 9:
             ref, to = at(tx, quad_z), core
         else:
             ref, to = at(tx, quad_d), core
         return Remote(ref, ref, *sems, to)
 
-    GATHER = {0: ((), (1, 2, 0)), 1: ((1,), (3, 4, 5)), 2: ((3,), (6, 7)), 3: ((4,), (8, 9)), 4: ((2, 8, 6), (10,)),
+    GATHER = {0: ((), (1, 0)), 1: ((1,), (3, 4, 5)), 2: ((3,), (6, 7)), 3: ((4,), (8, 9)), 4: ((8, 6), (10,)),
               5: ((0,), ()), 6: ((5, 7, 9, 10), ())}
 
     def gather_step(u, step):
@@ -367,31 +367,50 @@
     def to_core(j, src, dst):
         return Remote(src, dst, r.csend.at[j], r.crecv.at[j], (dp, tc))
 
-    trade = [over_x(j, v.at[mine, :], v.at[mine, :]) for j, v in enumerate((r.n1, r.cot, r.n3, r.rows1))]
-    trade_n1, trade_cot, trade_n3, trade_rows = trade
-    give = [over_x(4 + j, r.out.at[j], r.arrived.at[j]) for j in range(4)]
-    give_s1, give_lo, give_gn, give_gn1 = give
+    def half(start, h):
+        return rows_of(start + 128 * h, 128)
+
+    trade_cot, trade_rows = trade = [over_x(j, v.at[mine, :], v.at[mine, :]) for j, v in enumerate((r.cot, r.rows1))]
+    trade_n1, trade_n3 = ([over_x(2 + 2 * j + h, v.at[half(256 * x, h), :], v.at[half(256 * x, h), :]) for h in range(2)]
+                          for j, v in enumerate((r.n1, r.n3)))
+    give_lo, give_gn1 = give = [over_x(6 + j, r.out.at[i], r.arrived.at[i]) for j, i in enumerate((1, 3))]
+    give_s1, give_gn = ([over_x(8 + 2 * j + h, r.out.at[i, half(0, h), :], r.arrived.at[i, half(0, h), :]) for h in range(2)]
+                        for j, i in enumerate((0, 2)))
     core_own, core_feed, core_tab = (to_core(j, v.at[c], v.at[c]) for j, v in enumerate((r.own, r.feed, r.btab)))
-    trade_n1.start()
+    for d in key_loads:
+        d.wait()
+    gather_step(0, 0)
+    start(trade_n1)
     for d in self_loads:
         d.wait()
     core_own.start()
     core_tab.start()
-    for d in cross_loads:
+    for d in query_loads:
         d.wait()
-    gather_step(0, 0)
     gather_step(1, 0)
     for d in feed_loads:
         d.wait()
     core_feed.start()
 
-    lane576 = lax.broadcasted_iota(jnp.int32, (1, 576), 1)
-
     def bias_of(f, i):
         return pltpu.roll(jnp.broadcast_to(r.btab[f, i:i + 1, :], (256, 256)), 0, 1, stride=1, stride_axis=0)
 
     def allowed(e):
         return (ji <= ii) & (ji < r.lengths[2 * e + c])
+
+    lane = lax.broadcasted_iota(jnp.int32, (1, 128), 1)
+    low, high = lane < 64, lane >= 64
+
+    def of_keys(a):
+        wide = jnp.concatenate([a, jnp.zeros((a.shape[0], 64), a.dtype)], axis=1)
+        return [jnp.where(low, wide[:, 0:128], 0), jnp.where(high, wide[:, 0:128], 0), jnp.where(low, wide[:, 128:256], 0)]
+
+    def of_values(a):
+        wide = jnp.concatenate([jnp.zeros((a.shape[0], 64), a.dtype), a], axis=1)
+        return [jnp.where(high, wide[:, 0:128], 0), jnp.where(low, wide[:, 128:256], 0), jnp.where(high, wide[:, 128:256], 0)]
+
+    key_lanes = (slice(0, 128), slice(0, 128), slice(128, 256))
+    value_lanes = (slice(128, 256), slice(256, 384), slice(256, 384))
 
     def columns(e):
         return pl.ds(pl.multiple_of(256 * e, 256), 256)
@@ -416,23 +435,21 @@
         valid = r.mmask[pl.ds(t, 1), :]
         r.mask2[...] = jnp.broadcast_to(jnp.where(valid == 1, 0.0, MASKED).astype(F32), (128, 1024)).T
         project_memory(t)
-        run(turns[3])
+        here()
         gather_step(0, 5)
         project_memory(tc)
-        run(turns[4])
-        trade_n1.wait_recv()
 
     def self_forward(s, _):
-        hooks(s, [turns[0], turns[1], turns[2], turns[5]], {1: near_self, 2: near_memory})
-        e, f = item_shard(s)
+        hooks(s, turns, {1: near_self})
+        e, f = x, c + s * (1 - 2 * c)
         k = 2 * e + f
         rows = r.n1.at[rows_of(256 * e, 256), :]
-        a = mm(rows[...], r.own[f, 0:576, :], NT)
-        r.qkv[k] = jnp.where(lane576 < 192, a * 0.125, a).astype(BF)
+        r.q1[k] = (mm(rows[...], r.own[f, 0:192, :], NT) * 0.125).astype(BF)
+        r.kv1[k] = mm(rows[...], r.own[f, 192:576, :], NT).astype(BF)
+        q = of_keys(r.q1[k])
         r.kvT1[k] = mm(r.own[f, 192:576, :], rows[...], NT).astype(BF)
         for i in range(3):
-            q, kk = r.qkv[k, :, 64 * i:64 * i + 64], r.qkv[k, :, 192 + 64 * i:256 + 64 * i]
-            scores = jnp.where(allowed(e), mm(kk, q, NT) + bias_of(f, i), MASKED)
+            scores = jnp.where(allowed(e), mm(r.kv1[k, :, key_lanes[i]], q[i], NT) + bias_of(f, i), MASKED)
             most = jnp.max(scores, axis=0, keepdims=True)
             p = jnp.exp(scores - most)
             total = jnp.sum(p, axis=0, keepdims=True)
@@ -441,23 +458,55 @@
             r.lse[k, i:i + 1, :] = most + jnp.log(total)
         return 0
 
-    def self_out(e):
-        return mm(r.mix1[0, :, columns(e)].T, r.own[0, 576:768, :]) + mm(r.mix1[1, :, columns(e)].T, r.own[1, 576:768, :])
-
-    turns = take(6)
-    lax.fori_loop(0, 4, self_forward, 0)
-    r.out[0] = self_out(1 - x).astype(BF)
-    give_s1.start()
+    def self_far(h):
+        n, e, cols = 128 * (h + 1), 1 - x, slice(128 * h, 128 * h + 128)
+
+        def turn(i, _):
+            f = c + i * (1 - 2 * c)
+            k = 2 * e + f
+            rows = r.n1.at[half(256 * e, h), :]
+            r.q1[k, cols, :] = (mm(rows[...], r.own[f, 0:192, :], NT) * 0.125).astype(BF)
+            r.kv1[k, cols, :] = mm(rows[...], r.own[f, 192:576, :], NT).astype(BF)
+            r.kvT1[k, :, cols] = mm(r.own[f, 192:576, :], rows[...], NT).astype(BF)
+            q = of_keys(r.q1[k, cols, :])
+            for j in range(3):
+                scores = mm(r.kv1[k, 0:n, key_lanes[j]], q[j], NT) + bias_of(f, j)[0:n, cols]
+                scores = jnp.where(allowed(e)[0:n, cols], scores, MASKED)
+                most = jnp.max(scores, axis=0, keepdims=True)
+                p = jnp.exp(scores - most)
+                total = jnp.sum(p, axis=0, keepdims=True)
+                o = mm(r.kvT1[k, 192 + 64 * j:256 + 64 * j, 0:n], p.astype(BF))
+                r.mix1[f, 64 * j:64 * j + 64, pl.ds(pl.multiple_of(256 * e + 128 * h, 128), 128)] = (o / total).astype(BF)
+                r.lse[k, j:j + 1, cols] = most + jnp.log(total)
+            return 0
+
+        lax.fori_loop(0, 2, turn, 0)
+        r.out[0, cols, :] = self_out(pl.ds(pl.multiple_of(256 * e + 128 * h, 128), 128)).astype(BF)
+        give_s1[h].start()
+
+    def self_out(at):
+        return mm(r.mix1[0, :, at].T, r.own[0, 576:768, :]) + mm(r.mix1[1, :, at].T, r.own[1, 576:768, :])
+
+    turns = take(2)
+    lax.fori_loop(0, 2, self_forward, 0)
+    here()
+    near_memory()
+    for h in range(2):
+        here()
+        trade_n1[h].wait_recv()
+        self_far(h)
+    gather_step(2, 0)
     cotangent_load.wait()
     trade_cot.start()
-    r.s1[...] = r.s0[...] + self_out(x)
+    r.s1[...] = r.s0[...] + self_out(columns(x))
     here()
     project_memory(tx)
     here()
     gather_step(0, 6)
     project_memory(td)
     here()
-    give_s1.wait_recv()
+    for d in give_s1:
+        d.wait_recv()
     x1 = r.s1[...] + r.arrived[0].astype(F32)
     r.s1[...] = x1
     r.n2[...] = (x1 * inverse_of(x1) * g_cross).astype(BF)
@@ -465,15 +514,15 @@
 
     def cross_scores(shard, i, b, q):
         at = slice(256 * b, 256 * b + 256)
-        return mm(r.kv[shard, at, 64 * i:64 * i + 64], q, NT) + jnp.concatenate([r.mask2[at, :]] * 2, axis=1)
+        return mm(r.kv[shard, at, key_lanes[i]], q, NT) + jnp.concatenate([r.mask2[at, :]] * 2, axis=1)
 
     def cross_forward(s, _):
         hooks(s, turns_1, {3: lambda: gather_step(1, 6)})
         k = fwd_shard(s)
         r.q2[k] = (mm(r.n2[...], r.cross[k, 384:576, :], NT) * 0.125).astype(BF)
+        q = of_keys(r.q2[k])
         for i in range(3):
-            q = r.q2[k, :, 64 * i:64 * i + 64]
-            ss = [cross_scores(k, i, b, q) for b in range(4)]
+            ss = [cross_scores(k, i, b, q[i]) for b in range(4)]
             most = jnp.max(jnp.maximum(jnp.maximum(ss[0], ss[1]), jnp.maximum(ss[2], ss[3])), axis=0, keepdims=True)
             total, o = 0.0, 0.0
             for b in range(4):
@@ -487,25 +536,22 @@
     turns_1 = take(4)
     lax.fori_loop(0, 4, cross_forward, 0)
     here()
+    gather_step(2, 5)
+    gather_step(2, 6)
     x2 = r.s1[...]
     for k in range(4):
         x2 = x2 + mm(r.mix2[k].T, r.cross[k, 576:768, :])
     r.s2[...] = x2
     r.n3[mine, :] = (x2 * inverse_of(x2) * g_hid).astype(BF)
-    trade_n3.start()
+    start(trade_n3)
     r.sums[mine, :] = x2
     r.sums[other, :] = jnp.zeros_like(x2)
     r.grads[...] = jnp.zeros_like(r.grads)
     core_feed.wait_recv()
 
-    def far_rows():
-        trade_cot.wait_recv()
-        trade_n3.wait_recv()
-
-    def feed(s, _):
-        hooks(s, [turns_2[0], (), turns_2[1]], {2: far_rows})
-        e, f = item_shard(s)
-        at = rows_of(256 * e, 256)
+    def feed(f, first, n):
+        at = rows_of(first, n)
+        lanes = pl.ds(pl.multiple_of(first, 128), n)
         rows, cot = r.n3.at[at, :], r.cot.at[at, :]
         for i in range(3):
             cs = slice(256 * i, 256 * i + 256)
@@ -514,44 +560,45 @@
             phi = 0.5 * (1.0 + lax.erf(v * np.float32(1 / math.sqrt(2))))
             act = (v * phi).astype(BF)
             slope = phi + v * (jnp.exp(-0.5 * v * v) * np.float32(1 / math.sqrt(2 * math.pi)))
-            r.act[:, cs] = act
-            r.actT[f, cs, columns(e)] = act.T
+            r.act[0:n, cs] = act
+            r.actT[f, cs, lanes] = act.T
             r.gb[f, at, cs] = (slope * ga).astype(BF)
-        r.sums[at, :] += mm(r.act[...], r.feed[f, 768:1536, :])
+        r.sums[at, :] += mm(r.act[0:n, :], r.feed[f, 768:1536, :])
         r.grads[at, :] += mm(r.gb[f, at, :], r.feed[f, 0:768, :], NT)
-        return 0
-
-    turns_2 = take(2)
-    lax.fori_loop(0, 4, feed, 0)
-    r.out[2] = r.grads[other, :].astype(BF)
-    give_gn.start()
+
+    def feed_both(first, n):
+        def turn(i, _):
+            feed(c + i * (1 - 2 * c), first, n)
+            return 0
+        lax.fori_loop(0, 2, turn, 0)
+
+    here()
+    feed_both(256 * x, 256)
+    here()
+    trade_cot.wait_recv()
+    for h in range(2):
+        if h:
+            here()
+        trade_n3[h].wait_recv()
+        feed_both(256 - 256 * x + 128 * h, 128)
+        r.out[2, 128 * h:128 * h + 128, :] = r.grads[half(256 - 256 * x, h), :].astype(BF)
+        give_gn[h].start()
     r.out[1] = r.sums[other, :].astype(BF)
     give_lo.start()
     here()
     core_feed.wait_send()
 
-    def feed_weights(f, _):
-        def block(i, _):
-            at = rows_of(256 * i, 256)
-            r.feed[f, at, :] = mm(r.n3[:, pl.ds(pl.multiple_of(256 * i, 256), 256)].T, r.gb[f]).astype(BF)
-            return 0
-        lax.fori_loop(0, 3, block, 0)
-        return 0
-
-    lax.fori_loop(0, 2, feed_weights, 0)
-    here()
-
-    def feed_out_weights(f, _):
-        def block(i, _):
-            at = rows_of(256 * i, 256)
-            r.feed[f, rows_of(768 + 256 * i, 256), :] = mm(r.actT[f, at, :], r.cot[...]).astype(BF)
-            return 0
-        lax.fori_loop(0, 3, block, 0)
-        return 0
-
-    lax.fori_loop(0, 2, feed_out_weights, 0)
-    here()
-    give_gn.wait_recv()
+    for i in range(3):
+        n3T = r.n3[:, 256 * i:256 * i + 256].T
+        for f in range(2):
+            r.feed[f, 256 * i:256 * i + 256, :] = mm(n3T, r.gb[f]).astype(BF)
+        here()
+    for i in range(3):
+        for f in range(2):
+            r.feed[f, 768 + 256 * i:1024 + 256 * i, :] = mm(r.actT[f, 256 * i:256 * i + 256, :], r.cot[...]).astype(BF)
+        here()
+    for d in give_gn:
+        d.wait_recv()
     d, gain = norm_back(x2, inverse_of(x2), g_hid, r.grads[mine, :] + r.arrived[2].astype(F32))
 
     def put_small(row, value):
@@ -562,7 +609,7 @@
     r.sm[...] = jnp.zeros_like(r.sm)
     put_small(4, gain)
     r.gst[...] = r.cot[mine, :].astype(F32) + d
-    gather_sent(range(2), range(11))
+    gather_sent(range(3), (0, 1, 3, 4, 5, 6, 7, 8, 9, 10))
     here()
     r.rows2[...] = r.gst[...].astype(BF)
     r.acc[...] = jnp.zeros_like(x2)
@@ -575,33 +622,32 @@
         G = mm(rw, w, NT).astype(BF)
         GT = mm(w, rw, NT).astype(BF)
         r.cross[k, 576:768, :] = mm(r.mix2[k], rw).astype(BF)
-        dqs, dks, dvs = [], [], []
-        for i in range(3):
-            q = r.q2[k, :, 64 * i:64 * i + 64]
-            gi, gT = G[:, 64 * i:64 * i + 64], GT[64 * i:64 * i + 64, :]
-            inner = jnp.sum(r.mix2[k, 64 * i:64 * i + 64, :].astype(F32) * gT.astype(F32), axis=0, keepdims=True)
-            ls = r.lse[4 + k, i:i + 1, :]
-            dq, dk, dv = 0.0, [], []
-            for b in range(4):
-                at = slice(256 * b, 256 * b + 256)
-                p = jnp.exp(cross_scores(k, i, b, q) - ls)
-                dp_ = mm(r.kv[k, at, 192 + 64 * i:256 + 64 * i], gi, NT)
-                gs = (p * (dp_ - inner)).astype(BF)
-                dq = dq + mm(r.kvT[k, 64 * i:64 * i + 64, at], gs)
-                dk.append(mm(gs, q).astype(BF))
-                dv.append(mm(p.astype(BF), gi).astype(BF))
-            dqs.append((dq * 0.125).astype(BF))
-            dks.append(dk)
-            dvs.append(dv)
+        q, g = of_keys(r.q2[k]), of_values(G)
+        inner = [jnp.sum(r.mix2[k, 64 * i:64 * i + 64, :].astype(F32) * GT[64 * i:64 * i + 64, :].astype(F32), axis=0, keepdims=True)
+                 for i in range(3)]
+        dqs = [0.0, 0.0, 0.0]
         for b in range(4):
-            r.kv[k, 256 * b:256 * b + 256, :] = jnp.concatenate([v[b] for v in dks + dvs], axis=1)
+            if b == 2:
+                hooks(s, turns_m)
+            at = slice(256 * b, 256 * b + 256)
+            dks, dvs = [], []
+            for i in range(3):
+                p = jnp.exp(cross_scores(k, i, b, q[i]) - r.lse[4 + k, i:i + 1, :])
+                gs = (p * (mm(r.kv[k, at, value_lanes[i]], g[i], NT) - inner[i])).astype(BF)
+                dqs[i] = dqs[i] + mm(r.kvT[k, 64 * i:64 * i + 64, at], gs)
+                dks.append(mm(gs, q[i]))
+                dvs.append(mm(p.astype(BF), g[i]))
+            r.kv[k, at, 0:128] = (dks[0] + dks[1]).astype(BF)
+            r.kv[k, at, 128:256] = (dks[2] + dvs[0]).astype(BF)
+            r.kv[k, at, 256:384] = (dvs[1] + dvs[2]).astype(BF)
+        dqs = [(d * 0.125).astype(BF) for d in dqs]
         r.kvT[k] = r.kv[k].T
         dqT = jnp.concatenate(dqs, axis=0)
         r.acc[...] += mm(dqT.T, r.cross[k, 384:576, :])
         r.cross[k, 384:576, :] = mm(dqT, r.n2[...]).astype(BF)
         return 0
 
-    turns_3 = take(4)
+    turns_3, turns_m = take(4), take(4)
     lax.fori_loop(0, 4, cross_backward, 0)
     here()
     x1 = r.s1[...]
@@ -655,22 +701,21 @@
         G = mm(rw, w, NT).astype(BF)
         GT = mm(w, rw, NT).astype(BF)
         flip = (ji + ii == 255).astype(BF)
+        q, g = of_keys(r.q1[k]), of_values(G)
         dqs, dks, dvs = [], [], []
         for i in range(3):
-            q, kk = r.qkv[k, :, 64 * i:64 * i + 64], r.qkv[k, :, 192 + 64 * i:256 + 64 * i]
-            gi, gT = G[:, 64 * i:64 * i + 64], GT[64 * i:64 * i + 64, :]
+            gT = GT[64 * i:64 * i + 64, :]
             inner = jnp.sum(r.mix1[f, 64 * i:64 * i + 64, columns(e)].astype(F32) * gT.astype(F32), axis=0, keepdims=True)
-            scores = jnp.where(allowed(e), mm(kk, q, NT) + bias_of(f, i), MASKED)
+            scores = jnp.where(allowed(e), mm(r.kv1[k, :, key_lanes[i]], q[i], NT) + bias_of(f, i), MASKED)
             p = jnp.exp(scores - r.lse[k, i:i + 1, :])
-            dp_ = mm(r.qkv[k, :, 384 + 64 * i:448 + 64 * i], gi, NT)
-            gs = (p * (dp_ - inner)).astype(BF)
-            dvs.append(mm(p.astype(BF), gi).astype(BF))
-            dks.append(mm(gs, q).astype(BF))
+            gs = (p * (mm(r.kv1[k, :, value_lanes[i]], g[i], NT) - inner)).astype(BF)
+            dvs.append(mm(p.astype(BF), g[i]))
+            dks.append(mm(gs, q[i]))
             dqs.append((mm(r.kvT1[k, 64 * i:64 * i + 64, :], gs) * 0.125).astype(BF))
             shifted = pltpu.roll(mm(flip, gs), 1, 1, stride=1, stride_axis=0)
             r.sm[2 + 2 * x + f, i:i + 1, :] += jnp.sum(shifted, axis=0, keepdims=True)
         dqT = jnp.concatenate(dqs, axis=0)
-        dkv = jnp.concatenate(dks + dvs, axis=1)
+        dkv = jnp.concatenate([dks[0] + dks[1], dks[2] + dvs[0], dvs[1] + dvs[2]], axis=1).astype(BF)
         r.gT[f, 0:192, columns(e)] = dqT
         r.gT[f, 192:576, columns(e)] = dkv.T
         r.grads[here_rows, :] += mm(dqT.T, r.own[f, 0:192, :]) + mm(dkv, r.own[f, 192:576, :])
@@ -710,7 +755,7 @@
         out_copy(n).wait()
     for d in stores:
         d.wait()
-    for d in trade + give + [core_tab]:
+    for d in trade + trade_n1 + trade_n3 + give + give_s1 + give_gn + [core_tab]:
         d.wait_send()
 
 
@@ -718,7 +763,7 @@
     S = jax.ShapeDtypeStruct
     V, A, M = (pl.BlockSpec(memory_space=s) for s in (pltpu.VMEM, pl.ANY, pltpu.SMEM))
     vm = pltpu.VMEM
-    inputs = dict(tok_in=A, mem_in=A, cot_in=A, lengths=M, mmask=V, tags=V, emb=V, gain1=V, gain2=V, gain3=V, tab=V,
+    inputs = dict(tok_in=A, mem_in=A, cot_in=A, lengths=M, mmask_in=A, tags_in=A, emb_in=A, gain1_in=A, gain2_in=A, gain3_in=A, tab_in=A,
                   sq=A, sk=A, sv=A, so=A, cq=A, ck=A, cv=A, co=A, hin=A, hout=A)
     wide, square = (256, 768), (768, 768)
     out = dict(lo=S(wide, BF), gtok=S(wide, BF), gmem=S((1024, 768), BF), smo=S((2, 8, 256), F32), dgo=S((8, 256), F32),
@@ -744,9 +789,11 @@
         out=vm((4, 256, 768), BF), arrived=vm((4, 256, 768), BF),
         s0=vm(wide, F32), s1=vm(wide, F32), s2=vm(wide, F32), gst=vm(wide, F32), acc=vm(wide, F32), sums=vm(both, F32), grads=vm(both, F32),
         n2=vm(wide, BF), rows2=vm(wide, BF), act=vm(wide, BF), actT=vm((2, 768, 512), BF), gb=vm((2, 512, 768), BF),
-        qkv=vm((4, 256, 576), BF), kvT1=vm((4, 384, 256), BF), q2=vm((4, 256, 192), BF), gT=vm((2, 576, 512), BF),
+        q1=vm((4, 256, 192), BF), kv1=vm((4, 256, 384), BF), kvT1=vm((4, 384, 256), BF), q2=vm((4, 256, 192), BF), gT=vm((2, 576, 512), BF),
         kv=vm((4, 1024, 384), BF), kvT=vm((4, 384, 1024), BF), mix1=vm((2, 192, 512), BF), mix2=vm((4, 192, 256), BF),
         lse=vm((8, 8, 256), F32), mask2=vm((1024, 128), F32), tagv=vm((256, 128), F32), btab=vm((2, 8, 256), F32),
+        mmask=vm((4, 1024), jnp.int32), tags=vm((1, 256), jnp.int32), emb=vm((2, 768), BF), gain1=vm((768,), BF), gain2=vm((768,), BF),
+        gain3=vm((768,), BF), tab=vm((3, 32), BF),
         sm=vm((6, 8, 256), F32), smb=vm((2 + bits, 6, 8, 256), F32), gmv=vm((1024, 768), BF), lov=vm(wide, BF), gtv=vm(wide, BF),
     )
     first = [vm((2 if "x" in order else 1, n, 768), BF) for _, _, n, order in CHUNKS]
@@ -754,7 +801,7 @@
     results = [vm((n, 768), BF) for n in sizes]
     more = [vm((bits - 3, n // 8, 768), BF) for n in sizes] if bits > 3 else []
     dma = pltpu.SemaphoreType.DMA
-    sems = dict(gsend=dma((2, 11)), grecv=dma((2, 11)), xsend=dma((8,)), xrecv=dma((8,)), csend=dma((3,)), crecv=dma((3,)), rsend=dma((len(CHUNKS), 16 + bits)), rrecv=dma((len(CHUNKS), 16 + bits)), lsem=dma((13,)), osem=dma((len(CHUNKS),)),
+    sems = dict(gsend=dma((3, 11)), grecv=dma((3, 11)), xsend=dma((12,)), xrecv=dma((12,)), csend=dma((3,)), crecv=dma((3,)), rsend=dma((len(CHUNKS), 16 + bits)), rrecv=dma((len(CHUNKS), 16 + bits)), lsem=dma((20,)), osem=dma((len(CHUNKS),)),
                 esem=dma((3,)), ssend=dma((2 + bits,)), srecv=dma((2 + bits,)))
     names = list(inputs) + list(out) + list(scratch) + list(sems)
 
@@ -801,7 +848,7 @@
 
 def finish(args):
     S = jax.ShapeDtypeStruct
-    n = 3
+    n = 2
     cut = lambda rows: pl.BlockSpec((rows, 768 // n), lambda i: (0, i))
     full = lambda *s: pl.BlockSpec(s, lambda i: (0,) * len(s))
     flat, square = S((192, 768), F32), S((768, 768), F32)

time: 186 us -> 182 us (0.978)
  Pallas kernels: 185 us -> 181 us
    pallas_call x1, Pallas kernels: 177 us -> 174 us  [layer(): pl.pallas_call(kernel, out_shape=list(out.values()), in_specs=list(inputs...]
where the time goes in v5:
time: 182 us
  Pallas kernels  181 us (99%)
    pallas_call x1, Pallas kernels, layer(): pl.pallas_call(kernel, out_shape=list(out.values()), in_specs=list(inputs...  174 us
    pallas_call x1, Pallas kernels, finish(): pl.pallas_call(finish_kernel, grid=(n,), out_shape=shapes, in_specs=in_sp...  7.03 us

profile of v5, /device:TPU:0, one launch (start us, length us, event | category | flops | bytes accessed | tf_op | source)
XLA Modules:
  0.0 182.1 jit_solution(18045896925235074109)
XLA Ops:
  0.7 174.2 %shard_map.340 = (bf16[256,768]{1,0:T(8,128)(2,1)}, bf16[256,768]{1,0:T(8,128)(2,1)}, bf16[1024,768]{1,0:T(8,128)(2,1)}, f32[2,8,256]{2,1,0:T(8,128)}, f32[8,256...) custom-call(bf16[256,768]{1,0:T(8,128)(2,1)} %bitcast.21, ...), custom_call_target="tpu_custom_call" | custom-call | tf_op jit(solution)/shard_map/pallas_call | solution.py:817
  174.9 7.0 %shard_map.341 = (bf16[256,768]{1,0:T(8,128)(2,1)}, bf16[256,768]{1,0:T(8,128)(2,1)}, bf16[1024,768]{1,0:T(8,128)(2,1)}, f32[2,768]{1,0:T(2,128)}, f32[768]{0:T(...) custom-call(bf16[256,768]{1,0:T(8,128)(2,1)} %get-tuple-element.44.l, ...), custom_call_target="tpu_custom_call" | custom-call | tf_op jit(solution)/shard_map/pallas_call | solution.py:861

commit v6 on v5

--- a/solution.py
+++ b/solution.py
@@ -22,26 +22,27 @@
 
 UNITS = ((0, 384), (384, 192), (576, 192))
 CHUNKS = (
-    (2, 0, 256, 'yzw'),
-    (2, 256, 256, 'yzw'),
-    (2, 512, 256, 'yq'),
-    (2, 768, 256, 'zyw'),
+    (2, 0, 256, 'zyw'),
+    (2, 256, 256, 'zwy'),
+    (2, 512, 256, 'yzw'),
+    (2, 768, 256, 'yzw'),
     (2, 1024, 512, 'yzw'),
-    (1, 384, 128, 'yxzw'),
-    (1, 512, 256, 'yxzw'),
-    (1, 0, 128, 'yxzw'),
-    (1, 128, 256, 'yxzw'),
-    (0, 0, 384, 'yzw'),
-    (0, 384, 128, 'yq'),
-    (0, 512, 256, 'zwy'),
+    (1, 384, 128, 'xyzw'),
+    (1, 512, 256, 'xyzw'),
+    (1, 0, 128, 'xyzw'),
+    (1, 128, 128, 'xyzw'),
+    (1, 256, 128, 'xzyw'),
+    (0, 0, 256, 'yzw'),
+    (0, 256, 256, 'yzw'),
+    (0, 512, 256, 'yzw'),
 )
 SCHEDULE = (
     (), (), (), (1,), (), (2, 3), (4, 11), (), (12, 13), (14,), (21,), (), (22, 23), (24,), (), (), (), (), (1000,), (1010,),
-    (1020,), (1030,), (), (1040, 1001, 1011, 1021, 1031), (1041,), (), (), (1050, 1060), (1004,), (1002,), (1012, 1032, 1003),
-    (1022, 1013), (), (), (1051, 1052, 1042, 1061, 1062, 1023), (1033, 1014, 1005), (), (), (1070, 1080, 1053, 1043), (), (), (),
-    (), (1054, 1024), (1063, 1034), (1071, 1072, 1081, 1082, 1015), (1090,),
-    (1100, 1110, 1025, 1055, 1006, 1064, 1044, 1091, 1101, 1111, 1035, 1073, 1016, 1056, 1065), (200,),
-    (1074, 1083, 201, 1112, 1045, 1007, 1075, 1084, 202, 1113, 1066, 1092, 1102, 1085, 1093, 1046, 1017, 203, 1076, 1057, 1086, 1067, 204, 1114, 1058, 1094, 1047, 1068, 1077, 1087, 1059, 205, 1103, 1078, 1115, 1069, 1088, 1095, 1079, 1104, 1036, 1089, 1096, 1105, 1116, 1037, 1097, 1117),
+    (1020,), (1030,), (), (1040, 1001, 1011, 1021, 1031), (1041,), (), (1022,), (1032, 1050, 1060, 1023), (1002, 1033, 1013), (),
+    (1012,), (), (1024, 1042), (), (1051, 1052, 1061, 1062, 1003, 1014, 1034), (1015, 1025), (), (), (1070, 1080, 1090), (1004,),
+    (), (), (1035,), (1043, 1026), (1016, 1053), (1071, 1072, 1081, 1082, 1091, 1092, 1005, 1036), (1100, 1027),
+    (1110, 1120, 1054, 1044, 1101, 1111, 1017, 1063, 1121, 1006, 1055, 1037, 1045, 1007), (200, 1102, 1056),
+    (201, 1046, 1112, 1103, 1057, 1113, 1064, 1058, 1104, 1093, 1122, 202, 1114, 1065, 1105, 1073, 1123, 1047, 1083, 1115, 1059, 1094, 203, 1066, 1106, 1074, 1124, 1116, 1084, 204, 1095, 1067, 1107, 1075, 1125, 205, 1085, 1096, 1117, 1068, 1076, 1126, 1086, 1069, 1097, 1077, 1087, 1078, 1127, 1088, 1098, 1079, 1099, 1089),
 )
 
 
@@ -246,13 +247,15 @@
     turn = lambda b, f: b + f * (1 - 2 * b)
     along_z = [dp + f1 * (2 - 4 * z1) + f2 * (4 - 8 * z2) for f1, f2 in flips]
 
+    count = iter(range(999))
+
     def plan_of(n):
         order, buffers = CHUNKS[n][3], iter(r.parts[n])
-        halves, shards, stages, gathers, count = [], [tx, t] if "x" in order else [t], [], [], iter(range(99))
+        halves, shards, stages, gathers = [], [tx, t] if "x" in order else [t], [], []
 
         def copy(src, dst, to):
             j = next(count)
-            return Remote(src, dst, r.rsend.at[n, j], r.rrecv.at[n, j], to)
+            return Remote(src, dst, r.rsend.at[j], r.rrecv.at[j], to)
 
         def piece(shard, at):
             return view(n, shard, *place(n, at))
@@ -289,6 +292,9 @@
     def start(copies):
         for d in copies:
             d.start()
+
+    def sent_of(p):
+        return [d for d, _, _ in p.core] + sum([copies for copies, _ in p.stages], []) + sum(p.back, [])
 
     def reduce_step(n, j):
         p = plans[n]
@@ -324,13 +330,21 @@
                 start(p.back[i + 1])
             else:
                 out_copy(n).start()
+                for d in sent_of(p)[:-len(p.back[-1])]:
+                    d.wait_send()
 
     to = [(dp, tc), (dp, tx)] + [(p, t) for p in pb]
+
+    small_stores = [pltpu.make_async_copy(r.sm.at[pl.ds(0, 2)], r.smo, r.esem.at[3]),
+                    pltpu.make_async_copy(r.sm.at[2 + t], r.dgo, r.esem.at[4])]
 
     def small_step(j):
         if j:
             Remote(r.sm, r.smb.at[j - 1], r.ssend.at[j - 1], r.srecv.at[j - 1], to[j - 1]).wait()
             r.sm[...] = r.sm[...] + r.smb[j - 1]
+        if j == len(to):
+            for d in small_stores:
+                d.start()
         if j < len(to):
             Remote(r.sm, r.smb.at[j], r.ssend.at[j], r.srecv.at[j], to[j]).start()
 
@@ -734,6 +748,8 @@
         r.own[f, 384:576, :] = mm(r.gT[f, 384:576, :], r.n1[...]).astype(BF)
         r.own[f, 576:768, :] = mm(r.mix1[f], r.rows1[...]).astype(BF)
     here()
+    for d in trade + trade_n1 + trade_n3 + give + give_s1 + give_gn + [core_tab]:
+        d.wait_send()
     give_gn1.wait_recv()
     x0 = r.s0[...]
     d, gain = norm_back(x0, inverse_of(x0), g_self, r.grads[mine, :] + r.arrived[3].astype(F32))
@@ -747,16 +763,12 @@
     here()
     for j in range(6, len(to) + 1):
         small_step(j)
-    r.smo[...] = r.sm[0:2]
-    r.dgo[...] = r.sm[2 + t]
     for n, p in enumerate(plans):
-        for d in [d for d, _, _ in p.core] + sum([copies for copies, _ in p.stages], []) + sum(p.back, []):
+        for d in p.back[-1]:
             d.wait_send()
         out_copy(n).wait()
-    for d in stores:
+    for d in stores + small_stores:
         d.wait()
-    for d in trade + trade_n1 + trade_n3 + give + give_s1 + give_gn + [core_tab]:
-        d.wait_send()
 
 
 def layer(bits, ins):
@@ -768,7 +780,7 @@
     wide, square = (256, 768), (768, 768)
     out = dict(lo=S(wide, BF), gtok=S(wide, BF), gmem=S((1024, 768), BF), smo=S((2, 8, 256), F32), dgo=S((8, 256), F32),
                own_out=S(square, BF), cross_out=S(square, BF), feed_out=S((1536, 768), BF))
-    out_specs = [A, A, A, V, V, A, A, A]
+    out_specs = [A] * len(out)
     sizes = [n for _, _, n, _ in CHUNKS]
 
     def parts_of(n, order):
@@ -801,8 +813,17 @@
     results = [vm((n, 768), BF) for n in sizes]
     more = [vm((bits - 3, n // 8, 768), BF) for n in sizes] if bits > 3 else []
     dma = pltpu.SemaphoreType.DMA
-    sems = dict(gsend=dma((3, 11)), grecv=dma((3, 11)), xsend=dma((12,)), xrecv=dma((12,)), csend=dma((3,)), crecv=dma((3,)), rsend=dma((len(CHUNKS), 16 + bits)), rrecv=dma((len(CHUNKS), 16 + bits)), lsem=dma((20,)), osem=dma((len(CHUNKS),)),
-                esem=dma((3,)), ssend=dma((2 + bits,)), srecv=dma((2 + bits,)))
+    copies = 0
+    for _, _, _, order in CHUNKS:
+        shards = 2 if "x" in order else 1
+        copies += shards + bits - 3
+        for d in order:
+            if d == "x":
+                shards, copies = 1, copies + 1
+            else:
+                copies += (shards + 1) * (3 if d == "q" else 1)
+    sems = dict(gsend=dma((3, 11)), grecv=dma((3, 11)), xsend=dma((12,)), xrecv=dma((12,)), csend=dma((3,)), crecv=dma((3,)), rsend=dma((copies,)), rrecv=dma((copies,)), lsem=dma((20,)), osem=dma((len(CHUNKS),)),
+                esem=dma((5,)), ssend=dma((2 + bits,)), srecv=dma((2 + bits,)))
     names = list(inputs) + list(out) + list(scratch) + list(sems)
 
     def kernel(*refs):

time: 182 us -> 177 us (0.973)
  Pallas kernels: 181 us -> 176 us
    pallas_call x1, Pallas kernels: 174 us -> 169 us  [layer(): pl.pallas_call(kernel, out_shape=list(out.values()), in_specs=list(inputs...]
where the time goes in v6:
time: 177 us
  Pallas kernels  176 us (99%)
    pallas_call x1, Pallas kernels, layer(): pl.pallas_call(kernel, out_shape=list(out.values()), in_specs=list(inputs...  169 us
    pallas_call x1, Pallas kernels, finish(): pl.pallas_call(finish_kernel, grid=(n,), out_shape=shapes, in_specs=in_sp...  7.03 us

profile of v6, /device:TPU:0, one launch (start us, length us, event | category | flops | bytes accessed | tf_op | source)
XLA Modules:
  0.0 176.6 jit_solution(17465526109170644050)
XLA Ops:
  0.7 168.7 %shard_map.340 = (bf16[256,768]{1,0:T(8,128)(2,1)}, bf16[256,768]{1,0:T(8,128)(2,1)}, bf16[1024,768]{1,0:T(8,128)(2,1)}, f32[2,8,256]{2,1,0:T(8,128)}, f32[8,256...) custom-call(bf16[256,768]{1,0:T(8,128)(2,1)} %bitcast.21, ...), custom_call_target="tpu_custom_call" | custom-call | tf_op jit(solution)/shard_map/pallas_call | solution.py:838
  169.4 7.0 %shard_map.341 = (bf16[256,768]{1,0:T(8,128)(2,1)}, bf16[256,768]{1,0:T(8,128)(2,1)}, bf16[1024,768]{1,0:T(8,128)(2,1)}, f32[2,768]{1,0:T(2,128)}, f32[768]{0:T(...) custom-call(bf16[256,768]{1,0:T(8,128)(2,1)} %get-tuple-element.44.l, ...), custom_call_target="tpu_custom_call" | custom-call | tf_op jit(solution)/shard_map/pallas_call | solution.py:882

commit v7 on v6

--- a/solution.py
+++ b/solution.py
@@ -156,8 +156,6 @@
 
     slot = lambda v, k, i: v.at[k, pl.ds(192 * i, 192), :]
     token_load = load(r.tok_in, r.tok)
-    small_loads = [load(a, b) for a, b in ((r.emb_in, r.emb), (r.tags_in, r.tags), (r.gain1_in, r.gain1), (r.tab_in, r.tab),
-                                           (r.gain2_in, r.gain2), (r.gain3_in, r.gain3), (r.mmask_in, r.mmask))]
     key_loads = [load(src, slot(r.cross, t, i)) for i, src in enumerate((r.ck, r.cv))]
     self_loads = [load(src, slot(r.own, c, i)) for i, src in enumerate((r.sq, r.sk, r.sv, r.so))]
     query_loads = [load(src, slot(r.cross, t, 2 + i)) for i, src in enumerate((r.cq, r.co))]
@@ -170,8 +168,6 @@
     for p in partners:
         pl.semaphore_signal(barrier, inc=1, device_id=p, device_id_type=MESH)
 
-    for d in small_loads:
-        d.wait()
     g_self, g_cross, g_hid = (g[...].astype(F32).reshape(1, 768) for g in (r.gain1, r.gain2, r.gain3))
     ji = lax.broadcasted_iota(jnp.int32, (256, 256), 0)
     ii = lax.broadcasted_iota(jnp.int32, (256, 256), 1)
@@ -775,7 +771,7 @@
     S = jax.ShapeDtypeStruct
     V, A, M = (pl.BlockSpec(memory_space=s) for s in (pltpu.VMEM, pl.ANY, pltpu.SMEM))
     vm = pltpu.VMEM
-    inputs = dict(tok_in=A, mem_in=A, cot_in=A, lengths=M, mmask_in=A, tags_in=A, emb_in=A, gain1_in=A, gain2_in=A, gain3_in=A, tab_in=A,
+    inputs = dict(tok_in=A, mem_in=A, cot_in=A, lengths=M, mmask=V, tags=V, emb=V, gain1=V, gain2=V, gain3=V, tab=V,
                   sq=A, sk=A, sv=A, so=A, cq=A, ck=A, cv=A, co=A, hin=A, hout=A)
     wide, square = (256, 768), (768, 768)
     out = dict(lo=S(wide, BF), gtok=S(wide, BF), gmem=S((1024, 768), BF), smo=S((2, 8, 256), F32), dgo=S((8, 256), F32),
@@ -804,8 +800,6 @@
         q1=vm((4, 256, 192), BF), kv1=vm((4, 256, 384), BF), kvT1=vm((4, 384, 256), BF), q2=vm((4, 256, 192), BF), gT=vm((2, 576, 512), BF),
         kv=vm((4, 1024, 384), BF), kvT=vm((4, 384, 1024), BF), mix1=vm((2, 192, 512), BF), mix2=vm((4, 192, 256), BF),
         lse=vm((8, 8, 256), F32), mask2=vm((1024, 128), F32), tagv=vm((256, 128), F32), btab=vm((2, 8, 256), F32),
-        mmask=vm((4, 1024), jnp.int32), tags=vm((1, 256), jnp.int32), emb=vm((2, 768), BF), gain1=vm((768,), BF), gain2=vm((768,), BF),
-        gain3=vm((768,), BF), tab=vm((3, 32), BF),
         sm=vm((6, 8, 256), F32), smb=vm((2 + bits, 6, 8, 256), F32), gmv=vm((1024, 768), BF), lov=vm(wide, BF), gtv=vm(wide, BF),
     )
     first = [vm((2 if "x" in order else 1, n, 768), BF) for _, _, n, order in CHUNKS]
@@ -822,7 +816,7 @@
                 shards, copies = 1, copies + 1
             else:
                 copies += (shards + 1) * (3 if d == "q" else 1)
-    sems = dict(gsend=dma((3, 11)), grecv=dma((3, 11)), xsend=dma((12,)), xrecv=dma((12,)), csend=dma((3,)), crecv=dma((3,)), rsend=dma((copies,)), rrecv=dma((copies,)), lsem=dma((20,)), osem=dma((len(CHUNKS),)),
+    sems = dict(gsend=dma((3, 11)), grecv=dma((3, 11)), xsend=dma((12,)), xrecv=dma((12,)), csend=dma((3,)), crecv=dma((3,)), rsend=dma((copies,)), rrecv=dma((copies,)), lsem=dma((13,)), osem=dma((len(CHUNKS),)),
                 esem=dma((5,)), ssend=dma((2 + bits,)), srecv=dma((2 + bits,)))
     names = list(inputs) + list(out) + list(scratch) + list(sems)
 

time: 177 us -> 177 us (level)
  no operation moved by 1% of the time
where the time goes in v7:
time: 177 us
  Pallas kernels  176 us (99%)
    pallas_call x1, Pallas kernels, layer(): pl.pallas_call(kernel, out_shape=list(out.values()), in_specs=list(inputs...  169 us
    pallas_call x1, Pallas kernels, finish(): pl.pallas_call(finish_kernel, grid=(n,), out_shape=shapes, in_specs=in_sp...  7.03 us

profile of v7, /device:TPU:0, one launch (start us, length us, event | category | flops | bytes accessed | tf_op | source)
XLA Modules:
  0.0 176.7 jit_solution(14801657844862104580)
XLA Ops:
  0.7 168.8 %shard_map.340 = (bf16[256,768]{1,0:T(8,128)(2,1)}, bf16[256,768]{1,0:T(8,128)(2,1)}, bf16[1024,768]{1,0:T(8,128)(2,1)}, f32[2,8,256]{2,1,0:T(8,128)}, f32[8,256...) custom-call(bf16[256,768]{1,0:T(8,128)(2,1)} %bitcast.21, ...), custom_call_target="tpu_custom_call" | custom-call | tf_op jit(solution)/shard_map/pallas_call | solution.py:832
  169.5 7.0 %shard_map.341 = (bf16[256,768]{1,0:T(8,128)(2,1)}, bf16[256,768]{1,0:T(8,128)(2,1)}, bf16[1024,768]{1,0:T(8,128)(2,1)}, f32[2,768]{1,0:T(2,128)}, f32[768]{0:T(...) custom-call(bf16[256,768]{1,0:T(8,128)(2,1)} %get-tuple-element.44.l, ...), custom_call_target="tpu_custom_call" | custom-call | tf_op jit(solution)/shard_map/pallas_call | solution.py:876
